TPU v7x, 256 devices: a whole 4x4x8 slice. The times are simulated.
256 devices in a mesh: frame: 32 (over z_hi, y, core), head: 8 (over z_lo, x).
Axes of the slice: x: 4, y: 4, z: 8 (z_hi: 4, z_lo: 2; z = z_hi * 2 + z_lo), core: 2. Of those that a mesh axis runs over, the one named last changes fastest.
Arguments:
- tokens: bfloat16 [32768, 3072], P('frame'), may hold values from -6 to 6
- qkv_weight: bfloat16 [3, 3072, 3072], P(None, None, 'head'), may hold values from -0.109375 to 0.109375
- query_gain: float32 [128], replicated, may hold values from 0.1 to 1.9
- key_gain: float32 [128], replicated, may hold values from 0.1 to 1.9
- labels: int32 [24], P('head'), may hold values from 0 to 1, as said below
- space_mask: int32 [24, 16, 48], P('head'), may hold values from 0 to 1, as said below
- time_mask: int32 [24, 4, 4], P('head'), may hold values from 0 to 1, as said below
Outputs:
- attended: bfloat16 [32768, 3072], P(('frame', 'head'))
Inputs may be any that keep to these rules, and one draw needn't show every extreme that they name: `labels`: among heads 3 * j, 3 * j + 1 and 3 * j + 2 exactly one is temporal. space_mask[h, a, 16 + a] = 1 for every head and query block. For each head, at most 8 key blocks of the previous frame (b < 16) are allowed for some query block, and at most 8 of the next frame (b >= 32); some head reaches 8 on each side. time_mask[h, a, a] = 1 for every head and query block.
All inputs are finite; a program needn't handle non-finite values.
Results may differ from a plain program's by a relative error of at most 0.0073.
Values may be sent and summed in bfloat16 or wider, within the bound.
No kernel may reach another device: no remote copies, remote signals or barrier semaphores. Data moves between devices by JAX's collectives and lax.ppermute only.
A program may use at most 128 MiB of HBM per device.

v0:
```python
import math

import jax
import jax.numpy as jnp
from jax import lax
from jax.sharding import PartitionSpec as P

STRIP = 8
BLOCK = 64


epsilon = 1e-06


def padded(cells, sides, width):
    for axis, dim in sides:
        count = lax.axis_size(axis)
        ends = count - 1
        head = lax.slice_in_dim(cells, 0, width, axis=dim)
        tail = lax.slice_in_dim(cells, cells.shape[dim] - width, cells.shape[dim], axis=dim)
        cells = jnp.concatenate(
            [
                lax.ppermute(tail, axis, [(i, (i + 1) % count) for i in range(ends)]),
                cells,
                lax.ppermute(head, axis, [((i + 1) % count, i) for i in range(ends)]),
            ],
            axis=dim,
        )
    return cells


def normed(projected, gains):
    inverse_rms = lax.rsqrt(jnp.mean(projected * projected, axis=-1, keepdims=True) + epsilon)
    return (projected * inverse_rms * gains).astype(jnp.bfloat16)


def weigh(scores, column_mask):
    shape = scores.shape
    parts = scores.reshape(shape[:-2] + (shape[-2] // BLOCK, BLOCK, shape[-1]))
    weight = jnp.exp(parts) * column_mask[..., :, None, :]
    weight = weight.reshape(shape)
    denominator = jnp.sum(weight, axis=-1, keepdims=True)
    return (weight.astype(jnp.bfloat16), denominator)


def send_strips(packed):
    return lax.all_to_all(packed, "frame", split_axis=1, concat_axis=1, tiled=True)


def on_device(tokens, qkv_weight, query_gain, key_gain, labels, space_mask, time_mask):
    frame_count = lax.axis_size("frame")
    own_index = lax.axis_index("frame")
    row_count = tokens.shape[0]
    local_heads = labels.shape[0]
    head_dim = query_gain.shape[0]
    groups = local_heads // 3
    blocks = row_count // BLOCK
    space_count = 2 * groups
    scale = 1.0 / math.sqrt(head_dim)
    picked = labels.reshape(groups, 3)
    time_slot = jnp.sum(picked * jnp.arange(3, dtype=jnp.int32)[None, :], axis=1)
    group_base = 3 * jnp.arange(groups, dtype=jnp.int32)
    time_heads = group_base + time_slot
    first_space = group_base + jnp.where(time_slot == 0, 1, 0)
    second_space = group_base + jnp.where(time_slot == 2, 1, 2)
    space_heads = jnp.stack([first_space, second_space], axis=1).reshape(space_count)
    projected = jnp.einsum("td,kdc->ktc", tokens, qkv_weight, preferred_element_type=jnp.float32)
    projected = projected.reshape(3, row_count, local_heads, head_dim)
    queries = normed(projected[0], query_gain)
    key_rows = normed(projected[1], key_gain)
    values = projected[2].astype(jnp.bfloat16)
    space_q = jnp.take(queries, space_heads, axis=1)
    space_k = jnp.take(key_rows, space_heads, axis=1)
    space_v = jnp.take(values, space_heads, axis=1)
    time_q = jnp.take(queries, time_heads, axis=1)
    time_k = jnp.take(key_rows, time_heads, axis=1)
    time_v = jnp.take(values, time_heads, axis=1)
    packed = jnp.stack([time_q, time_k, time_v])
    space_live = jnp.take(space_mask, space_heads, axis=0)
    lower_ok = (own_index > 0).astype(jnp.float32)
    upper_ok = (own_index < frame_count - 1).astype(jnp.float32)
    own_pair = jnp.stack([space_k, space_v]).reshape(2, row_count, space_count * head_dim)
    near_pair = padded(own_pair, (("frame", 1),), row_count)
    reach = jnp.concatenate(
        [
            jnp.ones((blocks,), jnp.float32) * lower_ok,
            jnp.ones((blocks,), jnp.float32),
            jnp.ones((blocks,), jnp.float32) * upper_ok,
        ]
    )
    allowed_blocks = space_live.astype(jnp.float32) * reach[None, None, :]
    received = send_strips(packed)
    key_total = near_pair.shape[1]
    near_keys = near_pair[0].reshape(key_total, space_count, head_dim)
    near_values = near_pair[1].reshape(key_total, space_count, head_dim)
    space_scores = (
        jnp.einsum("rhd,chd->hrc", space_q, near_keys, preferred_element_type=jnp.float32) * scale
    )
    column_mask = jnp.repeat(allowed_blocks, BLOCK, axis=-1)
    space_weight, space_total = weigh(space_scores, column_mask)
    space_mixed = jnp.einsum(
        "hrc,chd->rhd", space_weight, near_values, preferred_element_type=jnp.float32
    )
    space_out = (space_mixed / jnp.transpose(space_total, (1, 0, 2))).astype(jnp.bfloat16)
    pos_count = row_count // frame_count
    strip_count = pos_count // STRIP
    strip_length = frame_count * STRIP
    strips = received.reshape(3, frame_count, strip_count, STRIP, groups, head_dim)
    strips = strips.transpose(0, 4, 2, 1, 3, 5).reshape(
        3, groups, strip_count, strip_length, head_dim
    )
    time_columns = jnp.repeat(
        jnp.take(time_mask, time_heads, axis=0).astype(jnp.float32), BLOCK, axis=-1
    )[:, None]
    time_scores = (
        jnp.einsum("gsrd,gscd->gsrc", strips[0], strips[1], preferred_element_type=jnp.float32)
        * scale
    )
    time_weight, time_total = weigh(time_scores, time_columns)
    time_mixed = jnp.einsum(
        "gsrc,gscd->gsrd", time_weight, strips[2], preferred_element_type=jnp.float32
    )
    time_result = (time_mixed / time_total).astype(jnp.bfloat16)
    returning = time_result.reshape(groups, strip_count, frame_count, STRIP, head_dim)
    returning = returning.transpose(2, 1, 3, 0, 4).reshape(row_count, groups, head_dim)
    time_out = lax.all_to_all(returning, "frame", split_axis=0, concat_axis=0, tiled=True)
    merged = jnp.concatenate([space_out, time_out], axis=1)
    order_all = jnp.concatenate([space_heads, time_heads])
    head_ids = jnp.arange(local_heads, dtype=jnp.int32)
    inverse = jnp.sum(
        head_ids[:, None] * (order_all[:, None] == head_ids[None, :]).astype(jnp.int32), axis=0
    )
    result = jnp.take(merged, inverse, axis=1).reshape(row_count, local_heads * head_dim)
    return lax.all_to_all(result, "head", split_axis=0, concat_axis=1, tiled=True)


def solution(mesh):
    placed = (
        P("frame", None),
        P(None, None, "head"),
        P(),
        P(),
        P("head"),
        P("head", None, None),
        P("head", None, None),
    )
    return jax.shard_map(
        on_device, mesh=mesh, in_specs=placed, out_specs=P(("frame", "head"), None), check_vma=False
    )
```

profile of v0, /device:TPU:8, one launch (start us, length us, event | category | flops | bytes accessed | tf_op | source)
XLA Modules:
  0.0 133.9 jit_solution(16908970669279733438)
XLA Ops:
  0.0 11.0 %fusion.4 = f32[3,1024,384]{1,2,0:T(8,128)S(1)} fusion(bf16[3,3072,384]{2,1,0:T(8,128)(2,1)} %param.12, bf16[1024,3072]{1,0:T(8,128)(2,1)} %param.11), kind=kOutput, calls=%fused_computation.11 | convolution fusion | flops 7247757312 | bytes 18087936 | tf_op jit(solution)/shard_map/td,kdc->ktc/dot_general | solution.py:67
  11.0 1.0 slice.76
  12.0 0.2 fusion.30
  12.2 0.0 copy-start.14
  12.2 1.6 %copy.78 = f32[1024,3,128]{2,0,1:T(8,128)} copy(f32[1024,3,128]{0,2,1:T(8,128)S(1)} %bitcast.113) | data formatting | bytes 3145728 | tf_op jit(solution)/shard_map/squeeze | solution.py:70
  13.8 0.2 multiply_reduce_fusion.1
  14.0 0.7 multiply_reduce_fusion.2
  15.9 0.1 fusion.27
  16.1 1.7 %gather_fusion.3 = bf16[2,1024,128]{1,2,0:T(8,128)(2,1)S(1)} fusion(bf16[1024,3,128]{0,2,1:T(8,128)(2,1)} %bitcast.122, s32[1024]{0:T(1024)S(1)} %pad_clamp_fusion.2), kind=kCustom, calls=%fused_computation.1.clone | custom fusion | bytes 1048584 | tf_op jit(solution)/shard_map/jit(_take)/gather | solution.py:74
  17.8 1.9 %multiply_convert_fusion.1 = bf16[1024,3,128]{2,0,1:T(8,128)(2,1)S(1)} fusion(f32[1024,3,128]{2,0,1:T(8,128)} %copy.78, f32[128]{0:T(128)S(1)} %copy-done.12, f32[1024,3]{0,1:T(4,128)S(1)} %add_rsqrt_fusion.1), kind=kLoop, calls=%fused_computation.15 | loop fusion | flops 1179648 | bytes 2372096 | tf_op jit(solution)/shard_map/convert_element_type | solution.py:34
  19.7 0.9 copy-done.8
  20.6 1.4 %gather_fusion.2 = bf16[2,1024,128]{2,1,0:T(8,128)(2,1)} fusion(bf16[1024,3,128]{2,0,1:T(8,128)(2,1)S(1)} %multiply_convert_fusion.1, s32[1024]{0:T(1024)S(1)} %pad_clamp_fusion.2), kind=kCustom, calls=%fused_computation.clone | custom fusion | bytes 1048584 | tf_op jit(solution)/shard_map/jit(_take)/gather | solution.py:73
  22.0 0.1 broadcast_select_fusion
  22.1 1.3 %select_bitcast_fusion = bf16[1024,2,128]{2,0,1:T(8,128)(2,1)S(1)} fusion(bf16[2,1024,128]{2,1,0:T(8,128)(2,1)} %gather_fusion.2, pred[2]{0:T(512)(128)(4,1)S(1)} %compare_and_fusion), kind=kLoop, calls=%fused_computation.33 | loop fusion | flops 262144 | bytes 1048578 | tf_op jit(solution)/shard_map/jit(_take)/select_n | solution.py:73
  23.4 0.2 copy.79
  23.7 1.1 pad_maximum_fusion.1
  24.8 1.9 %collective-permute-start.1 = (bf16[2,1024,256]{1,2,0:T(8,128)(2,1)}, bf16[2,1024,256]{1,2,0:T(8,128)(2,1)}, u32[]{:S(2)}, u32[]{:S(2)}) collective-permute-start(bf16[2,1024,256]{1,2,0:T(8,128)(2,1)} %pad_maximum_fusion.1), channel_id=1, source_target_pairs={{8,0},{16,8},{24,16},{32,24},{40,32},{48,40},{56,48},{64,56},{72,6... | collective-permute-start | bytes 3145736 | tf_op jit(solution)/shard_map/ppermute | solution.py:25
  26.8 2.4 %collective-permute-start = (bf16[2,1024,256]{1,2,0:T(8,128)(2,1)}, bf16[2,1024,256]{1,2,0:T(8,128)(2,1)}, u32[]{:S(2)}, u32[]{:S(2)}) collective-permute-start(bf16[2,1024,256]{1,2,0:T(8,128)(2,1)} %pad_maximum_fusion.1), channel_id=1, source_target_pairs={{0,8},{8,16},{16,24},{24,32},{32,40},{40,48},{48,56},{56,64},{64,7... | collective-permute-start | bytes 3145736 | tf_op jit(solution)/shard_map/ppermute | solution.py:23
  31.1 0.5 copy.80
  31.6 0.2 multiply_reduce_fusion
  31.7 1.0 constant_dynamic-slice_fusion
  32.7 0.2 copy.98
  33.0 0.5 multiply_convert_fusion
  33.4 0.0 copy-start.6
  33.4 1.2 select_bitcast_fusion.2
  34.7 0.0 copy-start.7
  34.7 0.1 pad_maximum_fusion.2
  34.8 1.7 %copy.83 = bf16[3,1024,1,128]{3,0,2,1:T(4,128)(2,1)} copy(bf16[3,1024,1,128]{3,1,2,0:T(8,128)(2,1)S(1)} %pad_maximum_fusion.2) | data formatting | bytes 1572864 | tf_op jit(solution)/shard_map/stack | solution.py:78
  36.4 15.3 %all-to-all-start = ((bf16[3,1024,1,128]{3,0,2,1:T(4,128)(2,1)}), bf16[3,1024,1,128]{3,0,2,1:T(4,128)(2,1)S(1)}, u32[]{:S(2)}, u32[]{:S(2)}) async-start(bf16[3,1024,1,128]{3,0,2,1:T(4,128)(2,1)} %copy.83), calls=%async_computation | async-start | bytes 2097152 | tf_op jit(solution)/shard_map/all_to_all | solution.py:47
  51.8 0.5 gather_fusion
  52.4 0.1 pad_maximum_fusion.4
  52.5 0.1 convert_multiply_fusion
  52.6 0.7 fusion.26
  53.3 0.6 gather_fusion.4
  53.9 0.1 broadcast_in_dim.86
  54.0 0.1 broadcast_in_dim.87
  54.1 0.8 copy.87
  54.9 0.3 broadcast_in_dim.82
  55.2 1.0 mul.136
  56.2 0.7 pad_add_fusion.1
  56.9 0.1 select_reduce_fusion
  57.0 0.1 broadcast_bitcast_fusion
  57.1 1.7 %pad_maximum_fusion = bf16[2,3072,256]{1,2,0:T(8,128)(2,1)S(1)} fusion(bf16[2,1024,256]{1,2,0:T(8,128)(2,1)} %collective-permute-done.1, bf16[1,1024,256]{1,2,0:T(8,128)(2,1)S(1)} %bitcast.119, bf16[1,1024,256]{1,2,0:T(8,128)(2,1)S(1)} %bitcast.117, bf16[2,1024,256]{1,2,0:T(8,128)(2,1)} %collective-permute-done), kind=kLoop, calls=%fused_computation.10 | loop fusion | flops 12582912 | bytes 6291456 | tf_op jit(solution)/shard_map/concatenate | solution.py:21
  58.8 1.4 %fusion.31 = (bf16[1,3072,256]{1,2,0:T(8,128)(2,1)S(1)}, bf16[1,3072,256]{1,2,0:T(8,128)(2,1)}) fusion(bf16[2,3072,256]{1,2,0:T(8,128)(2,1)S(1)} %pad_maximum_fusion), kind=kLoop, calls=%fused_computation.74 | loop fusion | bytes 6291456 | tf_op jit(solution)/shard_map/slice | solution.py:94
  60.2 8.3 %fusion = (f32[2,1024]{1,0:T(2,128)S(1)}, bf16[2,1024,3072]{2,1,0:T(8,128)(2,1)}) fusion(f32[2,16,3072]{2,1,0:T(8,128)S(1)} %copy-done.10, bf16[3072,2,128]{0,2,1:T(8,128)(2,1)S(1)} %bitcast.115, bf16[2,1024,128]{2,1,0:T(8,128)(2,1)S(1)} %gather_fusion.4, pred[2]{0:T(512)(128)(4,1)S(1)} %compare_and_fusion), kind=kOutput, calls=%fused_computation.6 | convolution fusion | flops 1636038656 | bytes 15081474 | tf_op jit(solution)/shard_map/rhd,chd->hrc/dot_general | solution.py:97
  68.6 13.0 %all-to-all-done = bf16[3,1024,1,128]{3,0,2,1:T(4,128)(2,1)S(1)} async-done(((bf16[3,1024,1,128]{3,0,2,1:T(4,128)(2,1)}), bf16[3,1024,1,128]{3,0,2,1:T(4,128)(2,1)S(1)}, u32[]{:S(2)}, u32[]{:S(2)}) %all-to-all-start) | async-done | bytes 786464 | tf_op jit(solution)/shard_map/all_to_all | solution.py:47
  81.5 0.1 copy.84
  81.6 0.1 fusion.32
  81.7 0.4 fusion.33
  82.1 0.4 fusion.12
  82.5 0.5 broadcast.317
  83.1 0.8 reduce.3
  83.9 0.8 reshape.356
  84.6 16.8 %all-to-all-start.1 = ((bf16[32,2,2048]{2,1,0:T(2,128)(2,1)}), bf16[32,2,2048]{2,1,0:T(2,128)(2,1)S(1)}, u32[]{:S(2)}, u32[]{:S(2)}) async-start(bf16[32,2,2048]{2,1,0:T(2,128)(2,1)} %reshape.356), calls=%async_computation.1 | async-start | bytes 524288 | tf_op jit(solution)/shard_map/all_to_all | solution.py:126
  101.5 8.8 %fusion.10 = bf16[1024,2,128]{0,2,1:T(8,128)(2,1)S(1)} fusion(bf16[3072,2,128]{0,2,1:T(8,128)(2,1)S(1)} %bitcast.126, bf16[2,1024,3072]{2,1,0:T(8,128)(2,1)} %get-tuple-element.32, f32[1024,2]{0,1:T(2,128)S(1)} %bitcast.129), kind=kOutput, calls=%fused_computation.22 | convolution fusion | flops 1611137024 | bytes 14688256 | tf_op jit(solution)/shard_map/hrc,chd->rhd/dot_general | solution.py:101
  110.3 2.5 %all-to-all-done.1 = bf16[32,2,2048]{2,1,0:T(2,128)(2,1)S(1)} async-done(((bf16[32,2,2048]{2,1,0:T(2,128)(2,1)}), bf16[32,2,2048]{2,1,0:T(2,128)(2,1)S(1)}, u32[]{:S(2)}, u32[]{:S(2)}) %all-to-all-start.1) | async-done | bytes 262176 | tf_op jit(solution)/shard_map/all_to_all | solution.py:126
  112.9 0.3 reshape.357
  113.1 0.4 copy.92
  113.5 0.1 pad_maximum_fusion.3
  113.6 0.6 gather_fusion.1
  114.2 0.2 copy.99
  114.4 0.2 copy_select_fusion
  114.5 18.2 %all_to_all.26 = bf16[8,128,384]{1,2,0:T(8,128)(2,1)S(1)} all-to-all(bf16[8,128,384]{1,2,0:T(8,128)(2,1)S(1)} %copy_select_fusion), channel_id=1, replica_groups=mesh['frame'=32,'head'=8] {'head'}, dimensions={0} | all-to-all | bytes 1572864 | tf_op jit(solution)/shard_map/all_to_all | solution.py:134
  132.7 1.2 copy.94
  (43 shorter events, 0.2 us)
Async XLA Ops:
  0.0 51.8 %copy-start = (s32[3,16,48]{2,1,0:T(8,128)S(1)}, s32[3,16,48]{2,1,0:T(8,128)}, u32[]{:S(2)}) copy-start(s32[3,16,48]{2,1,0:T(8,128)} %param.16) | copy-start | bytes 27652
  12.2 1.8 %copy-start.14 = (s32[3]{0:T(128)S(1)}, s32[3]{0:T(128)}, u32[]{:S(2)}) copy-start(s32[3]{0:T(128)} %param.15) | copy-start | bytes 40
  12.2 5.6 %copy-start.12 = (f32[128]{0:T(128)S(1)}, f32[128]{0:T(128)}, u32[]{:S(2)}) copy-start(f32[128]{0:T(128)} %param.14) | copy-start | bytes 1540
  19.7 0.9 copy-start.8
  22.1 9.0 %copy-start.4 = (bf16[2,1024,128]{1,2,0:T(8,128)(2,1)}, bf16[2,1024,128]{1,2,0:T(8,128)(2,1)S(1)}, u32[]{:S(2)}) copy-start(bf16[2,1024,128]{1,2,0:T(8,128)(2,1)S(1)} %broadcast_select_fusion) | copy-start | bytes 1572868
  23.7 7.4 %copy-start.2 = (bf16[1024,2,128]{0,2,1:T(8,128)(2,1)}, bf16[1024,2,128]{0,2,1:T(8,128)(2,1)S(1)}, u32[]{:S(2)}) copy-start(bf16[1024,2,128]{0,2,1:T(8,128)(2,1)S(1)} %copy.79) | copy-start | bytes 1572868
  24.8 32.3 %collective-permute-start.1 = (bf16[2,1024,256]{1,2,0:T(8,128)(2,1)}, bf16[2,1024,256]{1,2,0:T(8,128)(2,1)}, u32[]{:S(2)}, u32[]{:S(2)}) collective-permute-start(bf16[2,1024,256]{1,2,0:T(8,128)(2,1)} %pad_maximum_fusion.1), channel_id=1, source_target_pairs={{8,0},{16,8},{24,16},{32,24},{40,32},{48,40},{56,48},{64,56},{72,6... | collective-permute-start | bytes 3145736 | tf_op jit(solution)/shard_map/ppermute | solution.py:25
  26.8 30.3 %collective-permute-start = (bf16[2,1024,256]{1,2,0:T(8,128)(2,1)}, bf16[2,1024,256]{1,2,0:T(8,128)(2,1)}, u32[]{:S(2)}, u32[]{:S(2)}) collective-permute-start(bf16[2,1024,256]{1,2,0:T(8,128)(2,1)} %pad_maximum_fusion.1), channel_id=1, source_target_pairs={{0,8},{8,16},{16,24},{24,32},{32,40},{40,48},{48,56},{56,64},{64,7... | collective-permute-start | bytes 3145736 | tf_op jit(solution)/shard_map/ppermute | solution.py:23
  31.1 1.9 %copy-start.13 = (f32[128]{0:T(128)S(1)}, f32[128]{0:T(128)}, u32[]{:S(2)}) copy-start(f32[128]{0:T(128)} %param.13) | copy-start | bytes 1540
  33.4 1.2 copy-start.6
  34.7 18.6 %copy-start.7 = (bf16[1024,3,128]{2,0,1:T(8,128)(2,1)S(1)}, bf16[1024,3,128]{2,0,1:T(8,128)(2,1)}, u32[]{:S(2)}) copy-start(bf16[1024,3,128]{2,0,1:T(8,128)(2,1)} %copy-done.6) | copy-start | bytes 2359300
  36.4 20.7 %copy-start.3 = (bf16[1024,2,128]{0,2,1:T(8,128)(2,1)S(1)}, bf16[1024,2,128]{0,2,1:T(8,128)(2,1)}, u32[]{:S(2)}) copy-start(bf16[1024,2,128]{0,2,1:T(8,128)(2,1)} %copy-done.2) | copy-start | bytes 1572868
  36.4 20.7 %copy-start.5 = (bf16[2,1024,128]{1,2,0:T(8,128)(2,1)S(1)}, bf16[2,1024,128]{1,2,0:T(8,128)(2,1)}, u32[]{:S(2)}) copy-start(bf16[2,1024,128]{1,2,0:T(8,128)(2,1)} %copy-done.4) | copy-start | bytes 1572868
  36.4 45.1 %all-to-all-start = ((bf16[3,1024,1,128]{3,0,2,1:T(4,128)(2,1)}), bf16[3,1024,1,128]{3,0,2,1:T(4,128)(2,1)S(1)}, u32[]{:S(2)}, u32[]{:S(2)}) async-start(bf16[3,1024,1,128]{3,0,2,1:T(4,128)(2,1)} %copy.83), calls=%async_computation | async-start | bytes 2097152 | tf_op jit(solution)/shard_map/all_to_all | solution.py:47
  58.8 1.4 %copy-start.10 = (f32[2,16,3072]{2,1,0:T(8,128)S(1)}, f32[2,16,3072]{2,1,0:T(8,128)}, u32[]{:S(2)}) copy-start(f32[2,16,3072]{2,1,0:T(8,128)} %mul.136) | copy-start | bytes 1179652
  68.6 13.1 %copy-start.11 = (f32[256,256]{0,1:T(8,128)S(1)}, f32[256,256]{0,1:T(8,128)}, u32[]{:S(2)}) copy-start(f32[256,256]{0,1:T(8,128)} %copy.87) | copy-start | bytes 786436
  81.7 19.8 %copy-start.9 = (bf16[1,3072,256]{1,2,0:T(8,128)(2,1)S(1)}, bf16[1,3072,256]{1,2,0:T(8,128)(2,1)}, u32[]{:S(2)}) copy-start(bf16[1,3072,256]{1,2,0:T(8,128)(2,1)} %get-tuple-element.36) | copy-start | bytes 4718596
  84.6 28.2 %all-to-all-start.1 = ((bf16[32,2,2048]{2,1,0:T(2,128)(2,1)}), bf16[32,2,2048]{2,1,0:T(2,128)(2,1)S(1)}, u32[]{:S(2)}, u32[]{:S(2)}) async-start(bf16[32,2,2048]{2,1,0:T(2,128)(2,1)} %reshape.356), calls=%async_computation.1 | async-start | bytes 524288 | tf_op jit(solution)/shard_map/all_to_all | solution.py:126
  114.2 19.7 %copy-start.1 = (s32[3,16,48]{2,1,0:T(8,128)S(1)}, s32[3,16,48]{2,1,0:T(8,128)}, u32[]{:S(2)}) copy-start(s32[3,16,48]{2,1,0:T(8,128)} %param.16) | copy-start | bytes 27652
where the time goes:
time: 136 us; the launch traced here: 134 us
  starting transfers between devices  36.5 us (27%)
  matrix products  28.9 us (21%)
  local copies, waits for them, and re-layouts  19.4 us (14%)
  blocking collectives  18.2 us (13%)
  waiting for transfers between devices  15.5 us (11%)
  other arithmetic  11.8 us (9%)
  between operations  3.69 us (3%)
    all_to_all x1, blocking collectives, on_device(): lax.all_to_all(result, 'head', split_axis=0, concat_axis=1, tiled=True)  18.2 us
    all_to_all x1, starting transfers between devices, on_device(): lax.all_to_all(returning, 'frame', split_axis=0, concat_axis=0, tiled=True)  16.8 us
    all_to_all x1, starting transfers between devices, send_strips(): lax.all_to_all(packed, 'frame', split_axis=1, concat_axis=1, tiled=True)  15.3 us
    all_to_all x1, waiting for transfers between devices, send_strips(): lax.all_to_all(packed, 'frame', split_axis=1, concat_axis=1, tiled=True)  13 us
    dot_general x1, matrix products, on_device(): jnp.einsum('td,kdc->ktc', tokens, qkv_weight, preferred_element_type=jnp....  11 us
    dot_general x1, matrix products, on_device(): jnp.einsum('hrc,chd->rhd', space_weight, near_values, preferred_element_t...  8.84 us
    dot_general x1, matrix products, on_device(): jnp.einsum('rhd,chd->hrc', space_q, near_keys, preferred_element_type=jnp...  8.33 us
  transfers between devices with their start and end apart: 4, of which 2 were waited for; matrix products, arithmetic and copies ran while one was open for 23% of the time, Pallas kernels for 0%

commit v1 on v0

v1 whole, which is shorter than its diff:
```python
import functools
import math

import jax
import jax.numpy as jnp
from jax import lax
from jax.experimental import pallas as pl
from jax.experimental.pallas import tpu as pltpu
from jax.sharding import PartitionSpec as P

STRIP = 8
BLOCK = 64
D = 3072
HD = 128
ROWS = 1024
FRAMES = 32
GROUPS = 8
QBLOCKS = 16
NEAR = 8
OUT = FRAMES // GROUPS
CHUNK = 768
PARTS = D // CHUNK
TILE = 256
EPSILON = 1e-06
SCALE = math.log2(math.e) / math.sqrt(HD)
BLOCKED = -16384.0
DEAD = 64
LABEL_ROWS = 16

bf16 = jnp.bfloat16
f32 = jnp.float32


def slots_of(labels):
    time = labels[1] + 2 * labels[2]
    return time, jnp.where(time == 0, 1, 0), jnp.where(time == 2, 1, 2)


def swapped(two_bits):
    return (two_bits & 1) * 2 + ((two_bits >> 1) & 1)


def owner_of(source, target, quarter):
    flip = (source >> 2) ^ (target >> 2)
    shift = (target - source) & 3
    return (quarter * 4 + swapped((shift - 2 * flip) & 3)) * 2 + flip


def handover():
    pairs = []
    for owner in range(FRAMES):
        flip = owner & 1
        shift = (swapped((owner >> 1) & 3) + 2 * flip) & 3
        for head in range(GROUPS):
            target = ((head >> 2) ^ flip) * 4 + ((head + shift) & 3)
            pairs.append((owner * GROUPS + head, owner * GROUPS + target))
    return pairs


def normed(x, gain):
    inverse = lax.rsqrt(jnp.mean(x * x, axis=-1, keepdims=True) + EPSILON)
    return (x * inverse * gain).astype(bf16)


def load_parts(tokens, weight, columns, tok, wts, sems):
    def copies(c):
        made = [
            pltpu.make_async_copy(
                tokens.at[:, pl.ds(c * CHUNK, CHUNK)], tok.at[:, pl.ds(c * CHUNK, CHUNK)], sems.at[c, 0]
            )
        ]
        for i, (k, slot) in enumerate(columns):
            made.append(
                pltpu.make_async_copy(
                    weight.at[k, pl.ds(c * CHUNK, CHUNK), pl.ds(pl.multiple_of(slot * HD, HD), HD)],
                    wts.at[pl.ds(c * CHUNK, CHUNK), pl.ds(i * HD, HD)],
                    sems.at[c, 1 + i],
                )
            )
        return made

    return copies


def project(tokens, weight, columns, tok, wts, acc, sems):
    copies = load_parts(tokens, weight, columns, tok, wts, sems)
    for c in range(2):
        for copy in copies(c):
            copy.start()
    for c in range(PARTS):
        for copy in copies(c):
            copy.wait()
        if c + 2 < PARTS:
            for copy in copies(c + 2):
                copy.start()
        for r in range(ROWS // TILE):
            rows = pl.ds(r * TILE, TILE)
            part = jnp.dot(
                tok[rows, pl.ds(c * CHUNK, CHUNK)], wts[pl.ds(c * CHUNK, CHUNK), :], preferred_element_type=f32
            )
            if c == 0:
                acc[rows, :] = part
            else:
                acc[rows, :] += part


def time_project(labels, tokens, weight, query_gain, key_gain, out, tok, wts, acc, sems):
    time, _, _ = slots_of(labels)
    project(tokens, weight, [(0, time), (1, time), (2, time)], tok, wts, acc, sems)
    head = lax.axis_index("head")
    for b in range(FRAMES):
        owner = owner_of(head, b // OUT, b % OUT)
        rows = pl.ds(b * FRAMES, FRAMES)
        out[owner, 0:FRAMES, :] = normed(acc[rows, 0:HD], query_gain[...] * SCALE)
        out[owner, FRAMES : 2 * FRAMES, :] = normed(acc[rows, HD : 2 * HD], key_gain[...])
        out[owner, 2 * FRAMES :, :] = acc[rows, 2 * HD :].astype(bf16)


def space_project(labels, live, tokens, weight, query_gain, key_gain, q, kv, up, down, lanes, tok, wts, acc, sems):
    _, first, second = slots_of(labels)
    columns = [(k, slot) for k in range(3) for slot in (first, second)]
    for h, slot in enumerate((first, second)):
        for side in range(2):
            base = (2 * h + side) * 32
            for j in range(32):
                lanes[base + j] = DEAD
            count = 0
            for b in range(QBLOCKS):
                column = 2 * QBLOCKS * side + b
                alive = live[slot, column]
                lanes[base + count] = jnp.where(alive > 0, column, DEAD)
                count = count + (alive > 0).astype(jnp.int32)
    project(tokens, weight, columns, tok, wts, acc, sems)
    for h in range(2):
        for r in range(ROWS // TILE):
            rows = pl.ds(r * TILE, TILE)
            q[h, rows, :] = normed(acc[rows, h * HD : (h + 1) * HD], query_gain[...] * SCALE)
            kv[h, 0, rows, :] = normed(acc[rows, (2 + h) * HD : (3 + h) * HD], key_gain[...])
            kv[h, 1, rows, :] = acc[rows, (4 + h) * HD : (5 + h) * HD].astype(bf16)
        for side, packed in enumerate((up, down)):
            for j in range(NEAR):
                block = lanes[(2 * h + side) * 32 + j] & (QBLOCKS - 1)
                rows = pl.ds(pl.multiple_of(block * BLOCK, BLOCK), BLOCK)
                for part in range(2):
                    packed[h, part, pl.ds(j * BLOCK, BLOCK), :] = kv[h, part, rows, :]


def one_hot(rows, lane):
    return (lax.broadcasted_iota(jnp.int32, (rows, HD), 1) == lane).astype(f32).astype(bf16)


def space_attend(labels, lanes, q, kv, below, above, mask, out, keys, vals, bias):
    time, first, second = slots_of(labels)
    h = pl.program_id(0)
    t = pl.program_id(1)
    near = NEAR * BLOCK

    @pl.when(t == 0)
    def _():
        slot = jnp.where(h == 0, first, second)
        frame = lax.axis_index("frame")
        table = mask[slot].astype(f32)
        lane = lax.broadcasted_iota(jnp.int32, (QBLOCKS, HD), 1)
        table = jnp.where((lane < QBLOCKS) & (frame == 0), 0.0, table)
        table = jnp.where((lane >= 2 * QBLOCKS) & (frame == FRAMES - 1), 0.0, table)
        bias[...] = (table - 1.0) * -BLOCKED
        keys[0:ROWS, 0:HD] = kv[0, 0]
        vals[0:ROWS, 0:HD] = kv[0, 1]
        for side, got in enumerate((below, above)):
            rows = pl.ds(ROWS + side * near, near)
            keys[rows, 0:HD] = got[0, 0]
            vals[rows, 0:HD] = got[0, 1]
            for j in range(NEAR):
                lane = lanes[(2 * h + side) * 32 + j]
                keys[pl.ds(ROWS + side * near + j * BLOCK, BLOCK), HD:] = one_hot(BLOCK, lane)
        for b in range(QBLOCKS):
            keys[pl.ds(b * BLOCK, BLOCK), HD:] = one_hot(BLOCK, QBLOCKS + b)
        vals[:, HD:] = jnp.ones((ROWS + 2 * near, HD), bf16)

    per = TILE // BLOCK
    rows = [
        jnp.broadcast_to(bias[pl.ds(t * per + i, 1), :], (BLOCK, HD)).astype(bf16) for i in range(per)
    ]
    query = jnp.concatenate([q[0], jnp.concatenate(rows, axis=0)], axis=1)
    total = jnp.zeros((TILE, 2 * HD), f32)
    width = 512
    for c in range((ROWS + 2 * near) // width):
        part = pl.ds(c * width, width)
        scores = lax.dot_general(query, keys[part, :], (((1,), (1,)), ((), ())), preferred_element_type=f32)
        weight = jnp.exp2(scores).astype(bf16)
        total = total + jnp.dot(weight, vals[part, :], preferred_element_type=f32)
    mixed = (total[:, 0:HD] / total[:, HD:]).astype(bf16)
    per_target = ROWS // GROUPS
    out[:, 0:per_target, :] = mixed.reshape(TILE // per_target, per_target, HD)
    out[:, per_target:, :] = jnp.full((TILE // per_target, LABEL_ROWS, HD), time.astype(f32)).astype(bf16)


def time_attend(labels, time_mask, got, out):
    time, _, _ = slots_of(labels)
    lane = lax.broadcasted_iota(jnp.int32, (16, HD), 1)
    row = lax.broadcasted_iota(jnp.int32, (16, HD), 0)
    same = (lane & 1) == (row >> 3)
    tables = []
    for a in range(4):
        allowed = jnp.zeros((16, HD), jnp.int32)
        for b in range(4):
            allowed = jnp.where((lane >> 1) == b, time_mask[time, a, b], allowed)
        table = jnp.where(same & (allowed == 1), 0.0, BLOCKED).astype(bf16)
        tables.append(jnp.broadcast_to(table[None], (8, 16, HD)))
    bias = jnp.concatenate(tables, axis=0).reshape(512, HD)
    key_frame = lax.broadcasted_iota(jnp.int32, (512, HD), 0)
    key_lane = lax.broadcasted_iota(jnp.int32, (512, HD), 1)
    mark = (((key_frame >> 7) * 2 + ((key_frame >> 3) & 1)) == key_lane).astype(f32).astype(bf16)
    ones = jnp.ones((512, HD), bf16)
    for u in range(2):
        def rows(part):
            return got[:, pl.ds(part * FRAMES + u * 16, 16), :].reshape(512, HD)

        query = jnp.concatenate([rows(0), bias], axis=1)
        keys = jnp.concatenate([rows(1), mark], axis=1)
        vals = jnp.concatenate([rows(2), ones], axis=1)
        scores = lax.dot_general(query, keys, (((1,), (1,)), ((), ())), preferred_element_type=f32)
        weight = jnp.exp2(scores).astype(bf16)
        total = jnp.dot(weight, vals, preferred_element_type=f32)
        mixed = (total[:, 0:HD] / total[:, HD:]).astype(bf16)
        out[:, pl.ds(u * 16, 16), :] = mixed.reshape(FRAMES, 16, HD)


def assemble(space, slot, timed, out):
    here = lax.axis_index("head")
    quarter = pl.program_id(0)
    for g in range(GROUPS):
        t = timed[owner_of(g, here, quarter)]
        place = slot[g, :, 0:HD]
        place = jnp.concatenate([place] * (FRAMES // LABEL_ROWS), axis=0)
        s0 = space[g, :, 0:HD]
        s1 = space[g, :, HD:]
        base = 3 * g * HD
        out[:, base : base + HD] = jnp.where(place == 0, t, s0)
        out[:, base + HD : base + 2 * HD] = jnp.where(place == 0, s0, jnp.where(place == 1, t, s1))
        out[:, base + 2 * HD : base + 3 * HD] = jnp.where(place == 2, t, s1)


def params(mib):
    return pltpu.CompilerParams(vmem_limit_bytes=mib * 2**20)


def cost(flops, moved, exps=0):
    return pl.CostEstimate(flops=int(flops), bytes_accessed=int(moved), transcendentals=int(exps))


SMEM = pl.BlockSpec(memory_space=pltpu.SMEM)
VMEM = pl.BlockSpec(memory_space=pltpu.VMEM)
ANY = pl.BlockSpec(memory_space=pl.ANY)


def on_device(tokens, qkv_weight, query_gain, key_gain, labels, space_mask, time_mask):
    gains = (query_gain.reshape(1, HD), key_gain.reshape(1, HD))
    sent = pl.pallas_call(
        time_project,
        out_shape=jax.ShapeDtypeStruct((FRAMES, 3 * FRAMES, HD), bf16),
        in_specs=[SMEM, ANY, ANY, VMEM, VMEM],
        out_specs=VMEM,
        scratch_shapes=[
            pltpu.VMEM((ROWS, D), bf16),
            pltpu.VMEM((D, 3 * HD), bf16),
            pltpu.VMEM((ROWS, 3 * HD), f32),
            pltpu.SemaphoreType.DMA((PARTS, 4)),
        ],
        compiler_params=params(28),
        cost_estimate=cost(2 * ROWS * D * 3 * HD, 9e6),
        name="time_project",
    )(labels, tokens, qkv_weight, *gains)
    got = lax.all_to_all(sent, "frame", split_axis=0, concat_axis=0, tiled=True)

    live = jnp.pad(jnp.max(space_mask, axis=1), ((0, 0), (0, HD - 3 * QBLOCKS)))
    pair = jax.ShapeDtypeStruct((2, 2, NEAR * BLOCK, HD), bf16)
    q, kv, up, down, lanes = pl.pallas_call(
        space_project,
        out_shape=(
            jax.ShapeDtypeStruct((2, ROWS, HD), bf16),
            jax.ShapeDtypeStruct((2, 2, ROWS, HD), bf16),
            pair,
            pair,
            jax.ShapeDtypeStruct((HD,), jnp.int32),
        ),
        in_specs=[SMEM, SMEM, ANY, ANY, VMEM, VMEM],
        out_specs=(VMEM, VMEM, VMEM, VMEM, SMEM),
        scratch_shapes=[
            pltpu.VMEM((ROWS, D), bf16),
            pltpu.VMEM((D, 6 * HD), bf16),
            pltpu.VMEM((ROWS, 6 * HD), f32),
            pltpu.SemaphoreType.DMA((PARTS, 7)),
        ],
        compiler_params=params(28),
        cost_estimate=cost(2 * ROWS * D * 6 * HD, 12e6),
        name="space_project",
    )(labels, live, tokens, qkv_weight, *gains)
    below = lax.ppermute(up, "frame", [(i, i + 1) for i in range(FRAMES - 1)])
    above = lax.ppermute(down, "frame", [(i + 1, i) for i in range(FRAMES - 1)])

    mask = jnp.pad(space_mask, ((0, 0), (0, 0), (0, HD - 3 * QBLOCKS)))
    total_keys = ROWS + 2 * NEAR * BLOCK
    per_target = ROWS // GROUPS
    near_spec = pl.BlockSpec((1, 2, NEAR * BLOCK, HD), lambda h, t: (h, 0, 0, 0))
    space_out = pl.pallas_call(
        space_attend,
        grid=(2, ROWS // TILE),
        out_shape=jax.ShapeDtypeStruct((GROUPS, per_target + LABEL_ROWS, 2 * HD), bf16),
        in_specs=[
            SMEM,
            SMEM,
            pl.BlockSpec((1, TILE, HD), lambda h, t: (h, t, 0)),
            pl.BlockSpec((1, 2, ROWS, HD), lambda h, t: (h, 0, 0, 0)),
            near_spec,
            near_spec,
            VMEM,
        ],
        out_specs=pl.BlockSpec((TILE // per_target, per_target + LABEL_ROWS, HD), lambda h, t: (t, 0, h)),
        scratch_shapes=[
            pltpu.VMEM((total_keys, 2 * HD), bf16),
            pltpu.VMEM((total_keys, 2 * HD), bf16),
            pltpu.VMEM((QBLOCKS, HD), f32),
        ],
        compiler_params=params(24),
        cost_estimate=cost(2 * 4 * ROWS * total_keys * 2 * HD, 4e6, 2 * ROWS * total_keys),
        name="space_attend",
    )(labels, lanes, q, kv, below, above, mask)
    space_all = lax.all_to_all(space_out, "head", split_axis=0, concat_axis=0, tiled=True)

    time_out = pl.pallas_call(
        time_attend,
        out_shape=jax.ShapeDtypeStruct((FRAMES, FRAMES, HD), bf16),
        in_specs=[SMEM, SMEM, VMEM],
        out_specs=VMEM,
        compiler_params=params(16),
        cost_estimate=cost(8 * 512 * 512 * 2 * HD, 1e6, 2 * 512 * 512),
        name="time_attend",
    )(labels, time_mask, got)
    moved = lax.ppermute(time_out, ("frame", "head"), handover())
    timed = lax.all_to_all(moved, "frame", split_axis=0, concat_axis=0, tiled=True)

    quarter = per_target // 4
    return pl.pallas_call(
        assemble,
        grid=(4,),
        out_shape=jax.ShapeDtypeStruct((per_target, 3 * GROUPS * HD), bf16),
        in_specs=[
            pl.BlockSpec((GROUPS, quarter, 2 * HD), lambda i: (0, i, 0)),
            pl.BlockSpec((GROUPS, LABEL_ROWS, 2 * HD), lambda i: (0, per_target // LABEL_ROWS, 0)),
            VMEM,
        ],
        out_specs=pl.BlockSpec((quarter, 3 * GROUPS * HD), lambda i: (i, 0)),
        compiler_params=params(16),
        cost_estimate=cost(1e6, 2e6),
        name="assemble",
    )(space_all, space_all, timed)


def solution(mesh):
    placed = (
        P("frame", None),
        P(None, None, "head"),
        P(),
        P(),
        P("head"),
        P("head", None, None),
        P("head", None, None),
    )
    return jax.shard_map(
        on_device, mesh=mesh, in_specs=placed, out_specs=P(("frame", "head"), None), check_vma=False
    )
```

time: 136 us -> 115 us (0.85)
  the two profiles are of different devices: /device:TPU:8 before, /device:TPU:1 now
where the time goes in v1:
time: 115 us; the launch traced here: 114 us
  blocking collectives  30.7 us (27%)
  Pallas kernels  29 us (25%)
  starting transfers between devices  28.6 us (25%)
  local copies, waits for them, and re-layouts  13.6 us (12%)
  waiting for transfers between devices  12.1 us (11%)
    all_to_all x1, blocking collectives, on_device(): lax.all_to_all(moved, 'frame', split_axis=0, concat_axis=0, tiled=True)  30.7 us
    unnamed x24, local copies, waits for them, and re-layouts  13.6 us
    all_to_all x1, starting transfers between devices, on_device(): got = lax.all_to_all(sent, 'frame', split_axis=0, concat_axis=0, tiled=True)  12.8 us
    pallas_call x1, Pallas kernels, on_device(): pl.pallas_call(space_attend, grid=(2, ROWS // TILE), out_shape=jax.ShapeD...  10.1 us
    pallas_call x1, Pallas kernels, on_device(): pl.pallas_call(space_project, out_shape=(jax.ShapeDtypeStruct((2, ROWS, H...  8.96 us
    pallas_call x1, Pallas kernels, on_device(): pl.pallas_call(time_project, out_shape=jax.ShapeDtypeStruct((FRAMES, 3 *...  6.83 us
    ppermute x1, starting transfers between devices, on_device(): moved = lax.ppermute(time_out, ('frame', 'head'), handover())  5.77 us
    all_to_all x1, starting transfers between devices, on_device(): lax.all_to_all(space_out, 'head', split_axis=0, concat_axis=0, tiled=True)  4.47 us
  transfers between devices with their start and end apart: 5, of which 4 were waited for; matrix products, arithmetic and copies ran while one was open for 0% of the time, Pallas kernels for 18%

profile of v1, /device:TPU:1, one launch (start us, length us, event | category | flops | bytes accessed | tf_op | source)
XLA Modules:
  0.0 114.2 jit_solution(3328596351901667510)
XLA Ops:
  0.0 0.0 copy-start
  0.0 3.0 %copy-done = bf16[3,3072,384]{2,1,0:T(8,128)(2,1)S(1)} copy-done((bf16[3,3072,384]{2,1,0:T(8,128)(2,1)S(1)}, bf16[3,3072,384]{2,1,0:T(8,128)(2,1)}, u32[]{:S(2)}) %copy-start) | copy-done | bytes 7077912
  3.0 0.0 copy-start.2
  3.0 2.8 %copy-done.2 = bf16[1024,3072]{1,0:T(8,128)(2,1)S(1)} copy-done((bf16[1024,3072]{1,0:T(8,128)(2,1)S(1)}, bf16[1024,3072]{1,0:T(8,128)(2,1)}, u32[]{:S(2)}) %copy-start.2) | copy-done | bytes 6291480
  5.8 0.0 copy-start.4
  5.8 0.7 copy-done.4
  6.5 0.0 copy-start.6
  6.5 0.7 copy-done.6
  7.1 0.0 copy-start.8
  7.1 0.7 copy-done.8
  7.8 0.0 copy-start.11
  7.8 0.0 copy-start.5
  7.8 0.0 copy-start.7
  7.8 0.0 copy-start.9
  7.8 6.8 %time_project.1 = bf16[32,96,128]{2,1,0:T(8,128)(2,1)} custom-call(s32[3]{0:T(128)S(1)} %copy-done.8, bf16[1024,3072]{1,0:T(8,128)(2,1)S(1)} %copy-done.2, bf16[3,3072,384]{2,1,0:T(8,128)(2,1)S(1)} %copy-done, f32[1,128]{1,0:T(1,128)S(1)} %bitcast.2, f32[1,128]{1,0:T(1,128)S(1)} %bitcast.4), custom_call_target="tpu_custom_call" | custom-call | flops 2415919104 | bytes 9000000 | tf_op jit(solution)/shard_map/time_project/pallas_call | solution.py:259
  14.6 12.8 %all-to-all-start.1 = ((bf16[32,96,128]{2,1,0:T(8,128)(2,1)}), bf16[32,96,128]{2,1,0:T(8,128)(2,1)S(1)}, u32[]{:S(2)}, u32[]{:S(2)}) async-start(bf16[32,96,128]{2,1,0:T(8,128)(2,1)} %time_project.1), calls=%async_computation.1 | async-start | bytes 1572864 | tf_op jit(solution)/shard_map/all_to_all | solution.py:274
  27.4 0.0 copy-done.11
  27.4 0.0 copy-done.5
  27.4 0.0 copy-done.7
  27.4 0.0 copy-done.9
  27.5 0.0 copy-start.1
  27.5 3.0 %copy-done.1 = bf16[3,3072,384]{2,1,0:T(8,128)(2,1)S(1)} copy-done((bf16[3,3072,384]{2,1,0:T(8,128)(2,1)S(1)}, bf16[3,3072,384]{2,1,0:T(8,128)(2,1)}, u32[]{:S(2)}) %copy-start.1) | copy-done | bytes 7077912
  30.5 0.0 copy-start.3
  30.5 2.8 %copy-done.3 = bf16[1024,3072]{1,0:T(8,128)(2,1)S(1)} copy-done((bf16[1024,3072]{1,0:T(8,128)(2,1)S(1)}, bf16[1024,3072]{1,0:T(8,128)(2,1)}, u32[]{:S(2)}) %copy-start.3) | copy-done | bytes 6291480
  33.3 9.0 %space_project.1 = (bf16[2,1024,128]{2,1,0:T(8,128)(2,1)S(1)}, bf16[2,2,1024,128]{3,2,1,0:T(8,128)(2,1)S(1)}, bf16[2,2,512,128]{3,2,1,0:T(8,128)(2,1)S(1)}, bf16[2,2,512,128]{3,2,1,0:T(8,128)(2,1)S(1)}, s32[128]{0:T(128)S(1)}) custom-call(s32[3]{0:T(128)S(1)} %copy-done.9, s32[3,128]{1,0:T(4,128)S(1)} %pad.8.live, bf16[1024,3072]{1,0:T(8,128)(2,1)S(1)} %copy-done.3, ...), custom_call_target="tpu_custom_call" | custom-call | flops 4831838208 | bytes 12000000 | tf_op jit(solution)/shard_map/space_project/pallas_call | solution.py:278
  42.2 3.5 %collective-permute-start = (bf16[2,2,512,128]{3,2,1,0:T(8,128)(2,1)S(1)}, bf16[2,2,512,128]{3,2,1,0:T(8,128)(2,1)S(1)}, u32[]{:S(2)}, u32[]{:S(2)}) collective-permute-start(bf16[2,2,512,128]{3,2,1,0:T(8,128)(2,1)S(1)} %get-tuple-element.13), channel_id=1, source_target_pairs={{0,8},{8,16},{16,24},{24,32},{32,40},{40,48},{48,56},{56,64},{64,7... | collective-permute-start | bytes 1572872 | tf_op jit(solution)/shard_map/ppermute | solution.py:299
  45.8 2.1 %collective-permute-start.1 = (bf16[2,2,512,128]{3,2,1,0:T(8,128)(2,1)S(1)}, bf16[2,2,512,128]{3,2,1,0:T(8,128)(2,1)S(1)}, u32[]{:S(2)}, u32[]{:S(2)}) collective-permute-start(bf16[2,2,512,128]{3,2,1,0:T(8,128)(2,1)S(1)} %get-tuple-element.14), channel_id=1, source_target_pairs={{8,0},{16,8},{24,16},{32,24},{40,32},{48,40},{56,48},{64,56},{72,6... | collective-permute-start | bytes 1572872 | tf_op jit(solution)/shard_map/ppermute | solution.py:300
  47.9 4.2 %collective-permute-done.below = bf16[2,2,512,128]{3,2,1,0:T(8,128)(2,1)S(1)} collective-permute-done((bf16[2,2,512,128]{3,2,1,0:T(8,128)(2,1)S(1)}, bf16[2,2,512,128]{3,2,1,0:T(8,128)(2,1)S(1)}, u32[]{:S(2)}, u32[]{:S(2)}) %collective-permute-start) | collective-permute-done | bytes 524320 | tf_op jit(solution)/shard_map/ppermute | solution.py:299
  52.1 4.1 %collective-permute-done.1.above = bf16[2,2,512,128]{3,2,1,0:T(8,128)(2,1)S(1)} collective-permute-done((bf16[2,2,512,128]{3,2,1,0:T(8,128)(2,1)S(1)}, bf16[2,2,512,128]{3,2,1,0:T(8,128)(2,1)S(1)}, u32[]{:S(2)}, u32[]{:S(2)}) %collective-permute-start.1) | collective-permute-done | bytes 524320 | tf_op jit(solution)/shard_map/ppermute | solution.py:300
  56.3 0.0 copy-start.10
  56.3 10.1 %space_attend.1 = bf16[8,144,256]{2,1,0:T(8,128)(2,1)} custom-call(s32[3]{0:T(128)S(1)} %copy-done.9, s32[128]{0:T(128)S(1)} %get-tuple-element.10.lanes, bf16[2,1024,128]{2,1,0:T(8,128)(2,1)S(1)} %get-tuple-element.11.q, bf16[2,2,1024,128]{3,2,1,0:T(8,128)(2,1)S(1)} %get-tuple-element.12.kv, bf16[2,2,512,128]{3,2,1,0:T(8,128)(2,1)S(1)} %collective-permute-done.below, ...), custom_call_target="tpu_custom_call" | custom-call | flops 4294967296 | bytes 4000000 | tf_op jit(solution)/shard_map/space_attend/pallas_call | solution.py:306
  66.3 0.0 all-to-all-done.1.got
  66.3 4.5 %all-to-all-start = ((bf16[8,144,256]{2,1,0:T(8,128)(2,1)}), bf16[8,144,256]{2,1,0:T(8,128)(2,1)S(1)}, u32[]{:S(2)}, u32[]{:S(2)}) async-start(bf16[8,144,256]{2,1,0:T(8,128)(2,1)} %space_attend.1), calls=%async_computation | async-start | bytes 1179648 | tf_op jit(solution)/shard_map/all_to_all | solution.py:329
  70.8 0.0 copy-done.10
  70.8 1.5 %time_attend.1 = bf16[32,32,128]{2,1,0:T(8,128)(2,1)S(1)} custom-call(s32[3]{0:T(128)S(1)} %copy-done.9, s32[3,4,4]{2,1,0:T(4,128)S(1)} %copy-done.10, bf16[32,96,128]{2,1,0:T(8,128)(2,1)S(1)} %all-to-all-done.1.got), custom_call_target="tpu_custom_call" | custom-call | flops 536870912 | bytes 1000000 | tf_op jit(solution)/shard_map/time_attend/pallas_call | solution.py:331
  72.3 5.8 %collective-permute-start.2 = (bf16[32,32,128]{2,1,0:T(8,128)(2,1)S(1)}, bf16[32,32,128]{2,1,0:T(8,128)(2,1)S(1)}, u32[]{:S(2)}, u32[]{:S(2)}) collective-permute-start(bf16[32,32,128]{2,1,0:T(8,128)(2,1)S(1)} %time_attend.1), channel_id=1, source_target_pairs={{0,0},{1,1},{2,2},{3,3},{4,4},{5,5},{6,6},{7,7},{8,14},{9,15},{10,... | collective-permute-start | bytes 786440 | tf_op jit(solution)/shard_map/ppermute | solution.py:340
  78.1 0.1 all-to-all-done.space.slot
  78.2 3.6 %collective-permute-done.2 = bf16[32,32,128]{2,1,0:T(8,128)(2,1)S(1)} collective-permute-done((bf16[32,32,128]{2,1,0:T(8,128)(2,1)S(1)}, bf16[32,32,128]{2,1,0:T(8,128)(2,1)S(1)}, u32[]{:S(2)}, u32[]{:S(2)}) %collective-permute-start.2) | collective-permute-done | bytes 262176 | tf_op jit(solution)/shard_map/ppermute | solution.py:340
  81.9 30.7 %all_to_all.15.timed = bf16[32,32,128]{2,1,0:T(8,128)(2,1)S(1)} all-to-all(bf16[32,32,128]{2,1,0:T(8,128)(2,1)S(1)} %collective-permute-done.2), channel_id=1, replica_groups=mesh['frame'=32,'head'=8] {'frame'}, dimensions={0} | all-to-all | bytes 524288 | tf_op jit(solution)/shard_map/all_to_all | solution.py:341
  112.6 1.6 %assemble.1 = bf16[128,3072]{1,0:T(8,128)(2,1)} custom-call(bf16[8,144,256]{2,1,0:T(8,128)(2,1)S(1)} %all-to-all-done.space.slot, bf16[8,144,256]{2,1,0:T(8,128)(2,1)S(1)} %all-to-all-done.space.slot, bf16[32,32,128]{2,1,0:T(8,128)(2,1)S(1)} %all_to_all.15.timed), custom_call_target="tpu_custom_call" | custom-call | flops 1000000 | bytes 2000000 | tf_op jit(solution)/shard_map/assemble/pallas_call | solution.py:344
  (3 shorter events, 0.0 us)
Async XLA Ops:
  0.0 3.0 %copy-start = (bf16[3,3072,384]{2,1,0:T(8,128)(2,1)S(1)}, bf16[3,3072,384]{2,1,0:T(8,128)(2,1)}, u32[]{:S(2)}) copy-start(bf16[3,3072,384]{2,1,0:T(8,128)(2,1)} %weight.3) | copy-start | bytes 21233668
  3.0 2.8 %copy-start.2 = (bf16[1024,3072]{1,0:T(8,128)(2,1)S(1)}, bf16[1024,3072]{1,0:T(8,128)(2,1)}, u32[]{:S(2)}) copy-start(bf16[1024,3072]{1,0:T(8,128)(2,1)} %tokens.3) | copy-start | bytes 18874372
  5.8 0.7 copy-start.4
  6.5 0.7 copy-start.6
  7.1 0.7 copy-start.8
  7.8 19.6 %copy-start.11 = (s32[3,16,48]{2,1,0:T(8,128)S(1)}, s32[3,16,48]{2,1,0:T(8,128)}, u32[]{:S(2)}) copy-start(s32[3,16,48]{2,1,0:T(8,128)} %param.12) | copy-start | bytes 27652
  7.8 19.7 %copy-start.5 = (f32[128]{0:T(128)S(1)}, f32[128]{0:T(128)}, u32[]{:S(2)}) copy-start(f32[128]{0:T(128)} %param.9) | copy-start | bytes 1540
  7.8 19.7 %copy-start.7 = (f32[128]{0:T(128)S(1)}, f32[128]{0:T(128)}, u32[]{:S(2)}) copy-start(f32[128]{0:T(128)} %param.10) | copy-start | bytes 1540
  7.8 19.7 %copy-start.9 = (s32[3]{0:T(128)S(1)}, s32[3]{0:T(128)}, u32[]{:S(2)}) copy-start(s32[3]{0:T(128)} %labels.7) | copy-start | bytes 40
  14.6 51.7 %all-to-all-start.1 = ((bf16[32,96,128]{2,1,0:T(8,128)(2,1)}), bf16[32,96,128]{2,1,0:T(8,128)(2,1)S(1)}, u32[]{:S(2)}, u32[]{:S(2)}) async-start(bf16[32,96,128]{2,1,0:T(8,128)(2,1)} %time_project.1), calls=%async_computation.1 | async-start | bytes 1572864 | tf_op jit(solution)/shard_map/all_to_all | solution.py:274
  27.5 3.0 %copy-start.1 = (bf16[3,3072,384]{2,1,0:T(8,128)(2,1)S(1)}, bf16[3,3072,384]{2,1,0:T(8,128)(2,1)}, u32[]{:S(2)}) copy-start(bf16[3,3072,384]{2,1,0:T(8,128)(2,1)} %weight.3) | copy-start | bytes 21233668
  30.5 2.8 %copy-start.3 = (bf16[1024,3072]{1,0:T(8,128)(2,1)S(1)}, bf16[1024,3072]{1,0:T(8,128)(2,1)}, u32[]{:S(2)}) copy-start(bf16[1024,3072]{1,0:T(8,128)(2,1)} %tokens.3) | copy-start | bytes 18874372
  42.2 9.9 %collective-permute-start = (bf16[2,2,512,128]{3,2,1,0:T(8,128)(2,1)S(1)}, bf16[2,2,512,128]{3,2,1,0:T(8,128)(2,1)S(1)}, u32[]{:S(2)}, u32[]{:S(2)}) collective-permute-start(bf16[2,2,512,128]{3,2,1,0:T(8,128)(2,1)S(1)} %get-tuple-element.13), channel_id=1, source_target_pairs={{0,8},{8,16},{16,24},{24,32},{32,40},{40,48},{48,56},{56,64},{64,7... | collective-permute-start | bytes 1572872 | tf_op jit(solution)/shard_map/ppermute | solution.py:299
  45.8 10.5 %collective-permute-start.1 = (bf16[2,2,512,128]{3,2,1,0:T(8,128)(2,1)S(1)}, bf16[2,2,512,128]{3,2,1,0:T(8,128)(2,1)S(1)}, u32[]{:S(2)}, u32[]{:S(2)}) collective-permute-start(bf16[2,2,512,128]{3,2,1,0:T(8,128)(2,1)S(1)} %get-tuple-element.14), channel_id=1, source_target_pairs={{8,0},{16,8},{24,16},{32,24},{40,32},{48,40},{56,48},{64,56},{72,6... | collective-permute-start | bytes 1572872 | tf_op jit(solution)/shard_map/ppermute | solution.py:300
  56.3 14.6 %copy-start.10 = (s32[3,4,4]{2,1,0:T(4,128)S(1)}, s32[3,4,4]{2,1,0:T(4,128)}, u32[]{:S(2)}) copy-start(s32[3,4,4]{2,1,0:T(4,128)} %time_mask.1) | copy-start | bytes 580
  66.3 11.9 %all-to-all-start = ((bf16[8,144,256]{2,1,0:T(8,128)(2,1)}), bf16[8,144,256]{2,1,0:T(8,128)(2,1)S(1)}, u32[]{:S(2)}, u32[]{:S(2)}) async-start(bf16[8,144,256]{2,1,0:T(8,128)(2,1)} %space_attend.1), calls=%async_computation | async-start | bytes 1179648 | tf_op jit(solution)/shard_map/all_to_all | solution.py:329
  72.3 9.5 %collective-permute-start.2 = (bf16[32,32,128]{2,1,0:T(8,128)(2,1)S(1)}, bf16[32,32,128]{2,1,0:T(8,128)(2,1)S(1)}, u32[]{:S(2)}, u32[]{:S(2)}) collective-permute-start(bf16[32,32,128]{2,1,0:T(8,128)(2,1)S(1)} %time_attend.1), channel_id=1, source_target_pairs={{0,0},{1,1},{2,2},{3,3},{4,4},{5,5},{6,6},{7,7},{8,14},{9,15},{10,... | collective-permute-start | bytes 786440 | tf_op jit(solution)/shard_map/ppermute | solution.py:340

commit v2 on v1

v2 whole, which is shorter than its diff:
```python
import math

import jax
import jax.numpy as jnp
from jax import lax
from jax.experimental import pallas as pl
from jax.experimental.pallas import tpu as pltpu
from jax.sharding import PartitionSpec as P

STRIP = 8
BLOCK = 64
D = 3072
HD = 128
ROWS = 1024
FRAMES = 32
GROUPS = 8
QBLOCKS = 16
NEAR = 8
CHUNK = 768
PARTS = D // CHUNK
TILE = 256
EPSILON = 1e-06
SCALE = math.log2(math.e) / math.sqrt(HD)
BLOCKED = -16384.0
DEAD = 64

bf16 = jnp.bfloat16
f32 = jnp.float32


def slots_of(labels):
    time = labels[1] + 2 * labels[2]
    return time, jnp.where(time == 0, 1, 0), jnp.where(time == 2, 1, 2)


def normed(x, gain):
    inverse = lax.rsqrt(jnp.mean(x * x, axis=-1, keepdims=True) + EPSILON)
    return (x * inverse * gain).astype(bf16)


def load_parts(tokens, weight, columns, tok, wts, sems):
    def copies(c):
        made = [
            pltpu.make_async_copy(
                tokens.at[:, pl.ds(c * CHUNK, CHUNK)], tok.at[:, pl.ds(c * CHUNK, CHUNK)], sems.at[c, 0]
            )
        ]
        for i, (k, slot) in enumerate(columns):
            made.append(
                pltpu.make_async_copy(
                    weight.at[k, pl.ds(c * CHUNK, CHUNK), pl.ds(pl.multiple_of(slot * HD, HD), HD)],
                    wts.at[pl.ds(c * CHUNK, CHUNK), pl.ds(i * HD, HD)],
                    sems.at[c, 1 + i],
                )
            )
        return made

    return copies


def project(tokens, weight, columns, tok, wts, acc, sems):
    copies = load_parts(tokens, weight, columns, tok, wts, sems)
    for c in range(2):
        for copy in copies(c):
            copy.start()
    for c in range(PARTS):
        for copy in copies(c):
            copy.wait()
        if c + 2 < PARTS:
            for copy in copies(c + 2):
                copy.start()
        part = jnp.dot(
            tok[:, pl.ds(c * CHUNK, CHUNK)], wts[pl.ds(c * CHUNK, CHUNK), :], preferred_element_type=f32
        )
        if c == 0:
            acc[...] = part
        else:
            acc[...] += part


def time_project(labels, tokens, weight, query_gain, key_gain, out, tok, wts, acc, sems):
    time, _, _ = slots_of(labels)
    project(tokens, weight, [(0, time), (1, time), (2, time)], tok, wts, acc, sems)
    for b in range(FRAMES):
        rows = pl.ds(b * FRAMES, FRAMES)
        out[b, 0:FRAMES, :] = normed(acc[rows, 0:HD], query_gain[...] * SCALE)
        out[b, FRAMES : 2 * FRAMES, :] = normed(acc[rows, HD : 2 * HD], key_gain[...])
        out[b, 2 * FRAMES :, :] = acc[rows, 2 * HD :].astype(bf16)


def space_project(labels, live, tokens, weight, query_gain, key_gain, q, kv, up, down, lanes, tok, wts, acc, sems):
    _, first, second = slots_of(labels)
    columns = [(k, slot) for k in range(3) for slot in (first, second)]
    for h, slot in enumerate((first, second)):
        for side in range(2):
            base = (2 * h + side) * 32
            for j in range(32):
                lanes[base + j] = DEAD
            count = 0
            for b in range(QBLOCKS):
                column = 2 * QBLOCKS * side + b
                alive = live[slot, column]
                lanes[base + count] = jnp.where(alive > 0, column, DEAD)
                count = count + (alive > 0).astype(jnp.int32)
    project(tokens, weight, columns, tok, wts, acc, sems)
    for h in range(2):
        for r in range(ROWS // TILE):
            rows = pl.ds(r * TILE, TILE)
            q[h, rows, :] = normed(acc[rows, h * HD : (h + 1) * HD], query_gain[...] * SCALE)
            kv[h, 0, rows, :] = normed(acc[rows, (2 + h) * HD : (3 + h) * HD], key_gain[...])
            kv[h, 1, rows, :] = acc[rows, (4 + h) * HD : (5 + h) * HD].astype(bf16)
        for side, packed in enumerate((up, down)):
            for j in range(NEAR):
                block = lanes[(2 * h + side) * 32 + j] & (QBLOCKS - 1)
                rows = pl.ds(pl.multiple_of(block * BLOCK, BLOCK), BLOCK)
                for part in range(2):
                    packed[h, part, pl.ds(j * BLOCK, BLOCK), :] = kv[h, part, rows, :]


def one_hot(rows, lane):
    return (lax.broadcasted_iota(jnp.int32, (rows, HD), 1) == lane).astype(f32).astype(bf16)


def space_attend(labels, lanes, q, kv, below, above, mask, after, out, keys, vals):
    _, *slots = slots_of(labels)
    frame = lax.axis_index("frame")
    near = NEAR * BLOCK
    for b in range(QBLOCKS):
        own = one_hot(BLOCK, QBLOCKS + b)
        for h in range(2):
            keys[h, pl.ds(b * BLOCK, BLOCK), HD:] = own
    for h in range(2):
        keys[h, 0:ROWS, 0:HD] = kv[h, 0]
        vals[h, 0:ROWS, 0:HD] = kv[h, 1]
        vals[h, :, HD:] = jnp.ones((ROWS + 2 * near, HD), bf16)
        for side, got in enumerate((below, above)):
            rows = pl.ds(ROWS + side * near, near)
            keys[h, rows, 0:HD] = got[h, 0]
            vals[h, rows, 0:HD] = got[h, 1]
            for j in range(NEAR):
                lane = lanes[(2 * h + side) * 32 + j]
                keys[h, pl.ds(ROWS + side * near + j * BLOCK, BLOCK), HD:] = one_hot(BLOCK, lane)

    lane = lax.broadcasted_iota(jnp.int32, (QBLOCKS, HD), 1)
    per = TILE // BLOCK
    width = 512
    per_target = ROWS // GROUPS
    for h in range(2):
        table = mask[slots[h]].astype(f32)
        table = jnp.where((lane < QBLOCKS) & (frame == 0), 0.0, table)
        table = jnp.where((lane >= 2 * QBLOCKS) & (frame == FRAMES - 1), 0.0, table)
        bias = (table - 1.0) * -BLOCKED
        for t in range(ROWS // TILE):
            rows = [jnp.broadcast_to(bias[t * per + i : t * per + i + 1], (BLOCK, HD)) for i in range(per)]
            query = jnp.concatenate(
                [q[h, pl.ds(t * TILE, TILE), :], jnp.concatenate(rows, axis=0).astype(bf16)], axis=1
            )
            total = jnp.zeros((TILE, 2 * HD), f32)
            for c in range((ROWS + 2 * near) // width):
                part = pl.ds(c * width, width)
                scores = lax.dot_general(
                    query, keys[h, part, :], (((1,), (1,)), ((), ())), preferred_element_type=f32
                )
                weight = jnp.exp2(scores).astype(bf16)
                total = total + jnp.dot(weight, vals[h, part, :], preferred_element_type=f32)
            mixed = (total[:, 0:HD] / total[:, HD:]).astype(bf16)
            targets = pl.ds(t * TILE // per_target, TILE // per_target)
            column = pl.ds(pl.multiple_of(slots[h] * HD, HD), HD)
            out[targets, :, column] = mixed.reshape(-1, per_target, HD)


def time_attend(labels, time_mask, got, out, done):
    done[...] = jnp.zeros_like(done)
    time, _, _ = slots_of(labels)
    lane = lax.broadcasted_iota(jnp.int32, (16, HD), 1)
    row = lax.broadcasted_iota(jnp.int32, (16, HD), 0)
    same = (lane & 1) == (row >> 3)
    tables = []
    for a in range(4):
        allowed = jnp.zeros((16, HD), jnp.int32)
        for b in range(4):
            allowed = jnp.where((lane >> 1) == b, time_mask[time, a, b], allowed)
        table = jnp.where(same & (allowed == 1), 0.0, BLOCKED).astype(bf16)
        tables.append(jnp.broadcast_to(table[None], (8, 16, HD)))
    bias = jnp.concatenate(tables, axis=0).reshape(512, HD)
    key_frame = lax.broadcasted_iota(jnp.int32, (512, HD), 0)
    key_lane = lax.broadcasted_iota(jnp.int32, (512, HD), 1)
    mark = (((key_frame >> 7) * 2 + ((key_frame >> 3) & 1)) == key_lane).astype(f32).astype(bf16)
    ones = jnp.ones((512, HD), bf16)
    for u in range(2):
        def rows(part):
            return got[:, pl.ds(part * FRAMES + u * 16, 16), :].reshape(512, HD)

        query = jnp.concatenate([rows(0), bias], axis=1)
        keys = jnp.concatenate([rows(1), mark], axis=1)
        vals = jnp.concatenate([rows(2), ones], axis=1)
        scores = lax.dot_general(query, keys, (((1,), (1,)), ((), ())), preferred_element_type=f32)
        weight = jnp.exp2(scores).astype(bf16)
        total = jnp.dot(weight, vals, preferred_element_type=f32)
        mixed = (total[:, 0:HD] / total[:, HD:]).astype(bf16)
        out[:, pl.ds(u * 16, 16), :] = mixed.reshape(FRAMES, 16, HD)


def merge(labels, space, timed, out, sem):
    time, _, _ = slots_of(labels)
    column = pl.ds(pl.multiple_of(time * HD, HD), HD)
    copy = pltpu.make_async_copy(timed, out.at[:, :, column], sem)
    copy.start()
    copy.wait()


def assemble(parts, out, sems):
    width = parts.shape[2]
    copies = [
        pltpu.make_async_copy(parts.at[g], out.at[:, pl.ds(g * width, width)], sems.at[g]) for g in range(GROUPS)
    ]
    for copy in copies:
        copy.start()
    for copy in copies:
        copy.wait()


def params(mib):
    return pltpu.CompilerParams(vmem_limit_bytes=mib * 2**20)


def cost(flops, moved, exps=0):
    return pl.CostEstimate(flops=int(flops), bytes_accessed=int(moved), transcendentals=int(exps))


SMEM = pl.BlockSpec(memory_space=pltpu.SMEM)
VMEM = pl.BlockSpec(memory_space=pltpu.VMEM)
ANY = pl.BlockSpec(memory_space=pl.ANY)


def on_device(tokens, qkv_weight, query_gain, key_gain, labels, space_mask, time_mask):
    gains = (query_gain.reshape(1, HD), key_gain.reshape(1, HD))
    sent = pl.pallas_call(
        time_project,
        out_shape=jax.ShapeDtypeStruct((FRAMES, 3 * FRAMES, HD), bf16),
        in_specs=[SMEM, ANY, ANY, VMEM, VMEM],
        out_specs=VMEM,
        scratch_shapes=[
            pltpu.VMEM((ROWS, D), bf16),
            pltpu.VMEM((D, 3 * HD), bf16),
            pltpu.VMEM((ROWS, 3 * HD), f32),
            pltpu.SemaphoreType.DMA((PARTS, 4)),
        ],
        compiler_params=params(60),
        cost_estimate=cost(2 * ROWS * D * 3 * HD, 9e6),
        name="time_project",
    )(labels, tokens, qkv_weight, *gains)
    got = lax.all_to_all(sent, "frame", split_axis=0, concat_axis=0, tiled=True)

    live = jnp.pad(jnp.max(space_mask, axis=1), ((0, 0), (0, HD - 3 * QBLOCKS)))
    pair = jax.ShapeDtypeStruct((2, 2, NEAR * BLOCK, HD), bf16)
    q, kv, up, down, lanes = pl.pallas_call(
        space_project,
        out_shape=(
            jax.ShapeDtypeStruct((2, ROWS, HD), bf16),
            jax.ShapeDtypeStruct((2, 2, ROWS, HD), bf16),
            pair,
            pair,
            jax.ShapeDtypeStruct((HD,), jnp.int32),
        ),
        in_specs=[SMEM, SMEM, ANY, ANY, VMEM, VMEM],
        out_specs=(VMEM, VMEM, VMEM, VMEM, SMEM),
        scratch_shapes=[
            pltpu.VMEM((ROWS, D), bf16),
            pltpu.VMEM((D, 6 * HD), bf16),
            pltpu.VMEM((ROWS, 6 * HD), f32),
            pltpu.SemaphoreType.DMA((PARTS, 7)),
        ],
        compiler_params=params(58),
        cost_estimate=cost(2 * ROWS * D * 6 * HD, 12e6),
        name="space_project",
    )(labels, live, tokens, qkv_weight, *gains)
    below = lax.ppermute(up, "frame", [(i, i + 1) for i in range(FRAMES - 1)])
    above = lax.ppermute(down, "frame", [(i + 1, i) for i in range(FRAMES - 1)])

    time_out, done = pl.pallas_call(
        time_attend,
        out_shape=(jax.ShapeDtypeStruct((FRAMES, FRAMES, HD), bf16), jax.ShapeDtypeStruct((8, HD), f32)),
        in_specs=[SMEM, SMEM, VMEM],
        out_specs=(VMEM, VMEM),
        compiler_params=params(16),
        cost_estimate=cost(8 * 512 * 512 * 2 * HD, 1e6, 2 * 512 * 512),
        name="time_attend",
    )(labels, time_mask, got)

    mask = jnp.pad(space_mask, ((0, 0), (0, 0), (0, HD - 3 * QBLOCKS)))
    total_keys = ROWS + 2 * NEAR * BLOCK
    per_target = ROWS // GROUPS
    space_out = pl.pallas_call(
        space_attend,
        out_shape=jax.ShapeDtypeStruct((GROUPS, per_target, 3 * HD), bf16),
        in_specs=[SMEM, SMEM] + [VMEM] * 5 + [ANY],
        out_specs=VMEM,
        scratch_shapes=[
            pltpu.VMEM((2, total_keys, 2 * HD), bf16),
            pltpu.VMEM((2, total_keys, 2 * HD), bf16),
        ],
        compiler_params=params(16),
        cost_estimate=cost(2 * 4 * ROWS * total_keys * 2 * HD, 4e6, 2 * ROWS * total_keys),
        name="space_attend",
    )(labels, lanes, q, kv, below, above, mask, done)
    timed = lax.all_to_all(time_out, "frame", split_axis=0, concat_axis=0, tiled=True)
    merged = pl.pallas_call(
        merge,
        out_shape=jax.ShapeDtypeStruct((GROUPS, per_target, 3 * HD), bf16),
        in_specs=[SMEM, ANY, ANY],
        out_specs=ANY,
        scratch_shapes=[pltpu.SemaphoreType.DMA],
        input_output_aliases={1: 0},
        compiler_params=params(16),
        cost_estimate=cost(1, 5e5),
        name="merge",
    )(labels, space_out, timed.reshape(GROUPS, per_target, HD))
    parts = lax.all_to_all(merged, "head", split_axis=0, concat_axis=0, tiled=True)
    return pl.pallas_call(
        assemble,
        out_shape=jax.ShapeDtypeStruct((per_target, 3 * GROUPS * HD), bf16),
        in_specs=[ANY],
        out_specs=ANY,
        scratch_shapes=[pltpu.SemaphoreType.DMA((GROUPS,))],
        compiler_params=params(16),
        cost_estimate=cost(1, 2e6),
        name="assemble",
    )(parts)


def solution(mesh):
    placed = (
        P("frame", None),
        P(None, None, "head"),
        P(),
        P(),
        P("head"),
        P("head", None, None),
        P("head", None, None),
    )
    return jax.shard_map(
        on_device, mesh=mesh, in_specs=placed, out_specs=P(("frame", "head"), None), check_vma=False
    )
```

time: 115 us -> 84.3 us (0.73)
  the two profiles are of different devices: /device:TPU:1 before, /device:TPU:8 now
where the time goes in v2:
time: 84.3 us; the launch traced here: 83.1 us
  Pallas kernels  28.7 us (34%)
  starting transfers between devices  25.2 us (30%)
  blocking collectives  18.8 us (22%)
  waiting for transfers between devices  6.58 us (8%)
  local copies, waits for them, and re-layouts  3.47 us (4%)
    all_to_all x1, blocking collectives, on_device(): lax.all_to_all(merged, 'head', split_axis=0, concat_axis=0, tiled=True)  18.8 us
    pallas_call x1, Pallas kernels, on_device(): pl.pallas_call(space_project, out_shape=(jax.ShapeDtypeStruct((2, ROWS, H...  12.3 us
    all_to_all x1, starting transfers between devices, on_device(): got = lax.all_to_all(sent, 'frame', split_axis=0, concat_axis=0, tiled=True)  11.7 us
    all_to_all x1, starting transfers between devices, on_device(): lax.all_to_all(time_out, 'frame', split_axis=0, concat_axis=0, tiled=True)  7.97 us
    pallas_call x1, Pallas kernels, on_device(): pl.pallas_call(time_project, out_shape=jax.ShapeDtypeStruct((FRAMES, 3 *...  7.02 us
    pallas_call x1, Pallas kernels, on_device(): pl.pallas_call(space_attend, out_shape=jax.ShapeDtypeStruct((GROUPS, per_...  5.63 us
    all_to_all x1, waiting for transfers between devices, on_device(): got = lax.all_to_all(sent, 'frame', split_axis=0, concat_axis=0, tiled=True)  3.65 us
    ppermute x1, starting transfers between devices, on_device(): above = lax.ppermute(down, 'frame', [(i + 1, i) for i in range(FRAMES - 1)])  3.5 us
  transfers between devices with their start and end apart: 4, of which 2 were waited for; matrix products, arithmetic and copies ran while one was open for 1% of the time, Pallas kernels for 24%

profile of v2, /device:TPU:8, one launch (start us, length us, event | category | flops | bytes accessed | tf_op | source)
XLA Modules:
  0.0 83.1 jit_solution(12172127218826110066)
XLA Ops:
  0.0 0.0 copy-start.5
  0.0 7.0 %time_project.1 = bf16[32,96,128]{2,1,0:T(8,128)(2,1)} custom-call(s32[3]{0:T(128)} %labels.9, bf16[1024,3072]{1,0:T(8,128)(2,1)} %tokens.3, bf16[3,3072,384]{2,1,0:T(8,128)(2,1)} %weight.3, f32[1,128]{1,0:T(1,128)} %bitcast.4, f32[1,128]{1,0:T(1,128)} %bitcast.6), custom_call_target="tpu_custom_call" | custom-call | flops 2415919104 | bytes 9000000 | tf_op jit(solution)/shard_map/time_project/pallas_call | solution.py:238
  7.0 11.7 %all-to-all-start = ((bf16[32,96,128]{2,1,0:T(8,128)(2,1)}), bf16[32,96,128]{2,1,0:T(8,128)(2,1)S(1)}, u32[]{:S(2)}, u32[]{:S(2)}) async-start(bf16[32,96,128]{2,1,0:T(8,128)(2,1)} %time_project.1), calls=%async_computation | async-start | bytes 1572864 | tf_op jit(solution)/shard_map/all_to_all | solution.py:253
  18.7 0.0 copy-done.5
  18.8 0.6 pad.8.live
  19.4 0.0 copy-start
  19.4 0.0 copy-start.1
  19.4 12.3 %space_project.1 = (bf16[2,1024,128]{2,1,0:T(8,128)(2,1)}, bf16[2,2,1024,128]{3,2,1,0:T(8,128)(2,1)}, bf16[2,2,512,128]{3,2,1,0:T(8,128)(2,1)}, bf16[2,2,512,128]{3,2,1,0:T(8,128)(2,1)}, s32[128]{0:T(128)}) custom-call(s32[3]{0:T(128)} %labels.9, s32[3,128]{1,0:T(4,128)} %pad.8.live, bf16[1024,3072]{1,0:T(8,128)(2,1)} %tokens.3, ...), custom_call_target="tpu_custom_call" | custom-call | flops 4831838208 | bytes 12000000 | tf_op jit(solution)/shard_map/space_project/pallas_call | solution.py:257
  31.7 2.1 %collective-permute-start = (bf16[2,2,512,128]{3,2,1,0:T(8,128)(2,1)}, bf16[2,2,512,128]{3,2,1,0:T(8,128)(2,1)S(1)}, u32[]{:S(2)}, u32[]{:S(2)}) collective-permute-start(bf16[2,2,512,128]{3,2,1,0:T(8,128)(2,1)} %get-tuple-element.15), channel_id=1, source_target_pairs={{0,8},{8,16},{16,24},{24,32},{32,40},{40,48},{48,56},{56,64},{64,7... | collective-permute-start | bytes 1572872 | tf_op jit(solution)/shard_map/ppermute | solution.py:278
  33.8 3.5 %collective-permute-start.1 = (bf16[2,2,512,128]{3,2,1,0:T(8,128)(2,1)}, bf16[2,2,512,128]{3,2,1,0:T(8,128)(2,1)S(1)}, u32[]{:S(2)}, u32[]{:S(2)}) collective-permute-start(bf16[2,2,512,128]{3,2,1,0:T(8,128)(2,1)} %get-tuple-element.16), channel_id=1, source_target_pairs={{8,0},{16,8},{24,16},{32,24},{40,32},{48,40},{56,48},{64,56},{72,6... | collective-permute-start | bytes 1572872 | tf_op jit(solution)/shard_map/ppermute | solution.py:279
  37.3 3.6 %all-to-all-done.got = bf16[32,96,128]{2,1,0:T(8,128)(2,1)S(1)} async-done(((bf16[32,96,128]{2,1,0:T(8,128)(2,1)}), bf16[32,96,128]{2,1,0:T(8,128)(2,1)S(1)}, u32[]{:S(2)}, u32[]{:S(2)}) %all-to-all-start) | async-done | bytes 786464 | tf_op jit(solution)/shard_map/all_to_all | solution.py:253
  41.0 0.0 copy-done
  41.0 0.0 copy-done.1
  41.0 2.2 %time_attend.1 = (bf16[32,32,128]{2,1,0:T(8,128)(2,1)}, f32[8,128]{1,0:T(8,128)S(1)}) custom-call(s32[3]{0:T(128)S(1)} %copy-done, s32[3,4,4]{2,1,0:T(4,128)S(1)} %copy-done.1, bf16[32,96,128]{2,1,0:T(8,128)(2,1)S(1)} %all-to-all-done.got), custom_call_target="tpu_custom_call" | custom-call | flops 536870912 | bytes 1000000 | tf_op jit(solution)/shard_map/time_attend/pallas_call | solution.py:281
  43.2 8.0 %all-to-all-start.1 = ((bf16[32,32,128]{2,1,0:T(8,128)(2,1)}), bf16[32,32,128]{2,1,0:T(8,128)(2,1)S(1)}, u32[]{:S(2)}, u32[]{:S(2)}) async-start(bf16[32,32,128]{2,1,0:T(8,128)(2,1)} %get-tuple-element.18), calls=%async_computation.1 | async-start | bytes 524288 | tf_op jit(solution)/shard_map/all_to_all | solution.py:307
  51.2 0.0 collective-permute-done.below
  51.2 0.0 collective-permute-done.1.above
  51.2 0.0 copy-start.2
  51.2 1.2 %copy-done.2 = bf16[2,2,1024,128]{3,2,1,0:T(8,128)(2,1)S(1)} copy-done((bf16[2,2,1024,128]{3,2,1,0:T(8,128)(2,1)S(1)}, bf16[2,2,1024,128]{3,2,1,0:T(8,128)(2,1)}, u32[]{:S(2)}) %copy-start.2) | copy-done | bytes 1048600
  52.4 0.0 copy-start.3
  52.4 1.0 %copy-done.3 = bf16[2,1024,128]{2,1,0:T(8,128)(2,1)S(1)} copy-done((bf16[2,1024,128]{2,1,0:T(8,128)(2,1)S(1)}, bf16[2,1024,128]{2,1,0:T(8,128)(2,1)}, u32[]{:S(2)}) %copy-start.3) | copy-done | bytes 524312
  53.4 0.0 copy-start.4
  53.4 0.6 copy-done.4
  54.0 5.6 %space_attend.1.space = bf16[8,128,384]{2,1,0:T(8,128)(2,1)S(1)} custom-call(s32[3]{0:T(128)S(1)} %copy-done, s32[128]{0:T(128)S(1)} %copy-done.4, bf16[2,1024,128]{2,1,0:T(8,128)(2,1)S(1)} %copy-done.3, bf16[2,2,1024,128]{3,2,1,0:T(8,128)(2,1)S(1)} %copy-done.2, bf16[2,2,512,128]{3,2,1,0:T(8,128)(2,1)S(1)} %collective-permute-done.below, ...), custom_call_target="tpu_custom_call" | custom-call | flops 4294967296 | bytes 4000000 | tf_op jit(solution)/shard_map/space_attend/pallas_call | solution.py:294
  59.7 2.9 %all-to-all-done.1 = bf16[32,32,128]{2,1,0:T(8,128)(2,1)S(1)} async-done(((bf16[32,32,128]{2,1,0:T(8,128)(2,1)}), bf16[32,32,128]{2,1,0:T(8,128)(2,1)S(1)}, u32[]{:S(2)}, u32[]{:S(2)}) %all-to-all-start.1) | async-done | bytes 262176 | tf_op jit(solution)/shard_map/all_to_all | solution.py:307
  62.6 0.6 merge.1
  63.2 18.8 %all_to_all.15.parts = bf16[8,128,384]{2,1,0:T(8,128)(2,1)S(1)} all-to-all(bf16[8,128,384]{2,1,0:T(8,128)(2,1)S(1)} %merge.1), channel_id=1, replica_groups=mesh['frame'=32,'head'=8] {'head'}, dimensions={0} | all-to-all | bytes 1572864 | tf_op jit(solution)/shard_map/all_to_all | solution.py:319
  82.0 0.9 %assemble.1 = bf16[128,3072]{1,0:T(8,128)(2,1)} custom-call(bf16[8,128,384]{2,1,0:T(8,128)(2,1)S(1)} %all_to_all.15.parts), custom_call_target="tpu_custom_call" | custom-call | flops 1 | bytes 2000000 | tf_op jit(solution)/shard_map/assemble/pallas_call | solution.py:320
  (2 shorter events, 0.0 us)
Async XLA Ops:
  0.0 18.7 %copy-start.5 = (s32[3,16,48]{2,1,0:T(8,128)S(1)}, s32[3,16,48]{2,1,0:T(8,128)}, u32[]{:S(2)}) copy-start(s32[3,16,48]{2,1,0:T(8,128)} %param.12) | copy-start | bytes 27652
  7.0 33.9 %all-to-all-start = ((bf16[32,96,128]{2,1,0:T(8,128)(2,1)}), bf16[32,96,128]{2,1,0:T(8,128)(2,1)S(1)}, u32[]{:S(2)}, u32[]{:S(2)}) async-start(bf16[32,96,128]{2,1,0:T(8,128)(2,1)} %time_project.1), calls=%async_computation | async-start | bytes 1572864 | tf_op jit(solution)/shard_map/all_to_all | solution.py:253
  19.4 21.6 %copy-start = (s32[3]{0:T(128)S(1)}, s32[3]{0:T(128)}, u32[]{:S(2)}) copy-start(s32[3]{0:T(128)} %labels.9) | copy-start | bytes 40
  19.4 21.6 %copy-start.1 = (s32[3,4,4]{2,1,0:T(4,128)S(1)}, s32[3,4,4]{2,1,0:T(4,128)}, u32[]{:S(2)}) copy-start(s32[3,4,4]{2,1,0:T(4,128)} %time_mask.1) | copy-start | bytes 580
  31.7 19.4 %collective-permute-start = (bf16[2,2,512,128]{3,2,1,0:T(8,128)(2,1)}, bf16[2,2,512,128]{3,2,1,0:T(8,128)(2,1)S(1)}, u32[]{:S(2)}, u32[]{:S(2)}) collective-permute-start(bf16[2,2,512,128]{3,2,1,0:T(8,128)(2,1)} %get-tuple-element.15), channel_id=1, source_target_pairs={{0,8},{8,16},{16,24},{24,32},{32,40},{40,48},{48,56},{56,64},{64,7... | collective-permute-start | bytes 1572872 | tf_op jit(solution)/shard_map/ppermute | solution.py:278
  33.8 17.4 %collective-permute-start.1 = (bf16[2,2,512,128]{3,2,1,0:T(8,128)(2,1)}, bf16[2,2,512,128]{3,2,1,0:T(8,128)(2,1)S(1)}, u32[]{:S(2)}, u32[]{:S(2)}) collective-permute-start(bf16[2,2,512,128]{3,2,1,0:T(8,128)(2,1)} %get-tuple-element.16), channel_id=1, source_target_pairs={{8,0},{16,8},{24,16},{32,24},{40,32},{48,40},{56,48},{64,56},{72,6... | collective-permute-start | bytes 1572872 | tf_op jit(solution)/shard_map/ppermute | solution.py:279
  43.2 19.4 %all-to-all-start.1 = ((bf16[32,32,128]{2,1,0:T(8,128)(2,1)}), bf16[32,32,128]{2,1,0:T(8,128)(2,1)S(1)}, u32[]{:S(2)}, u32[]{:S(2)}) async-start(bf16[32,32,128]{2,1,0:T(8,128)(2,1)} %get-tuple-element.18), calls=%async_computation.1 | async-start | bytes 524288 | tf_op jit(solution)/shard_map/all_to_all | solution.py:307
  51.2 1.2 %copy-start.2 = (bf16[2,2,1024,128]{3,2,1,0:T(8,128)(2,1)S(1)}, bf16[2,2,1024,128]{3,2,1,0:T(8,128)(2,1)}, u32[]{:S(2)}) copy-start(bf16[2,2,1024,128]{3,2,1,0:T(8,128)(2,1)} %get-tuple-element.14.kv) | copy-start | bytes 3145732
  52.4 1.0 %copy-start.3 = (bf16[2,1024,128]{2,1,0:T(8,128)(2,1)S(1)}, bf16[2,1024,128]{2,1,0:T(8,128)(2,1)}, u32[]{:S(2)}) copy-start(bf16[2,1024,128]{2,1,0:T(8,128)(2,1)} %get-tuple-element.13.q) | copy-start | bytes 1572868
  53.4 0.6 copy-start.4

commit v3 on v2

--- a/solution.py
+++ b/solution.py
@@ -21,8 +21,12 @@
 TILE = 256
 EPSILON = 1e-06
 SCALE = math.log2(math.e) / math.sqrt(HD)
+OUT = FRAMES // GROUPS
+LABEL_ROWS = 16
 BLOCKED = -16384.0
 DEAD = 64
+
+SPACE_MIB = 58
 
 bf16 = jnp.bfloat16
 f32 = jnp.float32
@@ -31,6 +35,35 @@
 def slots_of(labels):
     time = labels[1] + 2 * labels[2]
     return time, jnp.where(time == 0, 1, 0), jnp.where(time == 2, 1, 2)
+
+
+def swapped(two_bits):
+    return (two_bits & 1) * 2 + ((two_bits >> 1) & 1)
+
+
+def owner_of(source, target, quarter):
+    flip = (source >> 2) ^ (target >> 2)
+    shift = (target - source) & 3
+    return (quarter * 4 + swapped((shift - 2 * flip) & 3)) * 2 + flip
+
+
+def handover():
+    pairs = []
+    for owner in range(FRAMES):
+        flip = owner & 1
+        shift = (swapped((owner >> 1) & 3) + 2 * flip) & 3
+        for head in range(GROUPS):
+            target = ((head >> 2) ^ flip) * 4 + ((head + shift) & 3)
+            pairs.append((owner * GROUPS + head, owner * GROUPS + target))
+    return pairs
+
+
+def target_of(head, step):
+    return ((head >> 2) ^ (step >> 2)) * 4 + ((head + step) & 3)
+
+
+def source_of(head, step):
+    return ((head >> 2) ^ (step >> 2)) * 4 + ((head - step) & 3)
 
 
 def normed(x, gain):
@@ -58,11 +91,13 @@
     return copies
 
 
-def project(tokens, weight, columns, tok, wts, acc, sems):
+def project(tokens, weight, columns, tok, wts, acc, sems, meanwhile=None):
     copies = load_parts(tokens, weight, columns, tok, wts, sems)
     for c in range(2):
         for copy in copies(c):
             copy.start()
+    if meanwhile is not None:
+        meanwhile()
     for c in range(PARTS):
         for copy in copies(c):
             copy.wait()
@@ -81,28 +116,34 @@
 def time_project(labels, tokens, weight, query_gain, key_gain, out, tok, wts, acc, sems):
     time, _, _ = slots_of(labels)
     project(tokens, weight, [(0, time), (1, time), (2, time)], tok, wts, acc, sems)
+    head = lax.axis_index("head")
     for b in range(FRAMES):
+        owner = owner_of(head, b // OUT, b % OUT)
         rows = pl.ds(b * FRAMES, FRAMES)
-        out[b, 0:FRAMES, :] = normed(acc[rows, 0:HD], query_gain[...] * SCALE)
-        out[b, FRAMES : 2 * FRAMES, :] = normed(acc[rows, HD : 2 * HD], key_gain[...])
-        out[b, 2 * FRAMES :, :] = acc[rows, 2 * HD :].astype(bf16)
-
-
-def space_project(labels, live, tokens, weight, query_gain, key_gain, q, kv, up, down, lanes, tok, wts, acc, sems):
-    _, first, second = slots_of(labels)
-    columns = [(k, slot) for k in range(3) for slot in (first, second)]
-    for h, slot in enumerate((first, second)):
+        out[owner, 0:FRAMES, :] = normed(acc[rows, 0:HD], query_gain[...] * SCALE)
+        out[owner, FRAMES : 2 * FRAMES, :] = normed(acc[rows, HD : 2 * HD], key_gain[...])
+        out[owner, 2 * FRAMES :, :] = acc[rows, 2 * HD :].astype(bf16)
+
+
+def list_near(labels, live, lanes):
+    _, *slots = slots_of(labels)
+    for h in range(2):
         for side in range(2):
             base = (2 * h + side) * 32
-            for j in range(32):
+            for j in range(NEAR):
                 lanes[base + j] = DEAD
             count = 0
             for b in range(QBLOCKS):
                 column = 2 * QBLOCKS * side + b
-                alive = live[slot, column]
-                lanes[base + count] = jnp.where(alive > 0, column, DEAD)
-                count = count + (alive > 0).astype(jnp.int32)
-    project(tokens, weight, columns, tok, wts, acc, sems)
+                alive = live[slots[h], column] > 0
+                lanes[base + count] = jnp.where(alive, column, DEAD)
+                count = count + alive.astype(jnp.int32)
+
+
+def space_project(labels, live, tokens, weight, query_gain, key_gain, q, kv, up, down, tok, wts, acc, lanes, sems):
+    _, first, second = slots_of(labels)
+    columns = [(k, slot) for k in range(3) for slot in (first, second)]
+    project(tokens, weight, columns, tok, wts, acc, sems, lambda: list_near(labels, live, lanes))
     for h in range(2):
         for r in range(ROWS // TILE):
             rows = pl.ds(r * TILE, TILE)
@@ -121,52 +162,72 @@
     return (lax.broadcasted_iota(jnp.int32, (rows, HD), 1) == lane).astype(f32).astype(bf16)
 
 
-def space_attend(labels, lanes, q, kv, below, above, mask, after, out, keys, vals):
-    _, *slots = slots_of(labels)
+def space_attend(labels, live, mask, q, kv, below, above, after, *rest):
+    outs = rest[:GROUPS]
+    keys, vals, query, bias, lanes, sems = rest[GROUPS:]
+    time, *slots = slots_of(labels)
     frame = lax.axis_index("frame")
+    head = lax.axis_index("head")
     near = NEAR * BLOCK
-    for b in range(QBLOCKS):
-        own = one_hot(BLOCK, QBLOCKS + b)
-        for h in range(2):
-            keys[h, pl.ds(b * BLOCK, BLOCK), HD:] = own
+    rows = [pl.ds(0, ROWS), pl.ds(ROWS, near), pl.ds(ROWS + near, near)]
+    left = pl.ds(0, HD)
+
+    def copies(h):
+        made = [pltpu.make_async_copy(q.at[h], query.at[h, :, left], sems.at[h, 0])]
+        for i, got in enumerate((kv, below, above)):
+            for part, kept in enumerate((keys, vals)):
+                made.append(
+                    pltpu.make_async_copy(got.at[h, part], kept.at[h, rows[i], left], sems.at[h, 1 + 2 * i + part])
+                )
+        return made
+
     for h in range(2):
-        keys[h, 0:ROWS, 0:HD] = kv[h, 0]
-        vals[h, 0:ROWS, 0:HD] = kv[h, 1]
-        vals[h, :, HD:] = jnp.ones((ROWS + 2 * near, HD), bf16)
-        for side, got in enumerate((below, above)):
-            rows = pl.ds(ROWS + side * near, near)
-            keys[h, rows, 0:HD] = got[h, 0]
-            vals[h, rows, 0:HD] = got[h, 1]
-            for j in range(NEAR):
-                lane = lanes[(2 * h + side) * 32 + j]
-                keys[h, pl.ds(ROWS + side * near + j * BLOCK, BLOCK), HD:] = one_hot(BLOCK, lane)
-
+        for copy in copies(h):
+            copy.start()
+    list_near(labels, live, lanes)
     lane = lax.broadcasted_iota(jnp.int32, (QBLOCKS, HD), 1)
-    per = TILE // BLOCK
-    width = 512
-    per_target = ROWS // GROUPS
     for h in range(2):
         table = mask[slots[h]].astype(f32)
         table = jnp.where((lane < QBLOCKS) & (frame == 0), 0.0, table)
         table = jnp.where((lane >= 2 * QBLOCKS) & (frame == FRAMES - 1), 0.0, table)
-        bias = (table - 1.0) * -BLOCKED
-        for t in range(ROWS // TILE):
-            rows = [jnp.broadcast_to(bias[t * per + i : t * per + i + 1], (BLOCK, HD)) for i in range(per)]
-            query = jnp.concatenate(
-                [q[h, pl.ds(t * TILE, TILE), :], jnp.concatenate(rows, axis=0).astype(bf16)], axis=1
-            )
-            total = jnp.zeros((TILE, 2 * HD), f32)
+        bias[...] = (table - 1.0) * -BLOCKED
+        for a in range(QBLOCKS):
+            wide = jnp.broadcast_to(bias[a : a + 1, :], (BLOCK, HD)).astype(bf16)
+            query[h, pl.ds(a * BLOCK, BLOCK), HD:] = wide
+        vals[h, :, HD:] = jnp.ones((ROWS + 2 * near, HD), bf16)
+        for b in range(QBLOCKS):
+            keys[h, pl.ds(b * BLOCK, BLOCK), HD:] = one_hot(BLOCK, QBLOCKS + b)
+        for side in range(2):
+            for j in range(NEAR):
+                mark = one_hot(BLOCK, lanes[(2 * h + side) * 32 + j])
+                keys[h, pl.ds(ROWS + side * near + j * BLOCK, BLOCK), HD:] = mark
+
+    per_target = ROWS // GROUPS
+    width = 512
+    for h in range(2):
+        for copy in copies(h):
+            copy.wait()
+        for step in range(0, GROUPS, 2):
+            tiles = []
+            for s in (step, step + 1):
+                start = pl.multiple_of(target_of(head, s) * per_target, per_target)
+                tiles.append(query[h, pl.ds(start, per_target), :])
+            tile = jnp.concatenate(tiles, axis=0)
+            total = jnp.zeros((2 * per_target, 2 * HD), f32)
             for c in range((ROWS + 2 * near) // width):
                 part = pl.ds(c * width, width)
                 scores = lax.dot_general(
-                    query, keys[h, part, :], (((1,), (1,)), ((), ())), preferred_element_type=f32
+                    tile, keys[h, part, :], (((1,), (1,)), ((), ())), preferred_element_type=f32
                 )
                 weight = jnp.exp2(scores).astype(bf16)
                 total = total + jnp.dot(weight, vals[h, part, :], preferred_element_type=f32)
             mixed = (total[:, 0:HD] / total[:, HD:]).astype(bf16)
-            targets = pl.ds(t * TILE // per_target, TILE // per_target)
-            column = pl.ds(pl.multiple_of(slots[h] * HD, HD), HD)
-            out[targets, :, column] = mixed.reshape(-1, per_target, HD)
+            for i in range(2):
+                done = mixed[i * per_target : (i + 1) * per_target]
+                outs[step + i][0:per_target, h * HD : (h + 1) * HD] = done
+    label = jnp.full((LABEL_ROWS, 2 * HD), time.astype(f32)).astype(bf16)
+    for out in outs:
+        out[per_target:, :] = label
 
 
 def time_attend(labels, time_mask, got, out, done):
@@ -201,23 +262,27 @@
         out[:, pl.ds(u * 16, 16), :] = mixed.reshape(FRAMES, 16, HD)
 
 
-def merge(labels, space, timed, out, sem):
-    time, _, _ = slots_of(labels)
-    column = pl.ds(pl.multiple_of(time * HD, HD), HD)
-    copy = pltpu.make_async_copy(timed, out.at[:, :, column], sem)
-    copy.start()
-    copy.wait()
-
-
-def assemble(parts, out, sems):
-    width = parts.shape[2]
-    copies = [
-        pltpu.make_async_copy(parts.at[g], out.at[:, pl.ds(g * width, width)], sems.at[g]) for g in range(GROUPS)
-    ]
-    for copy in copies:
-        copy.start()
-    for copy in copies:
-        copy.wait()
+def assemble(timed, *rest):
+    parts, out = rest[:GROUPS], rest[GROUPS]
+    here = lax.axis_index("head")
+    per_target = ROWS // GROUPS
+    quarter = per_target // OUT
+    for step in range(GROUPS):
+        group = source_of(here, step)
+        part = parts[step]
+        label = jnp.concatenate([part[per_target:, 0:HD]] * (quarter // LABEL_ROWS), axis=0)
+        for i in range(OUT):
+            rows = pl.ds(i * quarter, quarter)
+            t = timed[owner_of(group, here, i)]
+            s0 = part[rows, 0:HD]
+            s1 = part[rows, HD:]
+            heads = (
+                jnp.where(label == 0, t, s0),
+                jnp.where(label == 0, s0, jnp.where(label == 1, t, s1)),
+                jnp.where(label == 2, t, s1),
+            )
+            for j, values in enumerate(heads):
+                out[rows, pl.ds(pl.multiple_of((3 * group + j) * HD, HD), HD)] = values
 
 
 def params(mib):
@@ -254,21 +319,21 @@
 
     live = jnp.pad(jnp.max(space_mask, axis=1), ((0, 0), (0, HD - 3 * QBLOCKS)))
     pair = jax.ShapeDtypeStruct((2, 2, NEAR * BLOCK, HD), bf16)
-    q, kv, up, down, lanes = pl.pallas_call(
+    q, kv, up, down = pl.pallas_call(
         space_project,
         out_shape=(
             jax.ShapeDtypeStruct((2, ROWS, HD), bf16),
             jax.ShapeDtypeStruct((2, 2, ROWS, HD), bf16),
             pair,
             pair,
-            jax.ShapeDtypeStruct((HD,), jnp.int32),
         ),
         in_specs=[SMEM, SMEM, ANY, ANY, VMEM, VMEM],
-        out_specs=(VMEM, VMEM, VMEM, VMEM, SMEM),
+        out_specs=(VMEM, VMEM, VMEM, VMEM),
         scratch_shapes=[
             pltpu.VMEM((ROWS, D), bf16),
             pltpu.VMEM((D, 6 * HD), bf16),
             pltpu.VMEM((ROWS, 6 * HD), f32),
+            pltpu.SMEM((HD,), jnp.int32),
             pltpu.SemaphoreType.DMA((PARTS, 7)),
         ],
         compiler_params=params(58),
@@ -291,42 +356,39 @@
     mask = jnp.pad(space_mask, ((0, 0), (0, 0), (0, HD - 3 * QBLOCKS)))
     total_keys = ROWS + 2 * NEAR * BLOCK
     per_target = ROWS // GROUPS
-    space_out = pl.pallas_call(
+    space_outs = pl.pallas_call(
         space_attend,
-        out_shape=jax.ShapeDtypeStruct((GROUPS, per_target, 3 * HD), bf16),
-        in_specs=[SMEM, SMEM] + [VMEM] * 5 + [ANY],
-        out_specs=VMEM,
+        out_shape=[jax.ShapeDtypeStruct((per_target + LABEL_ROWS, 2 * HD), bf16)] * GROUPS,
+        in_specs=[SMEM, SMEM, VMEM] + [ANY] * 5,
+        out_specs=[VMEM] * GROUPS,
         scratch_shapes=[
             pltpu.VMEM((2, total_keys, 2 * HD), bf16),
             pltpu.VMEM((2, total_keys, 2 * HD), bf16),
+            pltpu.VMEM((2, ROWS, 2 * HD), bf16),
+            pltpu.VMEM((QBLOCKS, HD), f32),
+            pltpu.SMEM((HD,), jnp.int32),
+            pltpu.SemaphoreType.DMA((2, 7)),
         ],
-        compiler_params=params(16),
+        compiler_params=params(SPACE_MIB),
         cost_estimate=cost(2 * 4 * ROWS * total_keys * 2 * HD, 4e6, 2 * ROWS * total_keys),
         name="space_attend",
-    )(labels, lanes, q, kv, below, above, mask, done)
-    timed = lax.all_to_all(time_out, "frame", split_axis=0, concat_axis=0, tiled=True)
-    merged = pl.pallas_call(
-        merge,
-        out_shape=jax.ShapeDtypeStruct((GROUPS, per_target, 3 * HD), bf16),
-        in_specs=[SMEM, ANY, ANY],
-        out_specs=ANY,
-        scratch_shapes=[pltpu.SemaphoreType.DMA],
-        input_output_aliases={1: 0},
-        compiler_params=params(16),
-        cost_estimate=cost(1, 5e5),
-        name="merge",
-    )(labels, space_out, timed.reshape(GROUPS, per_target, HD))
-    parts = lax.all_to_all(merged, "head", split_axis=0, concat_axis=0, tiled=True)
+    )(labels, live, mask, q, kv, below, above, done)
+    moved = lax.ppermute(time_out, ("frame", "head"), handover())
+    moved, *space_outs = lax.optimization_barrier((moved, *space_outs))
+    timed = lax.all_to_all(moved, "frame", split_axis=0, concat_axis=0, tiled=True)
+    parts = [space_outs[0]]
+    for step in range(1, GROUPS):
+        steps = [(h, int(target_of(h, step))) for h in range(GROUPS)]
+        parts.append(lax.ppermute(space_outs[step], "head", steps))
     return pl.pallas_call(
         assemble,
         out_shape=jax.ShapeDtypeStruct((per_target, 3 * GROUPS * HD), bf16),
-        in_specs=[ANY],
-        out_specs=ANY,
-        scratch_shapes=[pltpu.SemaphoreType.DMA((GROUPS,))],
+        in_specs=[VMEM] * (1 + GROUPS),
+        out_specs=VMEM,
         compiler_params=params(16),
-        cost_estimate=cost(1, 2e6),
+        cost_estimate=cost(1e6, 2e6),
         name="assemble",
-    )(parts)
+    )(timed, *parts)
 
 
 def solution(mesh):

time: 84.3 us -> 93.3 us (1.11)
  starting transfers between devices: 25.2 us -> 51.8 us
  blocking collectives: 18.8 us -> 0 us
  Pallas kernels: 28.7 us -> 29.9 us
    ppermute x0 -> x8, starting transfers between devices: none -> 19.4 us  [the longest x7 14.3 us: on_device(): parts.append(lax.ppermute(space_outs[step], 'head', steps))]
    all_to_all x1 -> x0, blocking collectives: 18.8 us -> none  [on_device(): lax.all_to_all(merged, 'head', split_axis=0, concat_axis=0, tiled=True)]
    all_to_all x1, starting transfers between devices: 7.97 us -> 15.1 us  [on_device(): lax.all_to_all(moved, 'frame', split_axis=0, concat_axis=0, tiled=True)]
    ppermute x0 -> x8, waiting for transfers between devices: none -> 3.62 us  [the longest x7 3.61 us: on_device(): parts.append(lax.ppermute(space_outs[step], 'head', steps))]
    all_to_all x1, waiting for transfers between devices: 2.93 us -> 0.01 us  [on_device(): lax.all_to_all(moved, 'frame', split_axis=0, concat_axis=0, tiled=True)]
    pallas_call x2 -> x1, Pallas kernels: 6.23 us -> 8.06 us  [on_device(): pl.pallas_call(space_attend, out_shape=[jax.ShapeDtypeStruct((per_target...]
    unnamed x12 -> x14, local copies, waits for them, and re-layouts: 2.86 us -> 1.84 us
  transfers between devices with their start and end apart: 4 -> 12, of which waited for: 2 -> 3; matrix products, arithmetic and copies ran while one was open for 1% -> 1% of each run, Pallas kernels for 24% -> 24%
where the time goes in v3:
time: 93.3 us; the launch traced here: 91.6 us
  starting transfers between devices  51.8 us (56%)
  Pallas kernels  29.9 us (32%)
  waiting for transfers between devices  6.72 us (7%)
  local copies, waits for them, and re-layouts  3.03 us (3%)
    all_to_all x1, starting transfers between devices, on_device(): lax.all_to_all(moved, 'frame', split_axis=0, concat_axis=0, tiled=True)  15.1 us
    ppermute x7, starting transfers between devices, on_device(): parts.append(lax.ppermute(space_outs[step], 'head', steps))  14.3 us
    pallas_call x1, Pallas kernels, on_device(): pl.pallas_call(space_project, out_shape=(jax.ShapeDtypeStruct((2, ROWS, H...  12.3 us
    all_to_all x1, starting transfers between devices, on_device(): got = lax.all_to_all(sent, 'frame', split_axis=0, concat_axis=0, tiled=True)  11.7 us
    pallas_call x1, Pallas kernels, on_device(): pl.pallas_call(space_attend, out_shape=[jax.ShapeDtypeStruct((per_target...  8.06 us
    pallas_call x1, Pallas kernels, on_device(): pl.pallas_call(time_project, out_shape=jax.ShapeDtypeStruct((FRAMES, 3 *...  7.02 us
    ppermute x1, starting transfers between devices, on_device(): moved = lax.ppermute(time_out, ('frame', 'head'), handover())  5.11 us
    ppermute x7, waiting for transfers between devices, on_device(): parts.append(lax.ppermute(space_outs[step], 'head', steps))  3.61 us
  transfers between devices with their start and end apart: 12, of which 3 were waited for; matrix products, arithmetic and copies ran while one was open for 1% of the time, Pallas kernels for 24%

profile of v3, /device:TPU:8, one launch (start us, length us, event | category | flops | bytes accessed | tf_op | source)
XLA Modules:
  0.0 91.6 jit_solution(8238275153130251096)
XLA Ops:
  0.0 0.0 copy-start.4
  0.0 7.0 %time_project.1 = bf16[32,96,128]{2,1,0:T(8,128)(2,1)} custom-call(s32[3]{0:T(128)} %labels.7, bf16[1024,3072]{1,0:T(8,128)(2,1)} %tokens.3, bf16[3,3072,384]{2,1,0:T(8,128)(2,1)} %weight.3, f32[1,128]{1,0:T(1,128)} %bitcast.2, f32[1,128]{1,0:T(1,128)} %bitcast.4), custom_call_target="tpu_custom_call" | custom-call | flops 2415919104 | bytes 9000000 | tf_op jit(solution)/shard_map/time_project/pallas_call | solution.py:303
  7.0 11.7 %all-to-all-start = ((bf16[32,96,128]{2,1,0:T(8,128)(2,1)}), bf16[32,96,128]{2,1,0:T(8,128)(2,1)S(1)}, u32[]{:S(2)}, u32[]{:S(2)}) async-start(bf16[32,96,128]{2,1,0:T(8,128)(2,1)} %time_project.1), calls=%async_computation | async-start | bytes 1572864 | tf_op jit(solution)/shard_map/all_to_all | solution.py:318
  18.8 0.0 copy-done.4
  18.8 0.6 pad.8.live
  19.4 0.0 copy-start.1
  19.4 0.0 copy-start.2
  19.4 12.3 %space_project.1 = (bf16[2,1024,128]{2,1,0:T(8,128)(2,1)}, bf16[2,2,1024,128]{3,2,1,0:T(8,128)(2,1)}, bf16[2,2,512,128]{3,2,1,0:T(8,128)(2,1)}, bf16[2,2,512,128]{3,2,1,0:T(8,128)(2,1)}) custom-call(s32[3]{0:T(128)} %labels.7, s32[3,128]{1,0:T(4,128)} %pad.8.live, bf16[1024,3072]{1,0:T(8,128)(2,1)} %tokens.3, bf16[3,3072,384]{2,1,0:T(8,128)(2,1)} %weight.3, ...), custom_call_target="tpu_custom_call" | custom-call | flops 4831838208 | bytes 12000000 | tf_op jit(solution)/shard_map/space_project/pallas_call | solution.py:322
  31.7 2.1 %collective-permute-start.1 = (bf16[2,2,512,128]{3,2,1,0:T(8,128)(2,1)}, bf16[2,2,512,128]{3,2,1,0:T(8,128)(2,1)S(1)}, u32[]{:S(2)}, u32[]{:S(2)}) collective-permute-start(bf16[2,2,512,128]{3,2,1,0:T(8,128)(2,1)} %get-tuple-element.31), channel_id=1, source_target_pairs={{0,8},{8,16},{16,24},{24,32},{32,40},{40,48},{48,56},{56,64},{64,7... | collective-permute-start | bytes 1572872 | tf_op jit(solution)/shard_map/ppermute | solution.py:343
  33.7 3.5 %collective-permute-start.2 = (bf16[2,2,512,128]{3,2,1,0:T(8,128)(2,1)}, bf16[2,2,512,128]{3,2,1,0:T(8,128)(2,1)S(1)}, u32[]{:S(2)}, u32[]{:S(2)}) collective-permute-start(bf16[2,2,512,128]{3,2,1,0:T(8,128)(2,1)} %get-tuple-element.32), channel_id=1, source_target_pairs={{8,0},{16,8},{24,16},{32,24},{40,32},{48,40},{56,48},{64,56},{72,6... | collective-permute-start | bytes 1572872 | tf_op jit(solution)/shard_map/ppermute | solution.py:344
  37.3 0.6 pad.9.mask
  37.9 3.1 %all-to-all-done.got = bf16[32,96,128]{2,1,0:T(8,128)(2,1)S(1)} async-done(((bf16[32,96,128]{2,1,0:T(8,128)(2,1)}), bf16[32,96,128]{2,1,0:T(8,128)(2,1)S(1)}, u32[]{:S(2)}, u32[]{:S(2)}) %all-to-all-start) | async-done | bytes 786464 | tf_op jit(solution)/shard_map/all_to_all | solution.py:318
  41.0 0.0 copy-done.1
  41.0 0.0 copy-done.2
  41.0 1.5 %time_attend.1 = (bf16[32,32,128]{2,1,0:T(8,128)(2,1)S(1)}, f32[8,128]{1,0:T(8,128)S(1)}) custom-call(s32[3]{0:T(128)S(1)} %copy-done.1, s32[3,4,4]{2,1,0:T(4,128)S(1)} %copy-done.2, bf16[32,96,128]{2,1,0:T(8,128)(2,1)S(1)} %all-to-all-done.got), custom_call_target="tpu_custom_call" | custom-call | flops 536870912 | bytes 1000000 | tf_op jit(solution)/shard_map/time_attend/pallas_call | solution.py:346
  42.5 0.0 copy-start.3
  42.5 5.1 %collective-permute-start = (bf16[32,32,128]{2,1,0:T(8,128)(2,1)S(1)}, bf16[32,32,128]{2,1,0:T(8,128)(2,1)}, u32[]{:S(2)}, u32[]{:S(2)}) collective-permute-start(bf16[32,32,128]{2,1,0:T(8,128)(2,1)S(1)} %get-tuple-element.28), channel_id=1, source_target_pairs={{0,0},{1,1},{2,2},{3,3},{4,4},{5,5},{6,6},{7,7},{8,14},{9,15},{10,... | collective-permute-start | bytes 786440 | tf_op jit(solution)/shard_map/ppermute | solution.py:376
  47.6 0.0 collective-permute-done.1.below
  47.6 0.0 copy-start.5
  47.6 0.0 collective-permute-done.2.above
  47.6 0.0 copy-start.6
  47.6 0.0 copy-done.3
  47.6 0.8 copy-done.5
  48.4 0.2 copy-done.6
  48.6 8.1 %space_attend.1 = (bf16[144,256]{1,0:T(8,128)(2,1)}, bf16[144,256]{1,0:T(8,128)(2,1)}, bf16[144,256]{1,0:T(8,128)(2,1)}, bf16[144,256]{1,0:T(8,128)(2,1)}, bf16[...) custom-call(s32[3]{0:T(128)} %labels.7, ...), custom_call_target="tpu_custom_call" | custom-call | flops 4294967296 | bytes 4000000 | tf_op jit(solution)/shard_map/space_attend/pallas_call | solution.py:359
  56.6 0.0 collective-permute-done
  56.7 15.1 %all-to-all-start.1 = ((bf16[32,32,128]{2,1,0:T(8,128)(2,1)}), bf16[32,32,128]{2,1,0:T(8,128)(2,1)S(1)}, u32[]{:S(2)}, u32[]{:S(2)}) async-start(bf16[32,32,128]{2,1,0:T(8,128)(2,1)} %collective-permute-done), calls=%async_computation.1 | async-start | bytes 524288 | tf_op jit(solution)/shard_map/all_to_all | solution.py:378
  71.7 1.6 %collective-permute-start.3 = (bf16[144,256]{1,0:T(8,128)(2,1)}, bf16[144,256]{1,0:T(8,128)(2,1)S(1)}, u32[]{:S(2)}, u32[]{:S(2)}) collective-permute-start(bf16[144,256]{1,0:T(8,128)(2,1)} %get-tuple-element.44), channel_id=1, source_target_pairs={{0,1},{1,2},{2,3},{3,0},{4,5},{5,6},{6,7},{7,4},{8,9},{9,10},{10,1... | collective-permute-start | bytes 221192 | tf_op jit(solution)/shard_map/ppermute | solution.py:382
  73.3 2.7 %collective-permute-start.4 = (bf16[144,256]{1,0:T(8,128)(2,1)}, bf16[144,256]{1,0:T(8,128)(2,1)S(1)}, u32[]{:S(2)}, u32[]{:S(2)}) collective-permute-start(bf16[144,256]{1,0:T(8,128)(2,1)} %get-tuple-element.45), channel_id=1, source_target_pairs={{0,2},{1,3},{2,0},{3,1},{4,6},{5,7},{6,4},{7,5},{8,10},{9,11},{10,... | collective-permute-start | bytes 221192 | tf_op jit(solution)/shard_map/ppermute | solution.py:382
  76.0 1.4 %collective-permute-start.5 = (bf16[144,256]{1,0:T(8,128)(2,1)}, bf16[144,256]{1,0:T(8,128)(2,1)S(1)}, u32[]{:S(2)}, u32[]{:S(2)}) collective-permute-start(bf16[144,256]{1,0:T(8,128)(2,1)} %get-tuple-element.46), channel_id=1, source_target_pairs={{0,3},{1,0},{2,1},{3,2},{4,7},{5,4},{6,5},{7,6},{8,11},{9,8},{10,9... | collective-permute-start | bytes 221192 | tf_op jit(solution)/shard_map/ppermute | solution.py:382
  77.5 4.4 %collective-permute-start.6 = (bf16[144,256]{1,0:T(8,128)(2,1)}, bf16[144,256]{1,0:T(8,128)(2,1)S(1)}, u32[]{:S(2)}, u32[]{:S(2)}) collective-permute-start(bf16[144,256]{1,0:T(8,128)(2,1)} %get-tuple-element.47), channel_id=1, source_target_pairs={{0,4},{1,5},{2,6},{3,7},{4,0},{5,1},{6,2},{7,3},{8,12},{9,13},{10,... | collective-permute-start | bytes 221192 | tf_op jit(solution)/shard_map/ppermute | solution.py:382
  81.8 0.0 collective-permute-start.7
  81.9 0.0 collective-permute-done.3.rest_1_
  81.9 2.3 %collective-permute-start.8 = (bf16[144,256]{1,0:T(8,128)(2,1)}, bf16[144,256]{1,0:T(8,128)(2,1)S(1)}, u32[]{:S(2)}, u32[]{:S(2)}) collective-permute-start(bf16[144,256]{1,0:T(8,128)(2,1)} %get-tuple-element.49), channel_id=1, source_target_pairs={{0,6},{1,7},{2,4},{3,5},{4,2},{5,3},{6,0},{7,1},{8,14},{9,15},{10,... | collective-permute-start | bytes 221192 | tf_op jit(solution)/shard_map/ppermute | solution.py:382
  84.2 0.0 collective-permute-done.4.rest_2_
  84.2 1.9 %collective-permute-start.9 = (bf16[144,256]{1,0:T(8,128)(2,1)}, bf16[144,256]{1,0:T(8,128)(2,1)S(1)}, u32[]{:S(2)}, u32[]{:S(2)}) collective-permute-start(bf16[144,256]{1,0:T(8,128)(2,1)} %get-tuple-element.50), channel_id=1, source_target_pairs={{0,7},{1,4},{2,5},{3,6},{4,3},{5,0},{6,1},{7,2},{8,15},{9,12},{10,... | collective-permute-start | bytes 221192 | tf_op jit(solution)/shard_map/ppermute | solution.py:382
  86.1 0.0 collective-permute-done.5.rest_3_
  86.1 0.0 collective-permute-done.6.rest_4_
  86.1 3.4 %collective-permute-done.7.rest_5_ = bf16[144,256]{1,0:T(8,128)(2,1)S(1)} collective-permute-done((bf16[144,256]{1,0:T(8,128)(2,1)}, bf16[144,256]{1,0:T(8,128)(2,1)S(1)}, u32[]{:S(2)}, u32[]{:S(2)}) %collective-permute-start.7) | collective-permute-done | bytes 73760 | tf_op jit(solution)/shard_map/ppermute | solution.py:382
  89.5 0.0 collective-permute-done.8.rest_6_
  89.5 0.2 collective-permute-done.9.rest_7_
  89.7 0.0 all-to-all-done.1.timed
  89.7 0.0 copy-start
  89.7 0.9 copy-done
  90.6 1.0 %assemble.1 = bf16[128,3072]{1,0:T(8,128)(2,1)} custom-call(bf16[32,32,128]{2,1,0:T(8,128)(2,1)S(1)} %all-to-all-done.1.timed, bf16[144,256]{1,0:T(8,128)(2,1)S(1)} %copy-done, bf16[144,256]{1,0:T(8,128)(2,1)S(1)} %collective-permute-done.3.rest_1_, bf16[144,256]{1,0:T(8,128)(2,1)S(1)} %collective-permute-done.4.rest_2_, ...), custom_call_target="tpu_custom_call" | custom-call | flops 1000000 | bytes 2000000 | tf_op jit(solution)/shard_map/assemble/pallas_call | solution.py:383
  (1 shorter events, 0.0 us)
Async XLA Ops:
  0.0 18.8 %copy-start.4 = (s32[3,16,48]{2,1,0:T(8,128)S(1)}, s32[3,16,48]{2,1,0:T(8,128)}, u32[]{:S(2)}) copy-start(s32[3,16,48]{2,1,0:T(8,128)} %param.12) | copy-start | bytes 27652
  7.0 33.9 %all-to-all-start = ((bf16[32,96,128]{2,1,0:T(8,128)(2,1)}), bf16[32,96,128]{2,1,0:T(8,128)(2,1)S(1)}, u32[]{:S(2)}, u32[]{:S(2)}) async-start(bf16[32,96,128]{2,1,0:T(8,128)(2,1)} %time_project.1), calls=%async_computation | async-start | bytes 1572864 | tf_op jit(solution)/shard_map/all_to_all | solution.py:318
  19.4 21.6 %copy-start.1 = (s32[3]{0:T(128)S(1)}, s32[3]{0:T(128)}, u32[]{:S(2)}) copy-start(s32[3]{0:T(128)} %labels.7) | copy-start | bytes 40
  19.4 21.6 %copy-start.2 = (s32[3,4,4]{2,1,0:T(4,128)S(1)}, s32[3,4,4]{2,1,0:T(4,128)}, u32[]{:S(2)}) copy-start(s32[3,4,4]{2,1,0:T(4,128)} %time_mask.1) | copy-start | bytes 580
  31.7 15.9 %collective-permute-start.1 = (bf16[2,2,512,128]{3,2,1,0:T(8,128)(2,1)}, bf16[2,2,512,128]{3,2,1,0:T(8,128)(2,1)S(1)}, u32[]{:S(2)}, u32[]{:S(2)}) collective-permute-start(bf16[2,2,512,128]{3,2,1,0:T(8,128)(2,1)} %get-tuple-element.31), channel_id=1, source_target_pairs={{0,8},{8,16},{16,24},{24,32},{32,40},{40,48},{48,56},{56,64},{64,7... | collective-permute-start | bytes 1572872 | tf_op jit(solution)/shard_map/ppermute | solution.py:343
  33.7 13.9 %collective-permute-start.2 = (bf16[2,2,512,128]{3,2,1,0:T(8,128)(2,1)}, bf16[2,2,512,128]{3,2,1,0:T(8,128)(2,1)S(1)}, u32[]{:S(2)}, u32[]{:S(2)}) collective-permute-start(bf16[2,2,512,128]{3,2,1,0:T(8,128)(2,1)} %get-tuple-element.32), channel_id=1, source_target_pairs={{8,0},{16,8},{24,16},{32,24},{40,32},{48,40},{56,48},{64,56},{72,6... | collective-permute-start | bytes 1572872 | tf_op jit(solution)/shard_map/ppermute | solution.py:344
  42.5 5.2 %copy-start.3 = (f32[8,128]{1,0:T(8,128)}, f32[8,128]{1,0:T(8,128)S(1)}, u32[]{:S(2)}) copy-start(f32[8,128]{1,0:T(8,128)S(1)} %get-tuple-element.33.after) | copy-start | bytes 12292
  42.5 14.2 %collective-permute-start = (bf16[32,32,128]{2,1,0:T(8,128)(2,1)S(1)}, bf16[32,32,128]{2,1,0:T(8,128)(2,1)}, u32[]{:S(2)}, u32[]{:S(2)}) collective-permute-start(bf16[32,32,128]{2,1,0:T(8,128)(2,1)S(1)} %get-tuple-element.28), channel_id=1, source_target_pairs={{0,0},{1,1},{2,2},{3,3},{4,4},{5,5},{6,6},{7,7},{8,14},{9,15},{10,... | collective-permute-start | bytes 786440 | tf_op jit(solution)/shard_map/ppermute | solution.py:376
  47.6 0.8 copy-start.5
  47.6 0.9 %copy-start.6 = (bf16[2,2,512,128]{3,2,1,0:T(8,128)(2,1)}, bf16[2,2,512,128]{3,2,1,0:T(8,128)(2,1)S(1)}, u32[]{:S(2)}) copy-start(bf16[2,2,512,128]{3,2,1,0:T(8,128)(2,1)S(1)} %collective-permute-done.2.above) | copy-start | bytes 1572868
  56.7 33.0 %all-to-all-start.1 = ((bf16[32,32,128]{2,1,0:T(8,128)(2,1)}), bf16[32,32,128]{2,1,0:T(8,128)(2,1)S(1)}, u32[]{:S(2)}, u32[]{:S(2)}) async-start(bf16[32,32,128]{2,1,0:T(8,128)(2,1)} %collective-permute-done), calls=%async_computation.1 | async-start | bytes 524288 | tf_op jit(solution)/shard_map/all_to_all | solution.py:378
  71.7 10.2 %collective-permute-start.3 = (bf16[144,256]{1,0:T(8,128)(2,1)}, bf16[144,256]{1,0:T(8,128)(2,1)S(1)}, u32[]{:S(2)}, u32[]{:S(2)}) collective-permute-start(bf16[144,256]{1,0:T(8,128)(2,1)} %get-tuple-element.44), channel_id=1, source_target_pairs={{0,1},{1,2},{2,3},{3,0},{4,5},{5,6},{6,7},{7,4},{8,9},{9,10},{10,1... | collective-permute-start | bytes 221192 | tf_op jit(solution)/shard_map/ppermute | solution.py:382
  73.3 10.9 %collective-permute-start.4 = (bf16[144,256]{1,0:T(8,128)(2,1)}, bf16[144,256]{1,0:T(8,128)(2,1)S(1)}, u32[]{:S(2)}, u32[]{:S(2)}) collective-permute-start(bf16[144,256]{1,0:T(8,128)(2,1)} %get-tuple-element.45), channel_id=1, source_target_pairs={{0,2},{1,3},{2,0},{3,1},{4,6},{5,7},{6,4},{7,5},{8,10},{9,11},{10,... | collective-permute-start | bytes 221192 | tf_op jit(solution)/shard_map/ppermute | solution.py:382
  76.0 10.0 %collective-permute-start.5 = (bf16[144,256]{1,0:T(8,128)(2,1)}, bf16[144,256]{1,0:T(8,128)(2,1)S(1)}, u32[]{:S(2)}, u32[]{:S(2)}) collective-permute-start(bf16[144,256]{1,0:T(8,128)(2,1)} %get-tuple-element.46), channel_id=1, source_target_pairs={{0,3},{1,0},{2,1},{3,2},{4,7},{5,4},{6,5},{7,6},{8,11},{9,8},{10,9... | collective-permute-start | bytes 221192 | tf_op jit(solution)/shard_map/ppermute | solution.py:382
  77.5 8.6 %collective-permute-start.6 = (bf16[144,256]{1,0:T(8,128)(2,1)}, bf16[144,256]{1,0:T(8,128)(2,1)S(1)}, u32[]{:S(2)}, u32[]{:S(2)}) collective-permute-start(bf16[144,256]{1,0:T(8,128)(2,1)} %get-tuple-element.47), channel_id=1, source_target_pairs={{0,4},{1,5},{2,6},{3,7},{4,0},{5,1},{6,2},{7,3},{8,12},{9,13},{10,... | collective-permute-start | bytes 221192 | tf_op jit(solution)/shard_map/ppermute | solution.py:382
  81.8 7.6 %collective-permute-start.7 = (bf16[144,256]{1,0:T(8,128)(2,1)}, bf16[144,256]{1,0:T(8,128)(2,1)S(1)}, u32[]{:S(2)}, u32[]{:S(2)}) collective-permute-start(bf16[144,256]{1,0:T(8,128)(2,1)} %get-tuple-element.48), channel_id=1, source_target_pairs={{0,5},{1,6},{2,7},{3,4},{4,1},{5,2},{6,3},{7,0},{8,13},{9,14},{10,... | collective-permute-start | bytes 221192 | tf_op jit(solution)/shard_map/ppermute | solution.py:382
  81.9 7.6 %collective-permute-start.8 = (bf16[144,256]{1,0:T(8,128)(2,1)}, bf16[144,256]{1,0:T(8,128)(2,1)S(1)}, u32[]{:S(2)}, u32[]{:S(2)}) collective-permute-start(bf16[144,256]{1,0:T(8,128)(2,1)} %get-tuple-element.49), channel_id=1, source_target_pairs={{0,6},{1,7},{2,4},{3,5},{4,2},{5,3},{6,0},{7,1},{8,14},{9,15},{10,... | collective-permute-start | bytes 221192 | tf_op jit(solution)/shard_map/ppermute | solution.py:382
  84.2 5.5 %collective-permute-start.9 = (bf16[144,256]{1,0:T(8,128)(2,1)}, bf16[144,256]{1,0:T(8,128)(2,1)S(1)}, u32[]{:S(2)}, u32[]{:S(2)}) collective-permute-start(bf16[144,256]{1,0:T(8,128)(2,1)} %get-tuple-element.50), channel_id=1, source_target_pairs={{0,7},{1,4},{2,5},{3,6},{4,3},{5,0},{6,1},{7,2},{8,15},{9,12},{10,... | collective-permute-start | bytes 221192 | tf_op jit(solution)/shard_map/ppermute | solution.py:382
  89.7 0.9 copy-start

commit v4 on v2

v4 whole, which is shorter than its diff:
```python
import math

import jax
import jax.numpy as jnp
from jax import lax
from jax.experimental import pallas as pl
from jax.experimental.pallas import tpu as pltpu
from jax.sharding import PartitionSpec as P

STRIP = 8
BLOCK = 64
D = 3072
HD = 128
ROWS = 1024
FRAMES = 32
GROUPS = 8
QBLOCKS = 16
NEAR = 8
CHUNKS = (512, 768, 768, 768, 256)
STARTS = tuple(sum(CHUNKS[:c]) for c in range(len(CHUNKS)))
PARTS = len(CHUNKS)
TILE = 256
EPSILON = 1e-06
SCALE = math.log2(math.e) / math.sqrt(HD)
BLOCKED = -16384.0
DEAD = 64

bf16 = jnp.bfloat16
f32 = jnp.float32


def slots_of(labels):
    time = labels[1] + 2 * labels[2]
    return time, jnp.where(time == 0, 1, 0), jnp.where(time == 2, 1, 2)


def normed(x, gain):
    inverse = lax.rsqrt(jnp.mean(x * x, axis=-1, keepdims=True) + EPSILON)
    return (x * inverse * gain).astype(bf16)


def project(tokens, weight, columns, tok, wts, acc, sems, meanwhile=None):
    def copies(c):
        part = pl.ds(STARTS[c], CHUNKS[c])
        made = [pltpu.make_async_copy(tokens.at[:, part], tok.at[:, part], sems.at[c, 0])]
        for i, (k, slot) in enumerate(columns):
            column = pl.ds(pl.multiple_of(slot * HD, HD), HD)
            made.append(
                pltpu.make_async_copy(weight.at[k, part, column], wts.at[part, pl.ds(i * HD, HD)], sems.at[c, 1 + i])
            )
        return made

    for c in range(2):
        for copy in copies(c):
            copy.start()
    if meanwhile is not None:
        meanwhile()
    for c in range(PARTS):
        for copy in copies(c):
            copy.wait()
        if c + 2 < PARTS:
            for copy in copies(c + 2):
                copy.start()
        part = pl.ds(STARTS[c], CHUNKS[c])
        product = jnp.dot(tok[:, part], wts[part, :], preferred_element_type=f32)
        if c == 0:
            acc[...] = product
        else:
            acc[...] += product


def time_project(labels, tokens, weight, query_gain, key_gain, out, made, tok, wts, acc, sems, out_sems):
    time, _, _ = slots_of(labels)
    project(tokens, weight, [(0, time), (1, time), (2, time)], tok, wts, acc, sems)
    copies = []
    for b in range(FRAMES):
        rows = pl.ds(b * FRAMES, FRAMES)
        made[b, 0:FRAMES, :] = normed(acc[rows, 0:HD], query_gain[...] * SCALE)
        made[b, FRAMES : 2 * FRAMES, :] = normed(acc[rows, HD : 2 * HD], key_gain[...])
        made[b, 2 * FRAMES :, :] = acc[rows, 2 * HD :].astype(bf16)
        if b % 8 == 7:
            group = pl.ds(b - 7, 8)
            copies.append(pltpu.make_async_copy(made.at[group], out.at[group], out_sems.at[b // 8]))
            copies[-1].start()
    for copy in copies:
        copy.wait()


def list_near(labels, live, lanes):
    _, *slots = slots_of(labels)
    for h in range(2):
        for side in range(2):
            base = (2 * h + side) * 32
            for j in range(32):
                lanes[base + j] = DEAD
            count = 0
            for b in range(QBLOCKS):
                column = 2 * QBLOCKS * side + b
                alive = live[slots[h], column] > 0
                lanes[base + count] = jnp.where(alive, column, DEAD)
                count = count + alive.astype(jnp.int32)


def space_project(labels, live, tokens, weight, query_gain, key_gain, *rest):
    q_out, kv_out, up_out, down_out, lanes, q, kv, up, down, tok, wts, acc, sems, out_sems = rest
    _, first, second = slots_of(labels)
    columns = [(k, slot) for k in range(3) for slot in (first, second)]
    project(tokens, weight, columns, tok, wts, acc, sems, lambda: list_near(labels, live, lanes))
    copies = []

    def send(source, target):
        copies.append(pltpu.make_async_copy(source, target, out_sems.at[len(copies)]))
        copies[-1].start()

    for r in range(ROWS // TILE):
        rows = pl.ds(r * TILE, TILE)
        for h in range(2):
            kv[h, 0, rows, :] = normed(acc[rows, (2 + h) * HD : (3 + h) * HD], key_gain[...])
            kv[h, 1, rows, :] = acc[rows, (4 + h) * HD : (5 + h) * HD].astype(bf16)
        send(kv.at[:, :, rows], kv_out.at[:, :, rows])
    for side, (packed, target) in enumerate(((up, up_out), (down, down_out))):
        for h in range(2):
            for j in range(NEAR):
                block = lanes[(2 * h + side) * 32 + j] & (QBLOCKS - 1)
                rows = pl.ds(pl.multiple_of(block * BLOCK, BLOCK), BLOCK)
                for part in range(2):
                    packed[h, part, pl.ds(j * BLOCK, BLOCK), :] = kv[h, part, rows, :]
        send(packed, target)
    for r in range(ROWS // TILE):
        rows = pl.ds(r * TILE, TILE)
        for h in range(2):
            q[h, rows, :] = normed(acc[rows, h * HD : (h + 1) * HD], query_gain[...] * SCALE)
        send(q.at[:, rows], q_out.at[:, rows])
    for copy in copies:
        copy.wait()


def one_hot(rows, lane):
    return (lax.broadcasted_iota(jnp.int32, (rows, HD), 1) == lane).astype(f32).astype(bf16)


def block_bias(mask, slot):
    frame = lax.axis_index("frame")
    lane = lax.broadcasted_iota(jnp.int32, (QBLOCKS, HD), 1)
    table = mask[slot].astype(f32)
    table = jnp.where((lane < QBLOCKS) & (frame == 0), 0.0, table)
    table = jnp.where((lane >= 2 * QBLOCKS) & (frame == FRAMES - 1), 0.0, table)
    return (table - 1.0) * -BLOCKED


def attend_tile(q, bias, keys, vals, h, t, total):
    per = TILE // BLOCK
    rows = [jnp.broadcast_to(bias[t * per + i : t * per + i + 1], (BLOCK, HD)) for i in range(per)]
    query = jnp.concatenate([q[h, pl.ds(t * TILE, TILE), :], jnp.concatenate(rows, axis=0).astype(bf16)], axis=1)
    width = 512
    for c in range(keys.shape[1] // width):
        part = pl.ds(c * width, width)
        scores = lax.dot_general(query, keys[h, part, :], (((1,), (1,)), ((), ())), preferred_element_type=f32)
        weight = jnp.exp2(scores).astype(bf16)
        product = jnp.dot(weight, vals[h, part, :], preferred_element_type=f32)
        total = product if total is None else total + product
    return total


def attend_own(labels, mask, q, kv, after, totals, keys, vals):
    _, *slots = slots_of(labels)
    for b in range(QBLOCKS):
        own = one_hot(BLOCK, QBLOCKS + b)
        for h in range(2):
            keys[h, pl.ds(b * BLOCK, BLOCK), HD:] = own
    for h in range(2):
        keys[h, :, 0:HD] = kv[h, 0]
        vals[h, :, 0:HD] = kv[h, 1]
        vals[h, :, HD:] = jnp.ones((ROWS, HD), bf16)
    for h in range(2):
        bias = block_bias(mask, slots[h])
        for t in range(ROWS // TILE):
            totals[h, pl.ds(t * TILE, TILE), :] = attend_tile(q, bias, keys, vals, h, t, None)


def attend_near(labels, lanes, mask, q, totals, below, above, out, keys, vals):
    _, *slots = slots_of(labels)
    near = NEAR * BLOCK
    per_target = ROWS // GROUPS
    for h in range(2):
        vals[h, :, HD:] = jnp.ones((2 * near, HD), bf16)
        for side, got in enumerate((below, above)):
            rows = pl.ds(side * near, near)
            keys[h, rows, 0:HD] = got[h, 0]
            vals[h, rows, 0:HD] = got[h, 1]
            for j in range(NEAR):
                lane = lanes[(2 * h + side) * 32 + j]
                keys[h, pl.ds(side * near + j * BLOCK, BLOCK), HD:] = one_hot(BLOCK, lane)
    for h in range(2):
        bias = block_bias(mask, slots[h])
        for t in range(ROWS // TILE):
            total = attend_tile(q, bias, keys, vals, h, t, totals[h, pl.ds(t * TILE, TILE), :])
            mixed = (total[:, 0:HD] / total[:, HD:]).astype(bf16)
            targets = pl.ds(t * TILE // per_target, TILE // per_target)
            column = pl.ds(pl.multiple_of(slots[h] * HD, HD), HD)
            out[targets, :, column] = mixed.reshape(-1, per_target, HD)


def time_attend(labels, time_mask, got, out, done, made, sems):
    done[...] = jnp.zeros_like(done)
    time, _, _ = slots_of(labels)
    lane = lax.broadcasted_iota(jnp.int32, (16, HD), 1)
    row = lax.broadcasted_iota(jnp.int32, (16, HD), 0)
    same = (lane & 1) == (row >> 3)
    tables = []
    for a in range(4):
        allowed = jnp.zeros((16, HD), jnp.int32)
        for b in range(4):
            allowed = jnp.where((lane >> 1) == b, time_mask[time, a, b], allowed)
        table = jnp.where(same & (allowed == 1), 0.0, BLOCKED).astype(bf16)
        tables.append(jnp.broadcast_to(table[None], (8, 16, HD)))
    bias = jnp.concatenate(tables, axis=0).reshape(512, HD)
    key_frame = lax.broadcasted_iota(jnp.int32, (512, HD), 0)
    key_lane = lax.broadcasted_iota(jnp.int32, (512, HD), 1)
    mark = (((key_frame >> 7) * 2 + ((key_frame >> 3) & 1)) == key_lane).astype(f32).astype(bf16)
    ones = jnp.ones((512, HD), bf16)
    copies = []
    for u in range(2):
        def rows(part):
            return got[:, pl.ds(part * FRAMES + u * 16, 16), :].reshape(512, HD)

        query = jnp.concatenate([rows(0), bias], axis=1)
        keys = jnp.concatenate([rows(1), mark], axis=1)
        vals = jnp.concatenate([rows(2), ones], axis=1)
        scores = lax.dot_general(query, keys, (((1,), (1,)), ((), ())), preferred_element_type=f32)
        weight = jnp.exp2(scores).astype(bf16)
        total = jnp.dot(weight, vals, preferred_element_type=f32)
        mixed = (total[:, 0:HD] / total[:, HD:]).astype(bf16)
        made[u] = mixed.reshape(FRAMES, 16, HD)
        copies.append(pltpu.make_async_copy(made.at[u], out.at[:, pl.ds(u * 16, 16), :], sems.at[u]))
        copies[-1].start()
    for copy in copies:
        copy.wait()


def merge(labels, space, timed, out, sem):
    time, _, _ = slots_of(labels)
    column = pl.ds(pl.multiple_of(time * HD, HD), HD)
    copy = pltpu.make_async_copy(timed, out.at[:, :, column], sem)
    copy.start()
    copy.wait()


def assemble(parts, out, sems):
    width = parts.shape[2]
    copies = [
        pltpu.make_async_copy(parts.at[g], out.at[:, pl.ds(g * width, width)], sems.at[g]) for g in range(GROUPS)
    ]
    for copy in copies:
        copy.start()
    for copy in copies:
        copy.wait()


def params(mib):
    return pltpu.CompilerParams(vmem_limit_bytes=mib * 2**20)


def cost(flops, moved, exps=0):
    return pl.CostEstimate(flops=int(flops), bytes_accessed=int(moved), transcendentals=int(exps))


SMEM = pl.BlockSpec(memory_space=pltpu.SMEM)
VMEM = pl.BlockSpec(memory_space=pltpu.VMEM)
ANY = pl.BlockSpec(memory_space=pl.ANY)


def on_device(tokens, qkv_weight, query_gain, key_gain, labels, space_mask, time_mask):
    gains = (query_gain.reshape(1, HD), key_gain.reshape(1, HD))
    sent = pl.pallas_call(
        time_project,
        out_shape=jax.ShapeDtypeStruct((FRAMES, 3 * FRAMES, HD), bf16),
        in_specs=[SMEM, ANY, ANY, VMEM, VMEM],
        out_specs=ANY,
        scratch_shapes=[
            pltpu.VMEM((FRAMES, 3 * FRAMES, HD), bf16),
            pltpu.VMEM((ROWS, D), bf16),
            pltpu.VMEM((D, 3 * HD), bf16),
            pltpu.VMEM((ROWS, 3 * HD), f32),
            pltpu.SemaphoreType.DMA((PARTS, 4)),
            pltpu.SemaphoreType.DMA((4,)),
        ],
        compiler_params=params(60),
        cost_estimate=cost(2 * ROWS * D * 3 * HD, 9e6),
        name="time_project",
    )(labels, tokens, qkv_weight, *gains)
    got = lax.all_to_all(sent, "frame", split_axis=0, concat_axis=0, tiled=True)

    live = jnp.pad(jnp.max(space_mask, axis=1), ((0, 0), (0, HD - 3 * QBLOCKS)))
    pair = jax.ShapeDtypeStruct((2, 2, NEAR * BLOCK, HD), bf16)
    q, kv, up, down, lanes = pl.pallas_call(
        space_project,
        out_shape=(
            jax.ShapeDtypeStruct((2, ROWS, HD), bf16),
            jax.ShapeDtypeStruct((2, 2, ROWS, HD), bf16),
            pair,
            pair,
            jax.ShapeDtypeStruct((HD,), jnp.int32),
        ),
        in_specs=[SMEM, SMEM, ANY, ANY, VMEM, VMEM],
        out_specs=(ANY, ANY, ANY, ANY, SMEM),
        scratch_shapes=[
            pltpu.VMEM((2, ROWS, HD), bf16),
            pltpu.VMEM((2, 2, ROWS, HD), bf16),
            pltpu.VMEM((2, 2, NEAR * BLOCK, HD), bf16),
            pltpu.VMEM((2, 2, NEAR * BLOCK, HD), bf16),
            pltpu.VMEM((ROWS, D), bf16),
            pltpu.VMEM((D, 6 * HD), bf16),
            pltpu.VMEM((ROWS, 6 * HD), f32),
            pltpu.SemaphoreType.DMA((PARTS, 7)),
            pltpu.SemaphoreType.DMA((10,)),
        ],
        compiler_params=params(58),
        cost_estimate=cost(2 * ROWS * D * 6 * HD, 12e6),
        name="space_project",
    )(labels, live, tokens, qkv_weight, *gains)
    below = lax.ppermute(up, "frame", [(i, i + 1) for i in range(FRAMES - 1)])
    above = lax.ppermute(down, "frame", [(i + 1, i) for i in range(FRAMES - 1)])

    time_out, done = pl.pallas_call(
        time_attend,
        out_shape=(jax.ShapeDtypeStruct((FRAMES, FRAMES, HD), bf16), jax.ShapeDtypeStruct((8, HD), f32)),
        in_specs=[SMEM, SMEM, VMEM],
        out_specs=(ANY, VMEM),
        scratch_shapes=[pltpu.VMEM((2, FRAMES, 16, HD), bf16), pltpu.SemaphoreType.DMA((2,))],
        compiler_params=params(16),
        cost_estimate=cost(8 * 512 * 512 * 2 * HD, 1e6, 2 * 512 * 512),
        name="time_attend",
    )(labels, time_mask, got)

    mask = jnp.pad(space_mask, ((0, 0), (0, 0), (0, HD - 3 * QBLOCKS)))
    per_target = ROWS // GROUPS
    sides = (2, ROWS, 2 * HD)
    scratch = [pltpu.VMEM(sides, bf16), pltpu.VMEM(sides, bf16)]
    half = cost(2 * 4 * ROWS * ROWS * 2 * HD, 4e6, 2 * ROWS * ROWS)
    totals = pl.pallas_call(
        attend_own,
        out_shape=jax.ShapeDtypeStruct(sides, f32),
        in_specs=[SMEM, VMEM, VMEM, VMEM, ANY],
        out_specs=VMEM,
        scratch_shapes=scratch,
        compiler_params=params(16),
        cost_estimate=half,
        name="attend_own",
    )(labels, mask, q, kv, done)
    space_out = pl.pallas_call(
        attend_near,
        out_shape=jax.ShapeDtypeStruct((GROUPS, per_target, 3 * HD), bf16),
        in_specs=[SMEM, SMEM] + [VMEM] * 5,
        out_specs=VMEM,
        scratch_shapes=scratch,
        compiler_params=params(16),
        cost_estimate=half,
        name="attend_near",
    )(labels, lanes, mask, q, totals, below, above)
    timed = lax.all_to_all(time_out, "frame", split_axis=0, concat_axis=0, tiled=True)
    merged = pl.pallas_call(
        merge,
        out_shape=jax.ShapeDtypeStruct((GROUPS, per_target, 3 * HD), bf16),
        in_specs=[SMEM, ANY, ANY],
        out_specs=ANY,
        scratch_shapes=[pltpu.SemaphoreType.DMA],
        input_output_aliases={1: 0},
        compiler_params=params(16),
        cost_estimate=cost(1, 5e5),
        name="merge",
    )(labels, space_out, timed.reshape(GROUPS, per_target, HD))
    parts = lax.all_to_all(merged, "head", split_axis=0, concat_axis=0, tiled=True)
    return pl.pallas_call(
        assemble,
        out_shape=jax.ShapeDtypeStruct((per_target, 3 * GROUPS * HD), bf16),
        in_specs=[ANY],
        out_specs=ANY,
        scratch_shapes=[pltpu.SemaphoreType.DMA((GROUPS,))],
        compiler_params=params(16),
        cost_estimate=cost(1, 2e6),
        name="assemble",
    )(parts)


def solution(mesh):
    placed = (
        P("frame", None),
        P(None, None, "head"),
        P(),
        P(),
        P("head"),
        P("head", None, None),
        P("head", None, None),
    )
    return jax.shard_map(
        on_device, mesh=mesh, in_specs=placed, out_specs=P(("frame", "head"), None), check_vma=False
    )
```

time: 84.3 us -> 84.2 us (level)
    pallas_call x1 -> x2, Pallas kernels: 5.63 us -> 6.4 us  [the longest x1 3.27 us: on_device(): pl.pallas_call(attend_own, out_shape=jax.ShapeDtypeStruct(sides, f32), in...]
  transfers between devices with their start and end apart: 4 -> 4, of which waited for: 2 -> 2; matrix products, arithmetic and copies ran while one was open for 1% -> 1% of each run, Pallas kernels for 24% -> 25%
where the time goes in v4:
time: 84.2 us; the launch traced here: 83 us
  Pallas kernels  29.4 us (35%)
  starting transfers between devices  25.3 us (30%)
  blocking collectives  18.8 us (22%)
  waiting for transfers between devices  6.4 us (8%)
  local copies, waits for them, and re-layouts  2.88 us (3%)
    all_to_all x1, blocking collectives, on_device(): lax.all_to_all(merged, 'head', split_axis=0, concat_axis=0, tiled=True)  18.8 us
    pallas_call x1, Pallas kernels, on_device(): pl.pallas_call(space_project, out_shape=(jax.ShapeDtypeStruct((2, ROWS, H...  12.3 us
    all_to_all x1, starting transfers between devices, on_device(): got = lax.all_to_all(sent, 'frame', split_axis=0, concat_axis=0, tiled=True)  11.7 us
    all_to_all x1, starting transfers between devices, on_device(): lax.all_to_all(time_out, 'frame', split_axis=0, concat_axis=0, tiled=True)  7.98 us
    pallas_call x1, Pallas kernels, on_device(): pl.pallas_call(time_project, out_shape=jax.ShapeDtypeStruct((FRAMES, 3 *...  6.94 us
    all_to_all x1, waiting for transfers between devices, on_device(): got = lax.all_to_all(sent, 'frame', split_axis=0, concat_axis=0, tiled=True)  3.66 us
    ppermute x1, starting transfers between devices, on_device(): above = lax.ppermute(down, 'frame', [(i + 1, i) for i in range(FRAMES - 1)])  3.5 us
    pallas_call x1, Pallas kernels, on_device(): pl.pallas_call(attend_own, out_shape=jax.ShapeDtypeStruct(sides, f32), in...  3.27 us
  transfers between devices with their start and end apart: 4, of which 2 were waited for; matrix products, arithmetic and copies ran while one was open for 1% of the time, Pallas kernels for 25%

profile of v4, /device:TPU:8, one launch (start us, length us, event | category | flops | bytes accessed | tf_op | source)
XLA Modules:
  0.0 83.0 jit_solution(10462986413708905339)
XLA Ops:
  0.0 0.0 copy-start.5
  0.0 6.9 %time_project.1 = bf16[32,96,128]{2,1,0:T(8,128)(2,1)} custom-call(s32[3]{0:T(128)} %labels.11, bf16[1024,3072]{1,0:T(8,128)(2,1)} %tokens.3, bf16[3,3072,384]{2,1,0:T(8,128)(2,1)} %weight.3, f32[1,128]{1,0:T(1,128)} %bitcast.4, f32[1,128]{1,0:T(1,128)} %bitcast.6), custom_call_target="tpu_custom_call" | custom-call | flops 2415919104 | bytes 9000000 | tf_op jit(solution)/shard_map/time_project/pallas_call | solution.py:275
  6.9 11.7 %all-to-all-start = ((bf16[32,96,128]{2,1,0:T(8,128)(2,1)}), bf16[32,96,128]{2,1,0:T(8,128)(2,1)S(1)}, u32[]{:S(2)}, u32[]{:S(2)}) async-start(bf16[32,96,128]{2,1,0:T(8,128)(2,1)} %time_project.1), calls=%async_computation | async-start | bytes 1572864 | tf_op jit(solution)/shard_map/all_to_all | solution.py:292
  18.7 0.0 copy-done.5
  18.7 0.6 pad.8.live
  19.3 0.0 copy-start
  19.3 0.0 copy-start.1
  19.3 12.3 %space_project.1 = (bf16[2,1024,128]{2,1,0:T(8,128)(2,1)}, bf16[2,2,1024,128]{3,2,1,0:T(8,128)(2,1)}, bf16[2,2,512,128]{3,2,1,0:T(8,128)(2,1)}, bf16[2,2,512,128]{3,2,1,0:T(8,128)(2,1)}, s32[128]{0:T(128)}) custom-call(s32[3]{0:T(128)} %labels.11, s32[3,128]{1,0:T(4,128)} %pad.8.live, bf16[1024,3072]{1,0:T(8,128)(2,1)} %tokens.3, ...), custom_call_target="tpu_custom_call" | custom-call | flops 4831838208 | bytes 12000000 | tf_op jit(solution)/shard_map/space_project/pallas_call | solution.py:296
  31.6 0.0 copy-start.4
  31.6 2.1 %collective-permute-start = (bf16[2,2,512,128]{3,2,1,0:T(8,128)(2,1)}, bf16[2,2,512,128]{3,2,1,0:T(8,128)(2,1)S(1)}, u32[]{:S(2)}, u32[]{:S(2)}) collective-permute-start(bf16[2,2,512,128]{3,2,1,0:T(8,128)(2,1)} %get-tuple-element.16), channel_id=1, source_target_pairs={{0,8},{8,16},{16,24},{24,32},{32,40},{40,48},{48,56},{56,64},{64,7... | collective-permute-start | bytes 1572872 | tf_op jit(solution)/shard_map/ppermute | solution.py:322
  33.7 3.5 %collective-permute-start.1 = (bf16[2,2,512,128]{3,2,1,0:T(8,128)(2,1)}, bf16[2,2,512,128]{3,2,1,0:T(8,128)(2,1)S(1)}, u32[]{:S(2)}, u32[]{:S(2)}) collective-permute-start(bf16[2,2,512,128]{3,2,1,0:T(8,128)(2,1)} %get-tuple-element.17), channel_id=1, source_target_pairs={{8,0},{16,8},{24,16},{32,24},{40,32},{48,40},{56,48},{64,56},{72,6... | collective-permute-start | bytes 1572872 | tf_op jit(solution)/shard_map/ppermute | solution.py:323
  37.2 3.7 %all-to-all-done.got = bf16[32,96,128]{2,1,0:T(8,128)(2,1)S(1)} async-done(((bf16[32,96,128]{2,1,0:T(8,128)(2,1)}), bf16[32,96,128]{2,1,0:T(8,128)(2,1)S(1)}, u32[]{:S(2)}, u32[]{:S(2)}) %all-to-all-start) | async-done | bytes 786464 | tf_op jit(solution)/shard_map/all_to_all | solution.py:292
  40.9 0.0 copy-done
  40.9 0.0 copy-done.1
  40.9 2.2 %time_attend.1 = (bf16[32,32,128]{2,1,0:T(8,128)(2,1)}, f32[8,128]{1,0:T(8,128)S(1)}) custom-call(s32[3]{0:T(128)S(1)} %copy-done, s32[3,4,4]{2,1,0:T(4,128)S(1)} %copy-done.1, bf16[32,96,128]{2,1,0:T(8,128)(2,1)S(1)} %all-to-all-done.got), custom_call_target="tpu_custom_call" | custom-call | flops 536870912 | bytes 1000000 | tf_op jit(solution)/shard_map/time_attend/pallas_call | solution.py:325
  43.1 8.0 %all-to-all-start.1 = ((bf16[32,32,128]{2,1,0:T(8,128)(2,1)}), bf16[32,32,128]{2,1,0:T(8,128)(2,1)S(1)}, u32[]{:S(2)}, u32[]{:S(2)}) async-start(bf16[32,32,128]{2,1,0:T(8,128)(2,1)} %get-tuple-element.18), calls=%async_computation.1 | async-start | bytes 524288 | tf_op jit(solution)/shard_map/all_to_all | solution.py:361
  51.1 0.0 copy-start.2
  51.1 1.2 %copy-done.2 = bf16[2,2,1024,128]{3,2,1,0:T(8,128)(2,1)S(1)} copy-done((bf16[2,2,1024,128]{3,2,1,0:T(8,128)(2,1)S(1)}, bf16[2,2,1024,128]{3,2,1,0:T(8,128)(2,1)}, u32[]{:S(2)}) %copy-start.2) | copy-done | bytes 1048600
  52.3 0.0 copy-start.3
  52.3 1.0 %copy-done.3 = bf16[2,1024,128]{2,1,0:T(8,128)(2,1)S(1)} copy-done((bf16[2,1024,128]{2,1,0:T(8,128)(2,1)S(1)}, bf16[2,1024,128]{2,1,0:T(8,128)(2,1)}, u32[]{:S(2)}) %copy-start.3) | copy-done | bytes 524312
  53.3 3.3 %attend_own.1.totals = f32[2,1024,256]{2,1,0:T(8,128)S(1)} custom-call(s32[3]{0:T(128)S(1)} %copy-done, s32[3,16,128]{2,1,0:T(8,128)S(1)} %pad.9.mask, bf16[2,1024,128]{2,1,0:T(8,128)(2,1)S(1)} %copy-done.3, bf16[2,2,1024,128]{3,2,1,0:T(8,128)(2,1)S(1)} %copy-done.2, f32[8,128]{1,0:T(8,128)S(1)} %get-tuple-element.15.after), custom_call_target="tpu_custom_call" | custom-call | flops 2147483648 | bytes 4000000 | tf_op jit(solution)/shard_map/attend_own/pallas_call | solution.py:341
  56.6 0.0 collective-permute-done.below
  56.6 0.0 collective-permute-done.1.above
  56.6 0.0 copy-done.4
  56.6 3.1 %attend_near.1.space = bf16[8,128,384]{2,1,0:T(8,128)(2,1)S(1)} custom-call(s32[3]{0:T(128)S(1)} %copy-done, s32[128]{0:T(128)S(1)} %copy-done.4, s32[3,16,128]{2,1,0:T(8,128)S(1)} %pad.9.mask, bf16[2,1024,128]{2,1,0:T(8,128)(2,1)S(1)} %copy-done.3, f32[2,1024,256]{2,1,0:T(8,128)S(1)} %attend_own.1.totals, ...), custom_call_target="tpu_custom_call" | custom-call | flops 2147483648 | bytes 4000000 | tf_op jit(solution)/shard_map/attend_near/pallas_call | solution.py:351
  59.8 2.7 %all-to-all-done.1 = bf16[32,32,128]{2,1,0:T(8,128)(2,1)S(1)} async-done(((bf16[32,32,128]{2,1,0:T(8,128)(2,1)}), bf16[32,32,128]{2,1,0:T(8,128)(2,1)S(1)}, u32[]{:S(2)}, u32[]{:S(2)}) %all-to-all-start.1) | async-done | bytes 262176 | tf_op jit(solution)/shard_map/all_to_all | solution.py:361
  62.5 0.6 merge.1
  63.1 18.8 %all_to_all.15.parts = bf16[8,128,384]{2,1,0:T(8,128)(2,1)S(1)} all-to-all(bf16[8,128,384]{2,1,0:T(8,128)(2,1)S(1)} %merge.1), channel_id=1, replica_groups=mesh['frame'=32,'head'=8] {'head'}, dimensions={0} | all-to-all | bytes 1572864 | tf_op jit(solution)/shard_map/all_to_all | solution.py:373
  81.9 0.9 %assemble.1 = bf16[128,3072]{1,0:T(8,128)(2,1)} custom-call(bf16[8,128,384]{2,1,0:T(8,128)(2,1)S(1)} %all_to_all.15.parts), custom_call_target="tpu_custom_call" | custom-call | flops 1 | bytes 2000000 | tf_op jit(solution)/shard_map/assemble/pallas_call | solution.py:374
  (2 shorter events, 0.0 us)
Async XLA Ops:
  0.0 18.7 %copy-start.5 = (s32[3,16,48]{2,1,0:T(8,128)S(1)}, s32[3,16,48]{2,1,0:T(8,128)}, u32[]{:S(2)}) copy-start(s32[3,16,48]{2,1,0:T(8,128)} %param.12) | copy-start | bytes 27652
  6.9 33.9 %all-to-all-start = ((bf16[32,96,128]{2,1,0:T(8,128)(2,1)}), bf16[32,96,128]{2,1,0:T(8,128)(2,1)S(1)}, u32[]{:S(2)}, u32[]{:S(2)}) async-start(bf16[32,96,128]{2,1,0:T(8,128)(2,1)} %time_project.1), calls=%async_computation | async-start | bytes 1572864 | tf_op jit(solution)/shard_map/all_to_all | solution.py:292
  19.3 21.6 %copy-start = (s32[3]{0:T(128)S(1)}, s32[3]{0:T(128)}, u32[]{:S(2)}) copy-start(s32[3]{0:T(128)} %labels.11) | copy-start | bytes 40
  19.3 21.6 %copy-start.1 = (s32[3,4,4]{2,1,0:T(4,128)S(1)}, s32[3,4,4]{2,1,0:T(4,128)}, u32[]{:S(2)}) copy-start(s32[3,4,4]{2,1,0:T(4,128)} %time_mask.1) | copy-start | bytes 580
  31.6 25.0 %copy-start.4 = (s32[128]{0:T(128)S(1)}, s32[128]{0:T(128)}, u32[]{:S(2)}) copy-start(s32[128]{0:T(128)} %get-tuple-element.12.lanes) | copy-start | bytes 1540
  31.6 25.0 %collective-permute-start = (bf16[2,2,512,128]{3,2,1,0:T(8,128)(2,1)}, bf16[2,2,512,128]{3,2,1,0:T(8,128)(2,1)S(1)}, u32[]{:S(2)}, u32[]{:S(2)}) collective-permute-start(bf16[2,2,512,128]{3,2,1,0:T(8,128)(2,1)} %get-tuple-element.16), channel_id=1, source_target_pairs={{0,8},{8,16},{16,24},{24,32},{32,40},{40,48},{48,56},{56,64},{64,7... | collective-permute-start | bytes 1572872 | tf_op jit(solution)/shard_map/ppermute | solution.py:322
  33.7 22.9 %collective-permute-start.1 = (bf16[2,2,512,128]{3,2,1,0:T(8,128)(2,1)}, bf16[2,2,512,128]{3,2,1,0:T(8,128)(2,1)S(1)}, u32[]{:S(2)}, u32[]{:S(2)}) collective-permute-start(bf16[2,2,512,128]{3,2,1,0:T(8,128)(2,1)} %get-tuple-element.17), channel_id=1, source_target_pairs={{8,0},{16,8},{24,16},{32,24},{40,32},{48,40},{56,48},{64,56},{72,6... | collective-permute-start | bytes 1572872 | tf_op jit(solution)/shard_map/ppermute | solution.py:323
  43.1 19.4 %all-to-all-start.1 = ((bf16[32,32,128]{2,1,0:T(8,128)(2,1)}), bf16[32,32,128]{2,1,0:T(8,128)(2,1)S(1)}, u32[]{:S(2)}, u32[]{:S(2)}) async-start(bf16[32,32,128]{2,1,0:T(8,128)(2,1)} %get-tuple-element.18), calls=%async_computation.1 | async-start | bytes 524288 | tf_op jit(solution)/shard_map/all_to_all | solution.py:361
  51.1 1.2 %copy-start.2 = (bf16[2,2,1024,128]{3,2,1,0:T(8,128)(2,1)S(1)}, bf16[2,2,1024,128]{3,2,1,0:T(8,128)(2,1)}, u32[]{:S(2)}) copy-start(bf16[2,2,1024,128]{3,2,1,0:T(8,128)(2,1)} %get-tuple-element.14.kv) | copy-start | bytes 3145732
  52.3 1.0 %copy-start.3 = (bf16[2,1024,128]{2,1,0:T(8,128)(2,1)S(1)}, bf16[2,1024,128]{2,1,0:T(8,128)(2,1)}, u32[]{:S(2)}) copy-start(bf16[2,1024,128]{2,1,0:T(8,128)(2,1)} %get-tuple-element.13.q) | copy-start | bytes 1572868

commit v5 on v4

--- a/solution.py
+++ b/solution.py
@@ -75,11 +75,12 @@
     copies = []
     for b in range(FRAMES):
         rows = pl.ds(b * FRAMES, FRAMES)
-        made[b, 0:FRAMES, :] = normed(acc[rows, 0:HD], query_gain[...] * SCALE)
-        made[b, FRAMES : 2 * FRAMES, :] = normed(acc[rows, HD : 2 * HD], key_gain[...])
-        made[b, 2 * FRAMES :, :] = acc[rows, 2 * HD :].astype(bf16)
+        owner = FRAMES - 1 - b
+        made[owner, 0:FRAMES, :] = normed(acc[rows, 0:HD], query_gain[...] * SCALE)
+        made[owner, FRAMES : 2 * FRAMES, :] = normed(acc[rows, HD : 2 * HD], key_gain[...])
+        made[owner, 2 * FRAMES :, :] = acc[rows, 2 * HD :].astype(bf16)
         if b % 8 == 7:
-            group = pl.ds(b - 7, 8)
+            group = pl.ds(owner, 8)
             copies.append(pltpu.make_async_copy(made.at[group], out.at[group], out_sems.at[b // 8]))
             copies[-1].start()
     for copy in copies:
@@ -231,7 +232,8 @@
         weight = jnp.exp2(scores).astype(bf16)
         total = jnp.dot(weight, vals, preferred_element_type=f32)
         mixed = (total[:, 0:HD] / total[:, HD:]).astype(bf16)
-        made[u] = mixed.reshape(FRAMES, 16, HD)
+        for f in range(FRAMES):
+            made[u, FRAMES - 1 - f] = mixed[f * 16 : (f + 1) * 16]
         copies.append(pltpu.make_async_copy(made.at[u], out.at[:, pl.ds(u * 16, 16), :], sems.at[u]))
         copies[-1].start()
     for copy in copies:
@@ -358,7 +360,10 @@
         cost_estimate=half,
         name="attend_near",
     )(labels, lanes, mask, q, totals, below, above)
-    timed = lax.all_to_all(time_out, "frame", split_axis=0, concat_axis=0, tiled=True)
+    backwards = [list(range(FRAMES - 1, -1, -1))]
+    timed = lax.all_to_all(
+        time_out, "frame", split_axis=0, concat_axis=0, tiled=True, axis_index_groups=backwards
+    )
     merged = pl.pallas_call(
         merge,
         out_shape=jax.ShapeDtypeStruct((GROUPS, per_target, 3 * HD), bf16),

time: 84.2 us -> 83.9 us (level)
  waiting for transfers between devices: 6.4 us -> 3.67 us
  starting transfers between devices: 25.3 us -> 27.6 us
    all_to_all x1, waiting for transfers between devices: 2.74 us -> 0.01 us  [on_device(): lax.all_to_all(time_out, 'frame', split_axis=0, concat_axis=0, tiled=True...]
    all_to_all x1, starting transfers between devices: 7.98 us -> 10.3 us  [on_device(): lax.all_to_all(time_out, 'frame', split_axis=0, concat_axis=0, tiled=True...]
  transfers between devices with their start and end apart: 4 -> 4, of which waited for: 2 -> 1; matrix products, arithmetic and copies ran while one was open for 1% -> 1% of each run, Pallas kernels for 25% -> 25%
where the time goes in v5:
time: 83.9 us; the launch traced here: 83.4 us
  Pallas kernels  29.4 us (35%)
  starting transfers between devices  27.6 us (33%)
  blocking collectives  19.5 us (23%)
  waiting for transfers between devices  3.67 us (4%)
  local copies, waits for them, and re-layouts  2.88 us (3%)
    all_to_all x1, blocking collectives, on_device(): lax.all_to_all(merged, 'head', split_axis=0, concat_axis=0, tiled=True)  19.5 us
    pallas_call x1, Pallas kernels, on_device(): pl.pallas_call(space_project, out_shape=(jax.ShapeDtypeStruct((2, ROWS, H...  12.3 us
    all_to_all x1, starting transfers between devices, on_device(): got = lax.all_to_all(sent, 'frame', split_axis=0, concat_axis=0, tiled=True)  11.7 us
    all_to_all x1, starting transfers between devices, on_device(): lax.all_to_all(time_out, 'frame', split_axis=0, concat_axis=0, tiled=True...  10.3 us
    pallas_call x1, Pallas kernels, on_device(): pl.pallas_call(time_project, out_shape=jax.ShapeDtypeStruct((FRAMES, 3 *...  6.94 us
    all_to_all x1, waiting for transfers between devices, on_device(): got = lax.all_to_all(sent, 'frame', split_axis=0, concat_axis=0, tiled=True)  3.66 us
    ppermute x1, starting transfers between devices, on_device(): above = lax.ppermute(down, 'frame', [(i + 1, i) for i in range(FRAMES - 1)])  3.5 us
    pallas_call x1, Pallas kernels, on_device(): pl.pallas_call(attend_own, out_shape=jax.ShapeDtypeStruct(sides, f32), in...  3.27 us
  transfers between devices with their start and end apart: 4, of which 1 were waited for; matrix products, arithmetic and copies ran while one was open for 1% of the time, Pallas kernels for 25%

profile of v5, /device:TPU:8, one launch (start us, length us, event | category | flops | bytes accessed | tf_op | source)
XLA Modules:
  0.0 83.4 jit_solution(10909901960030913710)
XLA Ops:
  0.0 0.0 copy-start.5
  0.0 6.9 %time_project.1 = bf16[32,96,128]{2,1,0:T(8,128)(2,1)} custom-call(s32[3]{0:T(128)} %labels.11, bf16[1024,3072]{1,0:T(8,128)(2,1)} %tokens.3, bf16[3,3072,384]{2,1,0:T(8,128)(2,1)} %weight.3, f32[1,128]{1,0:T(1,128)} %bitcast.4, f32[1,128]{1,0:T(1,128)} %bitcast.6), custom_call_target="tpu_custom_call" | custom-call | flops 2415919104 | bytes 9000000 | tf_op jit(solution)/shard_map/time_project/pallas_call | solution.py:277
  6.9 11.7 %all-to-all-start = ((bf16[32,96,128]{2,1,0:T(8,128)(2,1)}), bf16[32,96,128]{2,1,0:T(8,128)(2,1)S(1)}, u32[]{:S(2)}, u32[]{:S(2)}) async-start(bf16[32,96,128]{2,1,0:T(8,128)(2,1)} %time_project.1), calls=%async_computation | async-start | bytes 1572864 | tf_op jit(solution)/shard_map/all_to_all | solution.py:294
  18.7 0.0 copy-done.5
  18.7 0.6 pad.8.live
  19.3 0.0 copy-start
  19.3 0.0 copy-start.1
  19.3 12.3 %space_project.1 = (bf16[2,1024,128]{2,1,0:T(8,128)(2,1)}, bf16[2,2,1024,128]{3,2,1,0:T(8,128)(2,1)}, bf16[2,2,512,128]{3,2,1,0:T(8,128)(2,1)}, bf16[2,2,512,128]{3,2,1,0:T(8,128)(2,1)}, s32[128]{0:T(128)}) custom-call(s32[3]{0:T(128)} %labels.11, s32[3,128]{1,0:T(4,128)} %pad.8.live, bf16[1024,3072]{1,0:T(8,128)(2,1)} %tokens.3, ...), custom_call_target="tpu_custom_call" | custom-call | flops 4831838208 | bytes 12000000 | tf_op jit(solution)/shard_map/space_project/pallas_call | solution.py:298
  31.6 0.0 copy-start.4
  31.6 2.1 %collective-permute-start = (bf16[2,2,512,128]{3,2,1,0:T(8,128)(2,1)}, bf16[2,2,512,128]{3,2,1,0:T(8,128)(2,1)S(1)}, u32[]{:S(2)}, u32[]{:S(2)}) collective-permute-start(bf16[2,2,512,128]{3,2,1,0:T(8,128)(2,1)} %get-tuple-element.16), channel_id=1, source_target_pairs={{0,8},{8,16},{16,24},{24,32},{32,40},{40,48},{48,56},{56,64},{64,7... | collective-permute-start | bytes 1572872 | tf_op jit(solution)/shard_map/ppermute | solution.py:324
  33.7 3.5 %collective-permute-start.1 = (bf16[2,2,512,128]{3,2,1,0:T(8,128)(2,1)}, bf16[2,2,512,128]{3,2,1,0:T(8,128)(2,1)S(1)}, u32[]{:S(2)}, u32[]{:S(2)}) collective-permute-start(bf16[2,2,512,128]{3,2,1,0:T(8,128)(2,1)} %get-tuple-element.17), channel_id=1, source_target_pairs={{8,0},{16,8},{24,16},{32,24},{40,32},{48,40},{56,48},{64,56},{72,6... | collective-permute-start | bytes 1572872 | tf_op jit(solution)/shard_map/ppermute | solution.py:325
  37.2 3.7 %all-to-all-done.got = bf16[32,96,128]{2,1,0:T(8,128)(2,1)S(1)} async-done(((bf16[32,96,128]{2,1,0:T(8,128)(2,1)}), bf16[32,96,128]{2,1,0:T(8,128)(2,1)S(1)}, u32[]{:S(2)}, u32[]{:S(2)}) %all-to-all-start) | async-done | bytes 786464 | tf_op jit(solution)/shard_map/all_to_all | solution.py:294
  40.9 0.0 copy-done
  40.9 0.0 copy-done.1
  40.9 2.2 %time_attend.1 = (bf16[32,32,128]{2,1,0:T(8,128)(2,1)}, f32[8,128]{1,0:T(8,128)S(1)}) custom-call(s32[3]{0:T(128)S(1)} %copy-done, s32[3,4,4]{2,1,0:T(4,128)S(1)} %copy-done.1, bf16[32,96,128]{2,1,0:T(8,128)(2,1)S(1)} %all-to-all-done.got), custom_call_target="tpu_custom_call" | custom-call | flops 536870912 | bytes 1000000 | tf_op jit(solution)/shard_map/time_attend/pallas_call | solution.py:327
  43.1 10.3 %all-to-all-start.1 = ((bf16[32,32,128]{2,1,0:T(8,128)(2,1)}), bf16[32,32,128]{2,1,0:T(8,128)(2,1)S(1)}, u32[]{:S(2)}, u32[]{:S(2)}) async-start(bf16[32,32,128]{2,1,0:T(8,128)(2,1)} %get-tuple-element.18), calls=%async_computation.1 | async-start | bytes 524288 | tf_op jit(solution)/shard_map/all_to_all | solution.py:364
  53.4 0.0 copy-start.2
  53.4 1.2 %copy-done.2 = bf16[2,2,1024,128]{3,2,1,0:T(8,128)(2,1)S(1)} copy-done((bf16[2,2,1024,128]{3,2,1,0:T(8,128)(2,1)S(1)}, bf16[2,2,1024,128]{3,2,1,0:T(8,128)(2,1)}, u32[]{:S(2)}) %copy-start.2) | copy-done | bytes 1048600
  54.7 0.0 copy-start.3
  54.7 1.0 %copy-done.3 = bf16[2,1024,128]{2,1,0:T(8,128)(2,1)S(1)} copy-done((bf16[2,1024,128]{2,1,0:T(8,128)(2,1)S(1)}, bf16[2,1024,128]{2,1,0:T(8,128)(2,1)}, u32[]{:S(2)}) %copy-start.3) | copy-done | bytes 524312
  55.7 3.3 %attend_own.1.totals = f32[2,1024,256]{2,1,0:T(8,128)S(1)} custom-call(s32[3]{0:T(128)S(1)} %copy-done, s32[3,16,128]{2,1,0:T(8,128)S(1)} %pad.9.mask, bf16[2,1024,128]{2,1,0:T(8,128)(2,1)S(1)} %copy-done.3, bf16[2,2,1024,128]{3,2,1,0:T(8,128)(2,1)S(1)} %copy-done.2, f32[8,128]{1,0:T(8,128)S(1)} %get-tuple-element.15.after), custom_call_target="tpu_custom_call" | custom-call | flops 2147483648 | bytes 4000000 | tf_op jit(solution)/shard_map/attend_own/pallas_call | solution.py:343
  59.0 0.0 collective-permute-done.below
  59.0 0.0 collective-permute-done.1.above
  59.0 0.0 copy-done.4
  59.0 3.1 %attend_near.1.space = bf16[8,128,384]{2,1,0:T(8,128)(2,1)S(1)} custom-call(s32[3]{0:T(128)S(1)} %copy-done, s32[128]{0:T(128)S(1)} %copy-done.4, s32[3,16,128]{2,1,0:T(8,128)S(1)} %pad.9.mask, bf16[2,1024,128]{2,1,0:T(8,128)(2,1)S(1)} %copy-done.3, f32[2,1024,256]{2,1,0:T(8,128)S(1)} %attend_own.1.totals, ...), custom_call_target="tpu_custom_call" | custom-call | flops 2147483648 | bytes 4000000 | tf_op jit(solution)/shard_map/attend_near/pallas_call | solution.py:353
  62.1 0.0 all-to-all-done.1
  62.2 0.6 merge.1
  62.8 19.5 %all_to_all.15.parts = bf16[8,128,384]{2,1,0:T(8,128)(2,1)S(1)} all-to-all(bf16[8,128,384]{2,1,0:T(8,128)(2,1)S(1)} %merge.1), channel_id=1, replica_groups=mesh['frame'=32,'head'=8] {'head'}, dimensions={0} | all-to-all | bytes 1572864 | tf_op jit(solution)/shard_map/all_to_all | solution.py:378
  82.3 0.9 %assemble.1 = bf16[128,3072]{1,0:T(8,128)(2,1)} custom-call(bf16[8,128,384]{2,1,0:T(8,128)(2,1)S(1)} %all_to_all.15.parts), custom_call_target="tpu_custom_call" | custom-call | flops 1 | bytes 2000000 | tf_op jit(solution)/shard_map/assemble/pallas_call | solution.py:379
  (2 shorter events, 0.0 us)
Async XLA Ops:
  0.0 18.7 %copy-start.5 = (s32[3,16,48]{2,1,0:T(8,128)S(1)}, s32[3,16,48]{2,1,0:T(8,128)}, u32[]{:S(2)}) copy-start(s32[3,16,48]{2,1,0:T(8,128)} %param.12) | copy-start | bytes 27652
  6.9 33.9 %all-to-all-start = ((bf16[32,96,128]{2,1,0:T(8,128)(2,1)}), bf16[32,96,128]{2,1,0:T(8,128)(2,1)S(1)}, u32[]{:S(2)}, u32[]{:S(2)}) async-start(bf16[32,96,128]{2,1,0:T(8,128)(2,1)} %time_project.1), calls=%async_computation | async-start | bytes 1572864 | tf_op jit(solution)/shard_map/all_to_all | solution.py:294
  19.3 21.6 %copy-start = (s32[3]{0:T(128)S(1)}, s32[3]{0:T(128)}, u32[]{:S(2)}) copy-start(s32[3]{0:T(128)} %labels.11) | copy-start | bytes 40
  19.3 21.6 %copy-start.1 = (s32[3,4,4]{2,1,0:T(4,128)S(1)}, s32[3,4,4]{2,1,0:T(4,128)}, u32[]{:S(2)}) copy-start(s32[3,4,4]{2,1,0:T(4,128)} %time_mask.1) | copy-start | bytes 580
  31.6 27.4 %copy-start.4 = (s32[128]{0:T(128)S(1)}, s32[128]{0:T(128)}, u32[]{:S(2)}) copy-start(s32[128]{0:T(128)} %get-tuple-element.12.lanes) | copy-start | bytes 1540
  31.6 27.3 %collective-permute-start = (bf16[2,2,512,128]{3,2,1,0:T(8,128)(2,1)}, bf16[2,2,512,128]{3,2,1,0:T(8,128)(2,1)S(1)}, u32[]{:S(2)}, u32[]{:S(2)}) collective-permute-start(bf16[2,2,512,128]{3,2,1,0:T(8,128)(2,1)} %get-tuple-element.16), channel_id=1, source_target_pairs={{0,8},{8,16},{16,24},{24,32},{32,40},{40,48},{48,56},{56,64},{64,7... | collective-permute-start | bytes 1572872 | tf_op jit(solution)/shard_map/ppermute | solution.py:324
  33.7 25.3 %collective-permute-start.1 = (bf16[2,2,512,128]{3,2,1,0:T(8,128)(2,1)}, bf16[2,2,512,128]{3,2,1,0:T(8,128)(2,1)S(1)}, u32[]{:S(2)}, u32[]{:S(2)}) collective-permute-start(bf16[2,2,512,128]{3,2,1,0:T(8,128)(2,1)} %get-tuple-element.17), channel_id=1, source_target_pairs={{8,0},{16,8},{24,16},{32,24},{40,32},{48,40},{56,48},{64,56},{72,6... | collective-permute-start | bytes 1572872 | tf_op jit(solution)/shard_map/ppermute | solution.py:325
  43.1 19.1 %all-to-all-start.1 = ((bf16[32,32,128]{2,1,0:T(8,128)(2,1)}), bf16[32,32,128]{2,1,0:T(8,128)(2,1)S(1)}, u32[]{:S(2)}, u32[]{:S(2)}) async-start(bf16[32,32,128]{2,1,0:T(8,128)(2,1)} %get-tuple-element.18), calls=%async_computation.1 | async-start | bytes 524288 | tf_op jit(solution)/shard_map/all_to_all | solution.py:364
  53.4 1.2 %copy-start.2 = (bf16[2,2,1024,128]{3,2,1,0:T(8,128)(2,1)S(1)}, bf16[2,2,1024,128]{3,2,1,0:T(8,128)(2,1)}, u32[]{:S(2)}) copy-start(bf16[2,2,1024,128]{3,2,1,0:T(8,128)(2,1)} %get-tuple-element.14.kv) | copy-start | bytes 3145732
  54.7 1.0 %copy-start.3 = (bf16[2,1024,128]{2,1,0:T(8,128)(2,1)S(1)}, bf16[2,1024,128]{2,1,0:T(8,128)(2,1)}, u32[]{:S(2)}) copy-start(bf16[2,1024,128]{2,1,0:T(8,128)(2,1)} %get-tuple-element.13.q) | copy-start | bytes 1572868

commit v6 on v4

--- a/solution.py
+++ b/solution.py
@@ -75,7 +75,7 @@
     copies = []
     for b in range(FRAMES):
         rows = pl.ds(b * FRAMES, FRAMES)
-        made[b, 0:FRAMES, :] = normed(acc[rows, 0:HD], query_gain[...] * SCALE)
+        made[b, 0:FRAMES, :] = normed(acc[rows, 0:HD], query_gain[...])
         made[b, FRAMES : 2 * FRAMES, :] = normed(acc[rows, HD : 2 * HD], key_gain[...])
         made[b, 2 * FRAMES :, :] = acc[rows, 2 * HD :].astype(bf16)
         if b % 8 == 7:
@@ -129,7 +129,7 @@
     for r in range(ROWS // TILE):
         rows = pl.ds(r * TILE, TILE)
         for h in range(2):
-            q[h, rows, :] = normed(acc[rows, h * HD : (h + 1) * HD], query_gain[...] * SCALE)
+            q[h, rows, :] = normed(acc[rows, h * HD : (h + 1) * HD], query_gain[...])
         send(q.at[:, rows], q_out.at[:, rows])
     for copy in copies:
         copy.wait()
@@ -156,7 +156,7 @@
     for c in range(keys.shape[1] // width):
         part = pl.ds(c * width, width)
         scores = lax.dot_general(query, keys[h, part, :], (((1,), (1,)), ((), ())), preferred_element_type=f32)
-        weight = jnp.exp2(scores).astype(bf16)
+        weight = jnp.exp2(scores * SCALE).astype(bf16)
         product = jnp.dot(weight, vals[h, part, :], preferred_element_type=f32)
         total = product if total is None else total + product
     return total
@@ -228,7 +228,7 @@
         keys = jnp.concatenate([rows(1), mark], axis=1)
         vals = jnp.concatenate([rows(2), ones], axis=1)
         scores = lax.dot_general(query, keys, (((1,), (1,)), ((), ())), preferred_element_type=f32)
-        weight = jnp.exp2(scores).astype(bf16)
+        weight = jnp.exp2(scores * SCALE).astype(bf16)
         total = jnp.dot(weight, vals, preferred_element_type=f32)
         mixed = (total[:, 0:HD] / total[:, HD:]).astype(bf16)
         made[u] = mixed.reshape(FRAMES, 16, HD)

time: 84.2 us -> 84.2 us (level)
  no operation moved by 1% of the time
where the time goes in v6:
time: 84.2 us; the launch traced here: 83 us
  Pallas kernels  29.4 us (35%)
  starting transfers between devices  25.3 us (30%)
  blocking collectives  18.8 us (22%)
  waiting for transfers between devices  6.4 us (8%)
  local copies, waits for them, and re-layouts  2.88 us (3%)
    all_to_all x1, blocking collectives, on_device(): lax.all_to_all(merged, 'head', split_axis=0, concat_axis=0, tiled=True)  18.8 us
    pallas_call x1, Pallas kernels, on_device(): pl.pallas_call(space_project, out_shape=(jax.ShapeDtypeStruct((2, ROWS, H...  12.3 us
    all_to_all x1, starting transfers between devices, on_device(): got = lax.all_to_all(sent, 'frame', split_axis=0, concat_axis=0, tiled=True)  11.7 us
    all_to_all x1, starting transfers between devices, on_device(): lax.all_to_all(time_out, 'frame', split_axis=0, concat_axis=0, tiled=True)  7.98 us
    pallas_call x1, Pallas kernels, on_device(): pl.pallas_call(time_project, out_shape=jax.ShapeDtypeStruct((FRAMES, 3 *...  6.94 us
    all_to_all x1, waiting for transfers between devices, on_device(): got = lax.all_to_all(sent, 'frame', split_axis=0, concat_axis=0, tiled=True)  3.66 us
    ppermute x1, starting transfers between devices, on_device(): above = lax.ppermute(down, 'frame', [(i + 1, i) for i in range(FRAMES - 1)])  3.5 us
    pallas_call x1, Pallas kernels, on_device(): pl.pallas_call(attend_own, out_shape=jax.ShapeDtypeStruct(sides, f32), in...  3.27 us
  transfers between devices with their start and end apart: 4, of which 2 were waited for; matrix products, arithmetic and copies ran while one was open for 1% of the time, Pallas kernels for 25%

profile of v6, /device:TPU:8, one launch (start us, length us, event | category | flops | bytes accessed | tf_op | source)
XLA Modules:
  0.0 83.0 jit_solution(3237386135034322552)
XLA Ops:
  0.0 0.0 copy-start.5
  0.0 6.9 %time_project.1 = bf16[32,96,128]{2,1,0:T(8,128)(2,1)} custom-call(s32[3]{0:T(128)} %labels.11, bf16[1024,3072]{1,0:T(8,128)(2,1)} %tokens.3, bf16[3,3072,384]{2,1,0:T(8,128)(2,1)} %weight.3, f32[1,128]{1,0:T(1,128)} %bitcast.4, f32[1,128]{1,0:T(1,128)} %bitcast.6), custom_call_target="tpu_custom_call" | custom-call | flops 2415919104 | bytes 9000000 | tf_op jit(solution)/shard_map/time_project/pallas_call | solution.py:275
  6.9 11.7 %all-to-all-start = ((bf16[32,96,128]{2,1,0:T(8,128)(2,1)}), bf16[32,96,128]{2,1,0:T(8,128)(2,1)S(1)}, u32[]{:S(2)}, u32[]{:S(2)}) async-start(bf16[32,96,128]{2,1,0:T(8,128)(2,1)} %time_project.1), calls=%async_computation | async-start | bytes 1572864 | tf_op jit(solution)/shard_map/all_to_all | solution.py:292
  18.7 0.0 copy-done.5
  18.7 0.6 pad.8.live
  19.3 0.0 copy-start
  19.3 0.0 copy-start.1
  19.3 12.3 %space_project.1 = (bf16[2,1024,128]{2,1,0:T(8,128)(2,1)}, bf16[2,2,1024,128]{3,2,1,0:T(8,128)(2,1)}, bf16[2,2,512,128]{3,2,1,0:T(8,128)(2,1)}, bf16[2,2,512,128]{3,2,1,0:T(8,128)(2,1)}, s32[128]{0:T(128)}) custom-call(s32[3]{0:T(128)} %labels.11, s32[3,128]{1,0:T(4,128)} %pad.8.live, bf16[1024,3072]{1,0:T(8,128)(2,1)} %tokens.3, ...), custom_call_target="tpu_custom_call" | custom-call | flops 4831838208 | bytes 12000000 | tf_op jit(solution)/shard_map/space_project/pallas_call | solution.py:296
  31.6 0.0 copy-start.4
  31.6 2.1 %collective-permute-start = (bf16[2,2,512,128]{3,2,1,0:T(8,128)(2,1)}, bf16[2,2,512,128]{3,2,1,0:T(8,128)(2,1)S(1)}, u32[]{:S(2)}, u32[]{:S(2)}) collective-permute-start(bf16[2,2,512,128]{3,2,1,0:T(8,128)(2,1)} %get-tuple-element.16), channel_id=1, source_target_pairs={{0,8},{8,16},{16,24},{24,32},{32,40},{40,48},{48,56},{56,64},{64,7... | collective-permute-start | bytes 1572872 | tf_op jit(solution)/shard_map/ppermute | solution.py:322
  33.7 3.5 %collective-permute-start.1 = (bf16[2,2,512,128]{3,2,1,0:T(8,128)(2,1)}, bf16[2,2,512,128]{3,2,1,0:T(8,128)(2,1)S(1)}, u32[]{:S(2)}, u32[]{:S(2)}) collective-permute-start(bf16[2,2,512,128]{3,2,1,0:T(8,128)(2,1)} %get-tuple-element.17), channel_id=1, source_target_pairs={{8,0},{16,8},{24,16},{32,24},{40,32},{48,40},{56,48},{64,56},{72,6... | collective-permute-start | bytes 1572872 | tf_op jit(solution)/shard_map/ppermute | solution.py:323
  37.2 3.7 %all-to-all-done.got = bf16[32,96,128]{2,1,0:T(8,128)(2,1)S(1)} async-done(((bf16[32,96,128]{2,1,0:T(8,128)(2,1)}), bf16[32,96,128]{2,1,0:T(8,128)(2,1)S(1)}, u32[]{:S(2)}, u32[]{:S(2)}) %all-to-all-start) | async-done | bytes 786464 | tf_op jit(solution)/shard_map/all_to_all | solution.py:292
  40.9 0.0 copy-done
  40.9 0.0 copy-done.1
  40.9 2.2 %time_attend.1 = (bf16[32,32,128]{2,1,0:T(8,128)(2,1)}, f32[8,128]{1,0:T(8,128)S(1)}) custom-call(s32[3]{0:T(128)S(1)} %copy-done, s32[3,4,4]{2,1,0:T(4,128)S(1)} %copy-done.1, bf16[32,96,128]{2,1,0:T(8,128)(2,1)S(1)} %all-to-all-done.got), custom_call_target="tpu_custom_call" | custom-call | flops 536870912 | bytes 1000000 | tf_op jit(solution)/shard_map/time_attend/pallas_call | solution.py:325
  43.1 8.0 %all-to-all-start.1 = ((bf16[32,32,128]{2,1,0:T(8,128)(2,1)}), bf16[32,32,128]{2,1,0:T(8,128)(2,1)S(1)}, u32[]{:S(2)}, u32[]{:S(2)}) async-start(bf16[32,32,128]{2,1,0:T(8,128)(2,1)} %get-tuple-element.18), calls=%async_computation.1 | async-start | bytes 524288 | tf_op jit(solution)/shard_map/all_to_all | solution.py:361
  51.1 0.0 copy-start.2
  51.1 1.2 %copy-done.2 = bf16[2,2,1024,128]{3,2,1,0:T(8,128)(2,1)S(1)} copy-done((bf16[2,2,1024,128]{3,2,1,0:T(8,128)(2,1)S(1)}, bf16[2,2,1024,128]{3,2,1,0:T(8,128)(2,1)}, u32[]{:S(2)}) %copy-start.2) | copy-done | bytes 1048600
  52.3 0.0 copy-start.3
  52.3 1.0 %copy-done.3 = bf16[2,1024,128]{2,1,0:T(8,128)(2,1)S(1)} copy-done((bf16[2,1024,128]{2,1,0:T(8,128)(2,1)S(1)}, bf16[2,1024,128]{2,1,0:T(8,128)(2,1)}, u32[]{:S(2)}) %copy-start.3) | copy-done | bytes 524312
  53.3 3.3 %attend_own.1.totals = f32[2,1024,256]{2,1,0:T(8,128)S(1)} custom-call(s32[3]{0:T(128)S(1)} %copy-done, s32[3,16,128]{2,1,0:T(8,128)S(1)} %pad.9.mask, bf16[2,1024,128]{2,1,0:T(8,128)(2,1)S(1)} %copy-done.3, bf16[2,2,1024,128]{3,2,1,0:T(8,128)(2,1)S(1)} %copy-done.2, f32[8,128]{1,0:T(8,128)S(1)} %get-tuple-element.15.after), custom_call_target="tpu_custom_call" | custom-call | flops 2147483648 | bytes 4000000 | tf_op jit(solution)/shard_map/attend_own/pallas_call | solution.py:341
  56.6 0.0 collective-permute-done.below
  56.6 0.0 collective-permute-done.1.above
  56.6 0.0 copy-done.4
  56.6 3.1 %attend_near.1.space = bf16[8,128,384]{2,1,0:T(8,128)(2,1)S(1)} custom-call(s32[3]{0:T(128)S(1)} %copy-done, s32[128]{0:T(128)S(1)} %copy-done.4, s32[3,16,128]{2,1,0:T(8,128)S(1)} %pad.9.mask, bf16[2,1024,128]{2,1,0:T(8,128)(2,1)S(1)} %copy-done.3, f32[2,1024,256]{2,1,0:T(8,128)S(1)} %attend_own.1.totals, ...), custom_call_target="tpu_custom_call" | custom-call | flops 2147483648 | bytes 4000000 | tf_op jit(solution)/shard_map/attend_near/pallas_call | solution.py:351
  59.8 2.7 %all-to-all-done.1 = bf16[32,32,128]{2,1,0:T(8,128)(2,1)S(1)} async-done(((bf16[32,32,128]{2,1,0:T(8,128)(2,1)}), bf16[32,32,128]{2,1,0:T(8,128)(2,1)S(1)}, u32[]{:S(2)}, u32[]{:S(2)}) %all-to-all-start.1) | async-done | bytes 262176 | tf_op jit(solution)/shard_map/all_to_all | solution.py:361
  62.5 0.6 merge.1
  63.1 18.8 %all_to_all.15.parts = bf16[8,128,384]{2,1,0:T(8,128)(2,1)S(1)} all-to-all(bf16[8,128,384]{2,1,0:T(8,128)(2,1)S(1)} %merge.1), channel_id=1, replica_groups=mesh['frame'=32,'head'=8] {'head'}, dimensions={0} | all-to-all | bytes 1572864 | tf_op jit(solution)/shard_map/all_to_all | solution.py:373
  81.9 0.9 %assemble.1 = bf16[128,3072]{1,0:T(8,128)(2,1)} custom-call(bf16[8,128,384]{2,1,0:T(8,128)(2,1)S(1)} %all_to_all.15.parts), custom_call_target="tpu_custom_call" | custom-call | flops 1 | bytes 2000000 | tf_op jit(solution)/shard_map/assemble/pallas_call | solution.py:374
  (2 shorter events, 0.0 us)
Async XLA Ops:
  0.0 18.7 %copy-start.5 = (s32[3,16,48]{2,1,0:T(8,128)S(1)}, s32[3,16,48]{2,1,0:T(8,128)}, u32[]{:S(2)}) copy-start(s32[3,16,48]{2,1,0:T(8,128)} %param.12) | copy-start | bytes 27652
  6.9 33.9 %all-to-all-start = ((bf16[32,96,128]{2,1,0:T(8,128)(2,1)}), bf16[32,96,128]{2,1,0:T(8,128)(2,1)S(1)}, u32[]{:S(2)}, u32[]{:S(2)}) async-start(bf16[32,96,128]{2,1,0:T(8,128)(2,1)} %time_project.1), calls=%async_computation | async-start | bytes 1572864 | tf_op jit(solution)/shard_map/all_to_all | solution.py:292
  19.3 21.6 %copy-start = (s32[3]{0:T(128)S(1)}, s32[3]{0:T(128)}, u32[]{:S(2)}) copy-start(s32[3]{0:T(128)} %labels.11) | copy-start | bytes 40
  19.3 21.6 %copy-start.1 = (s32[3,4,4]{2,1,0:T(4,128)S(1)}, s32[3,4,4]{2,1,0:T(4,128)}, u32[]{:S(2)}) copy-start(s32[3,4,4]{2,1,0:T(4,128)} %time_mask.1) | copy-start | bytes 580
  31.6 25.0 %copy-start.4 = (s32[128]{0:T(128)S(1)}, s32[128]{0:T(128)}, u32[]{:S(2)}) copy-start(s32[128]{0:T(128)} %get-tuple-element.12.lanes) | copy-start | bytes 1540
  31.6 25.0 %collective-permute-start = (bf16[2,2,512,128]{3,2,1,0:T(8,128)(2,1)}, bf16[2,2,512,128]{3,2,1,0:T(8,128)(2,1)S(1)}, u32[]{:S(2)}, u32[]{:S(2)}) collective-permute-start(bf16[2,2,512,128]{3,2,1,0:T(8,128)(2,1)} %get-tuple-element.16), channel_id=1, source_target_pairs={{0,8},{8,16},{16,24},{24,32},{32,40},{40,48},{48,56},{56,64},{64,7... | collective-permute-start | bytes 1572872 | tf_op jit(solution)/shard_map/ppermute | solution.py:322
  33.7 22.9 %collective-permute-start.1 = (bf16[2,2,512,128]{3,2,1,0:T(8,128)(2,1)}, bf16[2,2,512,128]{3,2,1,0:T(8,128)(2,1)S(1)}, u32[]{:S(2)}, u32[]{:S(2)}) collective-permute-start(bf16[2,2,512,128]{3,2,1,0:T(8,128)(2,1)} %get-tuple-element.17), channel_id=1, source_target_pairs={{8,0},{16,8},{24,16},{32,24},{40,32},{48,40},{56,48},{64,56},{72,6... | collective-permute-start | bytes 1572872 | tf_op jit(solution)/shard_map/ppermute | solution.py:323
  43.1 19.5 %all-to-all-start.1 = ((bf16[32,32,128]{2,1,0:T(8,128)(2,1)}), bf16[32,32,128]{2,1,0:T(8,128)(2,1)S(1)}, u32[]{:S(2)}, u32[]{:S(2)}) async-start(bf16[32,32,128]{2,1,0:T(8,128)(2,1)} %get-tuple-element.18), calls=%async_computation.1 | async-start | bytes 524288 | tf_op jit(solution)/shard_map/all_to_all | solution.py:361
  51.1 1.2 %copy-start.2 = (bf16[2,2,1024,128]{3,2,1,0:T(8,128)(2,1)S(1)}, bf16[2,2,1024,128]{3,2,1,0:T(8,128)(2,1)}, u32[]{:S(2)}) copy-start(bf16[2,2,1024,128]{3,2,1,0:T(8,128)(2,1)} %get-tuple-element.14.kv) | copy-start | bytes 3145732
  52.3 1.0 %copy-start.3 = (bf16[2,1024,128]{2,1,0:T(8,128)(2,1)S(1)}, bf16[2,1024,128]{2,1,0:T(8,128)(2,1)}, u32[]{:S(2)}) copy-start(bf16[2,1024,128]{2,1,0:T(8,128)(2,1)} %get-tuple-element.13.q) | copy-start | bytes 1572868
